TPU v7x, 512 devices: a whole 4x4x16 slice. The times are simulated.
512 devices in a mesh: pipe: 16 (over z_hi, x), tensor: 32 (over z_lo, y, core).
Axes of the slice: x: 4, y: 4, z: 16 (z_hi: 4, z_lo: 4; z = z_hi * 4 + z_lo), core: 2. Of those that a mesh axis runs over, the one named last changes fastest.
Arguments:
- hidden: bfloat16 [512, 8192], P('pipe'), may hold values from -6 to 6
- kv_weight: bfloat16 [16, 2048, 8192], P('pipe', 'tensor'), may hold values from -0.0625 to 0.0625
- queries: bfloat16 [16, 512, 8192], P('pipe', None, 'tensor'), may hold values from -5 to 5
- out_grads: bfloat16 [16, 512, 8192], P('pipe', None, 'tensor'), may hold values from -384 to 384
- cache: bfloat16 [16, 2, 32768, 128], P('pipe', None, 'tensor'), may hold values from -5 to 5
- prefix_len: int32 [512], replicated, may hold values from 512 to 4096, as said below
- doc_start: int32 [512], replicated, may hold values from 0 to 511, as said below
Outputs:
- hidden_grads: float32 [512, 8192], P('pipe', 'tensor')
- weight_grads: float32 [16, 2048, 8192], P('pipe', 'tensor')
Inputs may be any that keep to these rules, and one draw needn't show every extreme that they name: Row r sees the first prefix_len[r] cached positions; some row sees all 4096. doc_start[0] = 0, for r > 0 doc_start[r] is either doc_start[r-1] or r, and the last row starts a document of its own.
All inputs are finite; a program needn't handle non-finite values.
Results may differ from a plain program's by a relative error of at most 0.018.
Values may be sent and summed in bfloat16 or wider, within the bound.
No kernel may reach another device: no remote copies, remote signals or barrier semaphores. Data moves between devices by JAX's collectives and lax.ppermute only.
A program may use at most 64 MiB of HBM per device.

v0:
```python
import jax
import jax.numpy as jnp
from jax import lax
from jax.sharding import PartitionSpec as P

KVH = 8
HEAD = 128
R = 512
PREFIX = 4096


def swapped(value, axis, apart):
    mask = 2**apart
    pairs = [(source, source ^ mask) for source in range(lax.axis_size(axis))]
    return lax.ppermute(value, axis, pairs)


def shards(hidden, kv_weight, queries, out_grads, cache, prefix_len, doc_start):
    tensor_count = lax.axis_size("tensor")
    tensor_rank = lax.axis_index("tensor")
    group_size = tensor_count // KVH
    group_bits = group_size.bit_length() - 1
    weight = kv_weight[0]
    head_count = queries.shape[2] // HEAD
    softmax_scale = HEAD ** (-0.5)

    def bit_of(position):
        return tensor_rank // (1 << position) % 2

    turned = lax.all_to_all(weight, "tensor", split_axis=1, concat_axis=0, tiled=True)
    full_hidden = lax.all_gather(hidden, "pipe", axis=0, tiled=True)
    kv_piece = lax.dot_general(
        weight, full_hidden, (((1,), (1,)), ((), ())), preferred_element_type=jnp.float32
    )
    whole_kv = kv_piece.astype(jnp.bfloat16)
    for position in range(group_bits):
        other = swapped(whole_kv, "tensor", position)
        whole_kv = jnp.where(
            bit_of(position) == 0,
            jnp.concatenate([whole_kv, other], 0),
            jnp.concatenate([other, whole_kv], 0),
        )
    blocks = cache[0]
    for position in range(group_bits):
        other = swapped(blocks, "tensor", position)
        blocks = jnp.where(
            bit_of(position) == 0,
            jnp.concatenate([blocks, other], 1),
            jnp.concatenate([other, blocks], 1),
        )
    fresh_keys = whole_kv[:HEAD]
    fresh_values = whole_kv[HEAD:]
    query_matrix = queries[0].reshape(R, head_count, HEAD)
    output_gradient = out_grads[0].reshape(R, head_count, HEAD)
    fresh_scores = (
        jnp.einsum("rhd,dm->hrm", query_matrix, fresh_keys, preferred_element_type=jnp.float32)
        * softmax_scale
    )
    fresh_logits = jnp.einsum(
        "rhd,dm->hrm", output_gradient, fresh_values, preferred_element_type=jnp.float32
    )
    row_ids = jnp.arange(R, dtype=jnp.int32)
    mask_new = (row_ids[None, :] >= doc_start[:, None]) & (row_ids[None, :] <= row_ids[:, None])
    top = jnp.max(jnp.where(mask_new, fresh_scores, -jnp.inf), axis=2)
    first = jnp.exp(jnp.where(mask_new, fresh_scores - top[..., None], -jnp.inf))
    total = jnp.sum(first, axis=2)
    accum = jnp.sum(first * fresh_logits, axis=2)
    span = min(512, PREFIX)
    block_count = PREFIX // span
    key_blocks = blocks[0].reshape(block_count, span, HEAD)
    value_blocks = blocks[1].reshape(block_count, span, HEAD)
    starts = jnp.arange(block_count, dtype=jnp.int32) * span

    def sweep(carry, item):
        running_top, running_total, running_accum = carry
        key_block, value_block, start = item
        scores = (
            jnp.einsum("rhd,jd->hrj", query_matrix, key_block, preferred_element_type=jnp.float32)
            * softmax_scale
        )
        dots = jnp.einsum(
            "rhd,jd->hrj", output_gradient, value_block, preferred_element_type=jnp.float32
        )
        seen = (start + jnp.arange(span, dtype=jnp.int32))[None, :] < prefix_len[:, None]
        block_top = jnp.max(jnp.where(seen, scores, -jnp.inf), axis=2)
        new_top = jnp.maximum(running_top, block_top)
        fade = jnp.exp(running_top - new_top)
        weights = jnp.exp(jnp.where(seen, scores - new_top[..., None], -jnp.inf))
        new_total = running_total * fade + jnp.sum(weights, axis=2)
        new_accum = running_accum * fade + jnp.sum(weights * dots, axis=2)
        return ((new_top, new_total, new_accum), None)

    (top, total, accum), unused = lax.scan(
        sweep, (top, total, accum), (key_blocks, value_blocks, starts)
    )
    dsum = accum / total
    quotient = (
        jnp.exp(jnp.where(mask_new, fresh_scores - top[..., None], -jnp.inf)) / total[..., None]
    )
    attention_weights = quotient.astype(jnp.bfloat16)
    score_gradient = (quotient * (fresh_logits - dsum[..., None])).astype(jnp.bfloat16)
    value_gradient = jnp.einsum(
        "hrm,rhd->dm", attention_weights, output_gradient, preferred_element_type=jnp.float32
    )
    key_gradient = (
        jnp.einsum("hrm,rhd->dm", score_gradient, query_matrix, preferred_element_type=jnp.float32)
        * softmax_scale
    )
    partial_value = jnp.concatenate([key_gradient, value_gradient], 0)
    for position in reversed(range(group_bits)):
        half = partial_value.shape[0] // 2
        upper = bit_of(position) == 1
        keep = jnp.where(upper, partial_value[half:], partial_value[:half])
        send = jnp.where(upper, partial_value[:half], partial_value[half:])
        partial_value = keep + swapped(send, "tensor", position)
    kv_grads = partial_value.astype(jnp.bfloat16)
    all_grads = lax.all_gather(kv_grads, "tensor", axis=0, tiled=True)
    hidden_part_grad = lax.dot_general(
        all_grads, turned, (((0,), (0,)), ((), ())), preferred_element_type=jnp.float32
    )
    weight_grad = jnp.dot(kv_grads, full_hidden, preferred_element_type=jnp.float32)
    hidden_grads = lax.psum_scatter(
        hidden_part_grad.astype(jnp.bfloat16), "pipe", scatter_dimension=0, tiled=True
    ).astype(jnp.float32)
    return (hidden_grads, weight_grad[None])


def solution(mesh):
    placed = (
        P("pipe", None),
        P("pipe", "tensor", None),
        P("pipe", None, "tensor"),
        P("pipe", None, "tensor"),
        P("pipe", None, "tensor", None),
        P(),
        P(),
    )
    return jax.shard_map(
        shards,
        mesh=mesh,
        in_specs=placed,
        out_specs=(P("pipe", "tensor"), P("pipe", "tensor", None)),
        check_vma=False,
    )
```

profile of v0, /device:TPU:24, one launch (start us, length us, event | category | flops | bytes accessed | tf_op | source)
XLA Modules:
  0.0 498.0 jit_solution(8395502184845470857)
XLA Ops:
  7.9 1.9 collective-permute-start.2
  9.9 2.1 collective-permute-done.2
  13.4 2.7 collective-permute-start.3
  16.9 214.0 %all-gather.3.cloned.1.call-done = bf16[512,8192]{1,0:T(8,128)(2,1)} async-done(((bf16[32,8192]{1,0:T(8,128)(2,1)}), bf16[512,8192]{1,0:T(8,128)(2,1)}) %all-gather.3.cloned.1.call-update) | async-done | bytes 8388624 | tf_op jit(solution)/shard_map/all_gather | solution.py:31
  231.0 6.0 %convolution_convert_fusion.1 = bf16[64,512]{1,0:T(8,128)(2,1)S(1)} fusion(bf16[512,8192]{1,0:T(8,128)(2,1)} %all-gather.3.cloned.1.call-done, bf16[1,64,8192]{2,1,0:T(8,128)(2,1)S(1)} %copy-done), kind=kOutput, calls=%fused_computation.41 | convolution fusion | flops 536903680 | bytes 9502720 | tf_op jit(solution)/shard_map/dot_general | solution.py:32
  237.0 2.0 collective-permute-start
  239.0 2.2 maximum_select_fusion
  241.2 2.7 collective-permute-start.1
  245.1 3.9 collective-permute-done.1
  249.6 2.1 fusion.12
  251.7 35.2 %while.14 = (s32[]{:T(128)}, f32[2,512]{1,0:T(2,128)S(1)}, f32[2,512]{1,0:T(2,128)S(1)}, f32[2,512]{1,0:T(2,128)S(1)}, s32[8]{0:T(128)S(1)}, /*index=5*/s32[512]...) while((s32[]{:T(128)}, f32[2,512]{1,0:T(2,128)S(1)}, ...), condition=%wide.region_7.8_spmd, body=%wide.region_3.7_spmd.sunk | while | flops 274992640 | bytes 8206477 | solution.py:93
  262.7 1.7 fusion.58
  271.5 1.7 fusion.58
  275.9 1.7 fusion.58
  286.9 2.5 convolution_bitcast_fusion.2
  290.8 2.7 collective-permute-start.4
  293.5 7.0 %collective-permute-done.4 = f32[128,512]{1,0:T(8,128)S(1)} collective-permute-done((f32[128,512]{1,0:T(8,128)S(1)}, f32[128,512]{1,0:T(8,128)S(1)}, u32[]{:S(2)}, u32[]{:S(2)}) %collective-permute-start.4) | collective-permute-done | bytes 262176 | tf_op jit(solution)/shard_map/ppermute | solution.py:15
  300.7 1.9 collective-permute-start.5
  304.4 7.3 %all-to-all-start = ((bf16[64,32,256]{2,0,1:T(8,128)(2,1)}), bf16[64,32,256]{2,0,1:T(8,128)(2,1)S(1)}, u32[]{:S(2)}, u32[]{:S(2)}) async-start(bf16[64,32,256]{2,0,1:T(8,128)(2,1)} %copy.46), calls=%async_computation | async-start | bytes 2097152 | tf_op jit(solution)/shard_map/all_to_all | solution.py:30
  312.5 26.1 %all-to-all-done = bf16[64,32,256]{2,0,1:T(8,128)(2,1)S(1)} async-done(((bf16[64,32,256]{2,0,1:T(8,128)(2,1)}), bf16[64,32,256]{2,0,1:T(8,128)(2,1)S(1)}, u32[]{:S(2)}, u32[]{:S(2)}) %all-to-all-start) | async-done | bytes 1048608 | tf_op jit(solution)/shard_map/all_to_all | solution.py:30
  338.6 37.5 %all-gather.5.cloned.1.call-done = bf16[2048,512]{1,0:T(8,128)(2,1)} async-done(((bf16[64,512]{1,0:T(8,128)(2,1)}), bf16[2048,512]{1,0:T(8,128)(2,1)}) %all-gather.5.cloned.1.call-update) | async-done | bytes 2097168 | tf_op jit(solution)/shard_map/all_gather | solution.py:117
  376.1 3.1 convolution_convert_fusion
  379.2 6.3 %convolution_bitcast_fusion = f32[1,64,8192]{2,1,0:T(8,128)} fusion(bf16[64,512]{1,0:T(8,128)(2,1)S(1)} %copy-done.4, bf16[512,8192]{1,0:T(8,128)(2,1)} %all-gather.3.cloned.1.call-done), kind=kOutput, calls=%fused_computation.20 | convolution fusion | flops 536870912 | bytes 10551296 | tf_op jit(solution)/shard_map/dot_general | solution.py:121
  385.5 104.7 %reduce-scatter.2.cloned.1.call-done = bf16[32,256]{1,0:T(8,128)(2,1)} async-done(((bf16[512,256]{1,0:T(8,128)(2,1)}), bf16[32,256]{1,0:T(8,128)(2,1)}) %reduce-scatter.2.cloned.1.call-update) | async-done | bytes 16400 | tf_op jit(solution)/shard_map/reduce_scatter | solution.py:122
  (116 shorter events, 39.7 us)
Async XLA Ops:
  7.2 8.9 %copy-start.5 = (bf16[1,512,256]{2,1,0:T(8,128)(2,1)S(1)}, bf16[1,512,256]{2,1,0:T(8,128)(2,1)}, u32[]{:S(2)}) copy-start(bf16[1,512,256]{2,1,0:T(8,128)(2,1)} %param.11) | copy-start | bytes 786436
  7.2 9.1 %copy-start.6 = (bf16[1,512,256]{2,1,0:T(8,128)(2,1)S(1)}, bf16[1,512,256]{2,1,0:T(8,128)(2,1)}, u32[]{:S(2)}) copy-start(bf16[1,512,256]{2,1,0:T(8,128)(2,1)} %param.12) | copy-start | bytes 786436
  7.2 223.8 %all-gather.3.cloned.1.call-start = ((), (), s32[]{:S(2)}) async-start(), calls=%async_computation.2 | async-start | bytes 8912896 | tf_op jit(solution)/shard_map/all_gather | solution.py:31
  7.9 4.0 collective-permute-start.2
  9.9 6.9 %copy-start.8 = (s32[512]{0:T(512)S(1)}, s32[512]{0:T(512)}, u32[]{:S(2)}) copy-start(s32[512]{0:T(512)} %param.15) | copy-start | bytes 6148
  9.9 221.1 %copy-start = (bf16[1,64,8192]{2,1,0:T(8,128)(2,1)S(1)}, bf16[1,64,8192]{2,1,0:T(8,128)(2,1)}, u32[]{:S(2)}) copy-start(bf16[1,64,8192]{2,1,0:T(8,128)(2,1)} %param.10) | copy-start | bytes 3145732
  13.4 225.6 %collective-permute-start.3 = (bf16[2,2048,128]{2,1,0:T(8,128)(2,1)S(1)}, bf16[2,2048,128]{2,1,0:T(8,128)(2,1)}, u32[]{:S(2)}, u32[]{:S(2)}) collective-permute-start(bf16[2,2048,128]{2,1,0:T(8,128)(2,1)S(1)} %maximum_select_fusion.1), channel_id=1, source_target_pairs={{0,2},{1,3},{2,0},{3,1},{4,6},{5,7},{6,4},{7,5},{8,10},{9,11},{10,... | collective-permute-start | bytes 3145736 | tf_op jit(solution)/shard_map/ppermute | solution.py:15
  237.0 4.2 collective-permute-start
  241.2 7.8 %collective-permute-start.1 = (bf16[128,512]{1,0:T(8,128)(2,1)S(1)}, bf16[128,512]{1,0:T(8,128)(2,1)S(1)}, u32[]{:S(2)}, u32[]{:S(2)}) collective-permute-start(bf16[128,512]{1,0:T(8,128)(2,1)S(1)} %maximum_select_fusion.3), channel_id=1, source_target_pairs={{0,2},{1,3},{2,0},{3,1},{4,6},{5,7},{6,4},{7,5},{8,10},{9,11},{10,... | collective-permute-start | bytes 393224 | tf_op jit(solution)/shard_map/ppermute | solution.py:15
  249.6 2.1 copy-start.1
  249.6 2.1 copy-start.7
  286.9 2.6 copy-start.2
  286.9 2.8 copy-start.3
  290.8 9.8 %collective-permute-start.4 = (f32[128,512]{1,0:T(8,128)S(1)}, f32[128,512]{1,0:T(8,128)S(1)}, u32[]{:S(2)}, u32[]{:S(2)}) collective-permute-start(f32[128,512]{1,0:T(8,128)S(1)} %select_bitcast_fusion), channel_id=1, source_target_pairs={{0,2},{1,3},{2,0},{3,1},{4,6},{5,7},{6,4},{7,5},{8,10},{9,11},{10,... | collective-permute-start | bytes 786440 | tf_op jit(solution)/shard_map/ppermute | solution.py:15
  300.7 11.1 %collective-permute-start.5 = (f32[64,512]{1,0:T(8,128)S(1)}, f32[64,512]{1,0:T(8,128)S(1)}, u32[]{:S(2)}, u32[]{:S(2)}) collective-permute-start(f32[64,512]{1,0:T(8,128)S(1)} %slice_select_fusion), channel_id=1, source_target_pairs={{0,1},{1,0},{2,3},{3,2},{4,5},{5,4},{6,7},{7,6},{8,9},{9,8},{10,11... | collective-permute-start | bytes 393224 | tf_op jit(solution)/shard_map/ppermute | solution.py:15
  304.4 34.2 %all-to-all-start = ((bf16[64,32,256]{2,0,1:T(8,128)(2,1)}), bf16[64,32,256]{2,0,1:T(8,128)(2,1)S(1)}, u32[]{:S(2)}, u32[]{:S(2)}) async-start(bf16[64,32,256]{2,0,1:T(8,128)(2,1)} %copy.46), calls=%async_computation | async-start | bytes 2097152 | tf_op jit(solution)/shard_map/all_to_all | solution.py:30
  311.7 64.4 %all-gather.5.cloned.1.call-start = ((), (), s32[]{:S(2)}) async-start(), calls=%async_computation.3 | async-start | bytes 2162688 | tf_op jit(solution)/shard_map/all_gather | solution.py:117
  312.4 66.8 %copy-start.4 = (bf16[64,512]{1,0:T(8,128)(2,1)S(1)}, bf16[64,512]{1,0:T(8,128)(2,1)}, u32[]{:S(2)}) copy-start(bf16[64,512]{1,0:T(8,128)(2,1)} %add_convert_fusion) | copy-start | bytes 196612
  312.5 177.7 %reduce-scatter.2.cloned.1.call-start = ((), (), s32[]{:S(2)}) async-start(), calls=%async_computation.4 | async-start | bytes 278528 | tf_op jit(solution)/shard_map/reduce_scatter | solution.py:122
Sparse Core Ops, SparseCore 0:
  11.0 219.8 all-gather.2
  314.7 61.3 all-gather.4
  380.2 109.9 reduce-scatter.1
where the time goes:
time: 499 us; the launch traced here: 498 us
  waiting for transfers between devices  396 us (79%)
  matrix products  39.4 us (8%)
  starting transfers between devices  21.4 us (4%)
  other arithmetic  17.4 us (3%)
  between operations  14.1 us (3%)
  local copies, waits for them, and re-layouts  9.27 us (2%)
    all_gather x1, waiting for transfers between devices, shards(): full_hidden = lax.all_gather(hidden, 'pipe', axis=0, tiled=True)  214 us
    reduce_scatter x1, waiting for transfers between devices, shards(): lax.psum_scatter(hidden_part_grad.astype(jnp.bfloat16), 'pipe', scatter_d...  105 us
    all_gather x1, waiting for transfers between devices, shards(): all_grads = lax.all_gather(kv_grads, 'tensor', axis=0, tiled=True)  37.5 us
    all_to_all x1, waiting for transfers between devices, shards(): lax.all_to_all(weight, 'tensor', split_axis=1, concat_axis=0, tiled=True)  26.1 us
    ppermute x6, starting transfers between devices, swapped(): return lax.ppermute(value, axis, pairs)  13.9 us
    dot_general x8, matrix products, sweep(): jnp.einsum('rhd,jd->hrj', output_gradient, value_block, preferred_element...  13.5 us
    ppermute x6, waiting for transfers between devices, swapped(): return lax.ppermute(value, axis, pairs)  13 us
  transfers between devices with their start and end apart: 10, of which 7 were waited for; matrix products, arithmetic and copies ran while one was open for 4% of the time, Pallas kernels for 0%

commit v1 on v0

v1 whole, which is shorter than its diff:
```python
import functools

import jax
import jax.numpy as jnp
from jax import lax
from jax.experimental import pallas as pl
from jax.experimental.pallas import tpu as pltpu
from jax.sharding import Mesh, PartitionSpec as P

HEAD = 128
R = 512
POSITIONS = 1024
TOKENS = 128
SCALE = HEAD**-0.5
LOG2E = 1.4426950408889634
LOW = -1e30
PLANE = ("yh", "yl", "core")
QUAD = ("yl", "core")
NT = (((1,), (1,)), ((), ()))


def swapped(value, axes, moved):
    count = 1
    for axis in axes:
        count *= lax.axis_size(axis)
    pairs = [(source, source ^ moved) for source in range(count)]
    return lax.ppermute(value, axes, pairs)


def softmax_parts(scores, dots):
    top = jnp.max(scores, axis=0, keepdims=True)
    weights = jnp.exp2((scores - top) * (SCALE * LOG2E))
    total = jnp.sum(weights, axis=0, keepdims=True)
    accum = jnp.sum(weights * dots, axis=0, keepdims=True)
    return top, total, accum


def merged(first, second):
    top = jnp.maximum(first[0], second[0])
    fade_first = jnp.exp2((first[0] - top) * (SCALE * LOG2E))
    fade_second = jnp.exp2((second[0] - top) * (SCALE * LOG2E))
    return (
        top,
        first[1] * fade_first + second[1] * fade_second,
        first[2] * fade_first + second[2] * fade_second,
    )


def prefix_kernel(place, q0, o0, p1, p2, p3, cache, prefix_len, stats):
    rank = place[0]
    lengths = prefix_len[...]
    chunk = 512
    for other, (q, o) in enumerate(
        ((q0, o0), (p1.at[0], p1.at[1]), (p2.at[0], p2.at[1]), (p3.at[0], p3.at[1]))
    ):
        for head in range(2):
            columns = pl.ds(head * HEAD, HEAD)
            queries = q[:, columns]
            grads = o[:, columns]

            parts = None
            for start in range(0, POSITIONS, chunk):
                rows = pl.ds(start, chunk)
                scores = lax.dot_general(
                    cache[0, rows, :], queries, NT, preferred_element_type=jnp.float32
                )
                dots = lax.dot_general(
                    cache[1, rows, :], grads, NT, preferred_element_type=jnp.float32
                )
                ids = lax.broadcasted_iota(jnp.int32, (chunk, R), 0)
                limit = lengths - (rank * POSITIONS + start)
                piece = softmax_parts(jnp.where(ids < limit, scores, LOW), dots)
                parts = piece if parts is None else merged(parts, piece)
            slot = (rank ^ other) * 2 + head
            for kind in range(3):
                stats[kind, pl.ds(slot, 1), :] = parts[kind]


def new_scores(rank, ids_ref, doc_start, keys, values, queries, grads):
    scores = lax.dot_general(keys, queries, NT, preferred_element_type=jnp.float32)
    dots = lax.dot_general(values, grads, NT, preferred_element_type=jnp.float32)
    place = lax.broadcasted_iota(jnp.int32, (TOKENS, R), 0)
    token = (place // 32) * 128 + rank * 32 + place % 32
    row = lax.broadcasted_iota(jnp.int32, (TOKENS, R), 1)
    mask = (token >= doc_start) & (token <= row)
    return jnp.where(mask, scores, LOW), dots


def new_stats_kernel(place, partial, q0, o0, p1, p2, p3, doc_start, before, stats, kv):
    rank = place[0]
    total_kv = partial[0].astype(jnp.float32)
    for source in range(1, 8):
        total_kv = total_kv + partial[source].astype(jnp.float32)
    kv[...] = total_kv.astype(jnp.bfloat16)
    starts = doc_start[...]
    for other, (q, o) in enumerate(
        ((q0, o0), (p1.at[0], p1.at[1]), (p2.at[0], p2.at[1]), (p3.at[0], p3.at[1]))
    ):
        for head in range(2):
            columns = pl.ds(head * HEAD, HEAD)
            scores, dots = new_scores(
                rank, None, starts, kv[:, :HEAD], kv[:, HEAD:], q[:, columns], o[:, columns]
            )
            slot = pl.ds((rank ^ other) * 2 + head, 1)
            parts = merged(
                softmax_parts(scores, dots), tuple(before[kind, slot, :] for kind in range(3))
            )
            for kind in range(3):
                stats[kind, slot, :] = parts[kind]


def new_grads_kernel(place, kv, q0, o0, p1, p2, p3, doc_start, every, out, whole, key_sum, value_sum):
    rank = place[0]
    top = jnp.maximum(
        jnp.maximum(every[0, 0], every[1, 0]), jnp.maximum(every[2, 0], every[3, 0])
    )
    total = jnp.zeros_like(top)
    accum = jnp.zeros_like(top)
    for member in range(4):
        fade = jnp.exp2((every[member, 0] - top) * (SCALE * LOG2E))
        total = total + every[member, 1] * fade
        accum = accum + every[member, 2] * fade
    whole[0] = top
    whole[1] = 1.0 / total
    whole[2] = accum / total
    starts = doc_start[...]
    for other, (q, o) in enumerate(
        ((q0, o0), (p1.at[0], p1.at[1]), (p2.at[0], p2.at[1]), (p3.at[0], p3.at[1]))
    ):
        for head in range(2):
            columns = pl.ds(head * HEAD, HEAD)
            queries = q[:, columns]
            grads = o[:, columns]
            scores, dots = new_scores(
                rank, None, starts, kv[:, :HEAD], kv[:, HEAD:], queries, grads
            )
            slot = pl.ds((rank ^ other) * 2 + head, 1)
            quotient = jnp.exp2((scores - whole[0, slot, :]) * (SCALE * LOG2E)) * whole[1, slot, :]
            probs = quotient.astype(jnp.bfloat16)
            dscores = (quotient * (dots - whole[2, slot, :])).astype(jnp.bfloat16)
            key_part = jnp.dot(dscores, queries, preferred_element_type=jnp.float32)
            value_part = jnp.dot(probs, grads, preferred_element_type=jnp.float32)
            if other == 0 and head == 0:
                key_sum[...] = key_part
                value_sum[...] = value_part
            else:
                key_sum[...] += key_part
                value_sum[...] += value_part
    out[:, :HEAD] = (key_sum[...] * SCALE).astype(jnp.bfloat16)
    out[:, HEAD:] = value_sum[...].astype(jnp.bfloat16)


def called(kernel, out_shape, operands, flops, moved, scratch=()):
    vmem = pl.BlockSpec(memory_space=pltpu.VMEM)
    return pl.pallas_call(
        kernel,
        out_shape=out_shape,
        in_specs=[pl.BlockSpec(memory_space=pltpu.SMEM)] + [vmem] * (len(operands) - 1),
        out_specs=jax.tree.map(lambda leaf: vmem, out_shape),
        scratch_shapes=list(scratch),
        compiler_params=pltpu.CompilerParams(vmem_limit_bytes=32 * 1024 * 1024),
        cost_estimate=pl.CostEstimate(
            flops=flops, bytes_accessed=moved, transcendentals=flops // 512
        ),
    )(*operands)


def shards(hidden, kv_weight, queries, out_grads, cache, prefix_len, doc_start):
    plane_rank = lax.axis_index(PLANE)
    rank = lax.axis_index(QUAD)
    place = jnp.reshape(rank, (1,)).astype(jnp.int32)
    width = hidden.shape[1] // 8

    q0 = queries[0]
    o0 = out_grads[0]
    pair = jnp.stack([q0, o0])
    p2 = swapped(pair, QUAD, 2)
    p1 = swapped(pair, QUAD, 1)
    p3 = swapped(p2, QUAD, 1)

    turned = kv_weight[0].reshape(64, 4, 8, width // 4).transpose(2, 0, 1, 3).reshape(8, 64, width)
    turned = lax.all_to_all(turned, PLANE, 0, 0, tiled=True)

    own = lax.dynamic_index_in_dim(hidden.reshape(32, 4, 8, width // 4), plane_rank, 2, False)
    own = lax.all_gather(own.reshape(32, width), "zh", axis=0, tiled=True)
    states = lax.all_to_all(jnp.broadcast_to(own, (4, *own.shape)), "x", 0, 0, tiled=True)
    states = states.reshape(R, width)

    heads = turned.reshape(2, 256, width)
    partial = [
        lax.dot_general(states, heads[j], NT, preferred_element_type=jnp.float32).astype(
            jnp.bfloat16
        )
        for j in range(2)
    ]
    partial = jnp.stack(partial).reshape(8, TOKENS, 256)
    partial = lax.all_to_all(partial, PLANE, 0, 0, tiled=True)

    lengths = prefix_len.reshape(1, R)
    starts = doc_start.reshape(1, R)
    stats_shape = jax.ShapeDtypeStruct((3, 8, R), jnp.float32)
    before = called(
        prefix_kernel,
        stats_shape,
        (place, q0, o0, p1, p2, p3, cache[0], lengths),
        2 * 2 * 8 * R * POSITIONS * HEAD * 4,
        3 << 20,
    )
    stats, kv = called(
        new_stats_kernel,
        (stats_shape, jax.ShapeDtypeStruct((TOKENS, 256), jnp.bfloat16)),
        (place, partial, q0, o0, p1, p2, p3, starts, before),
        2 * 2 * 8 * R * TOKENS * HEAD * 4,
        3 << 20,
    )
    every = lax.all_gather(stats, QUAD, axis=0)
    grads = called(
        new_grads_kernel,
        jax.ShapeDtypeStruct((TOKENS, 256), jnp.bfloat16),
        (place, kv, q0, o0, p1, p2, p3, starts, every),
        4 * 2 * 8 * R * TOKENS * HEAD * 4,
        3 << 20,
        (
            pltpu.VMEM((3, 8, R), jnp.float32),
            pltpu.VMEM((TOKENS, HEAD), jnp.float32),
            pltpu.VMEM((TOKENS, HEAD), jnp.float32),
        ),
    )
    kv_grads = lax.all_gather(grads, PLANE, axis=0, tiled=True).reshape(2, R, 256)

    hidden_part = jnp.dot(kv_grads[0], heads[0], preferred_element_type=jnp.float32)
    hidden_part = hidden_part + jnp.dot(kv_grads[1], heads[1], preferred_element_type=jnp.float32)
    hidden_part = hidden_part.astype(jnp.bfloat16).reshape(4, 128, width)
    over_x = lax.all_to_all(hidden_part, "x", 0, 0, tiled=True)
    over_x = jnp.sum(over_x.astype(jnp.float32), axis=0).astype(jnp.bfloat16)
    over_x = over_x.reshape(4, 32, 4, width // 4).transpose(0, 2, 1, 3).reshape(16, 32, width // 4)
    over_z = lax.all_to_all(over_x, ("zh", "zl"), 0, 0, tiled=True)
    hidden_grads = jnp.sum(over_z.astype(jnp.float32), axis=0)

    weight_part = lax.dot_general(
        kv_grads, states, (((1,), (0,)), ((), ())), preferred_element_type=jnp.float32
    )
    weight_part = weight_part.astype(jnp.bfloat16).reshape(8, 64, width)
    weight_part = lax.all_to_all(weight_part, PLANE, 0, 0, tiled=True)
    weight_grads = (
        weight_part.reshape(8, 64, 4, width // 4).transpose(1, 2, 0, 3).reshape(1, 64, 8 * width)
    )
    return hidden_grads, weight_grads.astype(jnp.float32)


def solution(mesh):
    axes = ("zh", "x", "zl", "yh", "yl", "core")
    split = Mesh(mesh.devices.reshape(4, 4, 4, 2, 2, 2), axes)
    pipe = ("zh", "x")
    tensor = ("zl", "yh", "yl", "core")
    return jax.shard_map(
        shards,
        mesh=split,
        in_specs=(
            P(pipe, None),
            P(pipe, tensor, None),
            P(pipe, None, tensor),
            P(pipe, None, tensor),
            P(pipe, None, tensor, None),
            P(),
            P(),
        ),
        out_specs=(P(pipe, tensor), P(pipe, tensor, None)),
        check_vma=False,
    )
```

time: 499 us -> 168 us (0.34)
  waiting for transfers between devices: 396 us -> 47.1 us
  blocking collectives: 0 us -> 41.6 us
  matrix products: 39.4 us -> 8.53 us
  starting transfers between devices: 21.4 us -> 41.5 us
  other arithmetic: 17.4 us -> 1.69 us
  between operations: 14.1 us -> 0.88 us
  Pallas kernels: 0 us -> 9.67 us
  local copies, waits for them, and re-layouts: 9.27 us -> 14.8 us
    all_gather x2 -> x0, waiting for transfers between devices: 252 us -> none  [the longest x1 214 us: shards(): full_hidden = lax.all_gather(hidden, 'pipe', axis=0, tiled=True)]
    reduce_scatter x1 -> x0, waiting for transfers between devices: 105 us -> none  [shards(): lax.psum_scatter(hidden_part_grad.astype(jnp.bfloat16), 'pipe', scatter_d...]
    all_gather x0 -> x3, blocking collectives: none -> 41.6 us  [the longest x1 22.5 us: shards(): own = lax.all_gather(own.reshape(32, width), 'zh', axis=0, tiled=True)]
    dot_general x23 -> x5, matrix products: 39.4 us -> 8.53 us  [the longest x2 3.72 us: shards(): lax.dot_general(states, heads[j], NT, preferred_element_type=jnp.float32)]
    all_to_all x1 -> x6, starting transfers between devices: 7.32 us -> 34.4 us  [the longest x1 9.22 us: shards(): turned = lax.all_to_all(turned, PLANE, 0, 0, tiled=True)]
    all_to_all x1 -> x6, waiting for transfers between devices: 26.1 us -> 47.1 us  [the longest x1 12.9 us: shards(): over_x = lax.all_to_all(hidden_part, 'x', 0, 0, tiled=True)]
    ppermute x6 -> x3, waiting for transfers between devices: 13 us -> 0.01 us  [swapped(): return lax.ppermute(value, axes, pairs)]
    pallas_call x0 -> x3, Pallas kernels: none -> 9.67 us  [called(): pl.pallas_call(kernel, out_shape=out_shape, in_specs=[pl.BlockSpec(memory...]
  transfers between devices with their start and end apart: 10 -> 9, of which waited for: 7 -> 5; matrix products, arithmetic and copies ran while one was open for 4% -> 12% of each run, Pallas kernels for 0% -> 4%
where the time goes in v1:
time: 168 us; the launch traced here: 166 us
  waiting for transfers between devices  47.1 us (28%)
  blocking collectives  41.6 us (25%)
  starting transfers between devices  41.5 us (25%)
  local copies, waits for them, and re-layouts  14.8 us (9%)
  Pallas kernels  9.67 us (6%)
  matrix products  8.53 us (5%)
  other arithmetic  1.69 us (1%)
    all_gather x1, blocking collectives, shards(): own = lax.all_gather(own.reshape(32, width), 'zh', axis=0, tiled=True)  22.5 us
    all_gather x1, blocking collectives, shards(): lax.all_gather(grads, PLANE, axis=0, tiled=True).reshape(2, R, 256)  13.2 us
    all_to_all x1, waiting for transfers between devices, shards(): over_x = lax.all_to_all(hidden_part, 'x', 0, 0, tiled=True)  12.9 us
    all_to_all x1, waiting for transfers between devices, shards(): weight_part = lax.all_to_all(weight_part, PLANE, 0, 0, tiled=True)  12.7 us
    all_to_all x1, waiting for transfers between devices, shards(): over_z = lax.all_to_all(over_x, ('zh', 'zl'), 0, 0, tiled=True)  12.1 us
    pallas_call x3, Pallas kernels, called(): pl.pallas_call(kernel, out_shape=out_shape, in_specs=[pl.BlockSpec(memory...  9.67 us
    all_to_all x1, starting transfers between devices, shards(): turned = lax.all_to_all(turned, PLANE, 0, 0, tiled=True)  9.22 us
    all_to_all x1, waiting for transfers between devices, shards(): lax.all_to_all(jnp.broadcast_to(own, (4, *own.shape)), 'x', 0, 0, tiled=T...  7.48 us
  transfers between devices with their start and end apart: 9, of which 5 were waited for; matrix products, arithmetic and copies ran while one was open for 12% of the time, Pallas kernels for 4%

profile of v1, /device:TPU:24, one launch (start us, length us, event | category | flops | bytes accessed | tf_op | source)
XLA Modules:
  0.0 165.8 jit_solution(16918084702684557707)
XLA Ops:
  4.1 9.2 %all-to-all-start.1 = ((bf16[8,64,1024]{2,1,0:T(8,128)(2,1)}), bf16[8,64,1024]{2,1,0:T(8,128)(2,1)S(1)}, u32[]{:S(2)}, u32[]{:S(2)}) async-start(bf16[8,64,1024]{2,1,0:T(8,128)(2,1)} %reshape.75), calls=%async_computation.1 | async-start | bytes 2097152 | tf_op jit(solution)/shard_map/all_to_all | solution.py:182
  14.8 2.7 %collective-permute-start.1 = (bf16[2,512,256]{2,1,0:T(8,128)(2,1)}, bf16[2,512,256]{2,1,0:T(8,128)(2,1)S(1)}, u32[]{:S(2)}, u32[]{:S(2)}) collective-permute-start(bf16[2,512,256]{2,1,0:T(8,128)(2,1)} %constant_dynamic-update-slice_fusion), channel_id=1, source_target_pairs={{0,2},{1,3},{2,0},{3,1},{4,6},{5,7},{6,4},{7,5},{8,10},{9,11},{10,... | collective-permute-start | bytes 1572872 | tf_op jit(solution)/shard_map/ppermute | solution.py:27
  18.1 22.5 %all_gather.12 = bf16[128,1024]{1,0:T(8,128)(2,1)S(1)} all-gather(bf16[32,1024]{1,0:T(8,128)(2,1)S(1)} %bitcast.72), channel_id=1, replica_groups=mesh['zh'=4,'x'=4,'zl'=4,'yh'=2,'yl'=2,'core'=2] {'zh'}, dimensions={0}, use_global_device_ids=true | all-gather | bytes 327680 | tf_op jit(solution)/shard_map/all_gather | solution.py:185
  41.8 4.3 %all-to-all-start = ((bf16[4,128,1024]{2,1,0:T(8,128)(2,1)}), bf16[4,128,1024]{2,1,0:T(8,128)(2,1)}, u32[]{:S(2)}, u32[]{:S(2)}) async-start(bf16[4,128,1024]{2,1,0:T(8,128)(2,1)} %broadcast_in_dim.3), calls=%async_computation | async-start | bytes 2097152 | tf_op jit(solution)/shard_map/all_to_all | solution.py:186
  46.1 1.9 %collective-permute-start = (bf16[2,512,256]{2,1,0:T(8,128)(2,1)}, bf16[2,512,256]{2,1,0:T(8,128)(2,1)S(1)}, u32[]{:S(2)}, u32[]{:S(2)}) collective-permute-start(bf16[2,512,256]{2,1,0:T(8,128)(2,1)} %constant_dynamic-update-slice_fusion), channel_id=1, source_target_pairs={{0,1},{1,0},{2,3},{3,2},{4,5},{5,4},{6,7},{7,6},{8,9},{9,8},{10,11... | collective-permute-start | bytes 1572872 | tf_op jit(solution)/shard_map/ppermute | solution.py:27
  48.0 2.4 %collective-permute-start.2 = (bf16[2,512,256]{2,1,0:T(8,128)(2,1)S(1)}, bf16[2,512,256]{2,1,0:T(8,128)(2,1)S(1)}, u32[]{:S(2)}, u32[]{:S(2)}) collective-permute-start(bf16[2,512,256]{2,1,0:T(8,128)(2,1)S(1)} %collective-permute-done.1.p2), channel_id=1, source_target_pairs={{0,1},{1,0},{2,3},{3,2},{4,5},{5,4},{6,7},{7,6},{8,9},{9,8},{10,11... | collective-permute-start | bytes 1572872 | tf_op jit(solution)/shard_map/ppermute | solution.py:27
  51.5 7.5 %all-to-all-done = bf16[4,128,1024]{2,1,0:T(8,128)(2,1)} async-done(((bf16[4,128,1024]{2,1,0:T(8,128)(2,1)}), bf16[4,128,1024]{2,1,0:T(8,128)(2,1)}, u32[]{:S(2)}, u32[]{:S(2)}) %all-to-all-start) | async-done | bytes 1048608 | tf_op jit(solution)/shard_map/all_to_all | solution.py:186
  59.0 1.8 %fusion.1 = bf16[1,512,256]{2,1,0:T(8,128)(2,1)S(1)} fusion(bf16[512,1024]{1,0:T(8,128)(2,1)} %bitcast.1, bf16[256,1024]{1,0:T(8,128)(2,1)} %bitcast.64), kind=kOutput, calls=%fused_computation.6 | convolution fusion | flops 268566528 | bytes 1835008 | tf_op jit(solution)/shard_map/dot_general | solution.py:191
  60.8 1.9 %fusion = bf16[1,512,256]{2,1,0:T(8,128)(2,1)S(1)} fusion(bf16[512,1024]{1,0:T(8,128)(2,1)} %bitcast.1, bf16[256,1024]{1,0:T(8,128)(2,1)} %bitcast.61), kind=kOutput, calls=%fused_computation.5 | convolution fusion | flops 268566528 | bytes 1835008 | tf_op jit(solution)/shard_map/dot_general | solution.py:191
  63.6 5.1 %all-to-all-start.2 = ((bf16[8,128,256]{2,1,0:T(8,128)(2,1)}), bf16[8,128,256]{2,1,0:T(8,128)(2,1)S(1)}, u32[]{:S(2)}, u32[]{:S(2)}) async-start(bf16[8,128,256]{2,1,0:T(8,128)(2,1)} %bitcast.63), calls=%async_computation.2 | async-start | bytes 1048576 | tf_op jit(solution)/shard_map/all_to_all | solution.py:197
  68.7 6.3 %shard_map.86.before = f32[3,8,512]{2,1,0:T(8,128)S(1)} custom-call(s32[1]{0:T(128)} %bitcast.place, bf16[512,256]{1,0:T(8,128)(2,1)S(1)} %bitcast.47, bf16[512,256]{1,0:T(8,128)(2,1)S(1)} %bitcast.50, bf16[2,512,256]{2,1,0:T(8,128)(2,1)S(1)} %collective-permute-done.p1, bf16[2,512,256]{2,1,0:T(8,128)(2,1)S(1)} %collective-permute-done.1.p2, ...), custom_call_target="tpu_custom_call" | custom-call | flops 8589934592 | bytes 3145728 | tf_op jit(solution)/shard_map/pallas_call | solution.py:155
  75.1 1.9 %all-to-all-done.2.partial = bf16[8,128,256]{2,1,0:T(8,128)(2,1)S(1)} async-done(((bf16[8,128,256]{2,1,0:T(8,128)(2,1)}), bf16[8,128,256]{2,1,0:T(8,128)(2,1)S(1)}, u32[]{:S(2)}, u32[]{:S(2)}) %all-to-all-start.2) | async-done | bytes 524320 | tf_op jit(solution)/shard_map/all_to_all | solution.py:197
  78.1 5.8 %all-gather = f32[12,8,512]{2,1,0:T(8,128)S(1)} all-gather(f32[3,8,512]{2,1,0:T(8,128)S(1)} %get-tuple-element.5), channel_id=2, replica_groups=mesh['zh'=4,'x'=4,'zl'=4,'yh'=2,'yl'=2,'core'=2] {'yl','core'}, dimensions={0}, use_global_device_ids=true | all-gather | bytes 245760 | tf_op jit(solution)/shard_map/all_gather | solution.py:216
  83.9 2.2 %shard_map.88 = bf16[128,256]{1,0:T(8,128)(2,1)S(1)} custom-call(s32[1]{0:T(128)} %bitcast.place, bf16[128,256]{1,0:T(8,128)(2,1)S(1)} %get-tuple-element.4.kv, bf16[512,256]{1,0:T(8,128)(2,1)S(1)} %bitcast.49, bf16[512,256]{1,0:T(8,128)(2,1)S(1)} %bitcast.52, bf16[2,512,256]{2,1,0:T(8,128)(2,1)S(1)} %collective-permute-done.p1, ...), custom_call_target="tpu_custom_call" | custom-call | flops 2147483648 | bytes 3145728 | tf_op jit(solution)/shard_map/pallas_call | solution.py:155
  86.1 13.2 %all_gather.15 = bf16[1024,256]{1,0:T(8,128)(2,1)S(1)} all-gather(bf16[128,256]{1,0:T(8,128)(2,1)S(1)} %shard_map.88), channel_id=1, replica_groups=mesh['zh'=4,'x'=4,'zl'=4,'yh'=2,'yl'=2,'core'=2] {'yh','yl','core'}, dimensions={0}, use_global_device_ids=true | all-gather | bytes 589824 | tf_op jit(solution)/shard_map/all_gather | solution.py:229
  101.3 3.5 %all-to-all-start.3 = ((bf16[4,128,1024]{2,1,0:T(8,128)(2,1)}), bf16[4,128,1024]{2,1,0:T(8,128)(2,1)S(1)}, u32[]{:S(2)}, u32[]{:S(2)}) async-start(bf16[4,128,1024]{2,1,0:T(8,128)(2,1)} %bitcast.14), calls=%async_computation.3 | async-start | bytes 2097152 | tf_op jit(solution)/shard_map/all_to_all | solution.py:234
  104.8 2.9 %convolution_convert_fusion = bf16[2,256,1024]{2,1,0:T(8,128)(2,1)} fusion(bf16[2,512,256]{2,1,0:T(8,128)(2,1)S(1)} %bitcast.66, bf16[512,1024,1]{1,0,2:T(8,128)(2,1)} %bitcast.18), kind=kOutput, calls=%fused_computation.2 | convolution fusion | flops 537395200 | bytes 2621440 | tf_op jit(solution)/shard_map/dot_general | solution.py:240
  107.7 12.9 %all-to-all-done.3 = bf16[4,128,1024]{2,1,0:T(8,128)(2,1)S(1)} async-done(((bf16[4,128,1024]{2,1,0:T(8,128)(2,1)}), bf16[4,128,1024]{2,1,0:T(8,128)(2,1)S(1)}, u32[]{:S(2)}, u32[]{:S(2)}) %all-to-all-start.3) | async-done | bytes 1048608 | tf_op jit(solution)/shard_map/all_to_all | solution.py:234
  120.6 5.6 %all-to-all-start.5 = ((bf16[8,64,1024]{2,1,0:T(8,128)(2,1)}), bf16[8,64,1024]{2,1,0:T(8,128)(2,1)S(1)}, u32[]{:S(2)}, u32[]{:S(2)}) async-start(bf16[8,64,1024]{2,1,0:T(8,128)(2,1)} %bitcast.19), calls=%async_computation.5 | async-start | bytes 2097152 | tf_op jit(solution)/shard_map/all_to_all | solution.py:244
  127.3 12.7 %all-to-all-done.5 = bf16[8,64,1024]{2,1,0:T(8,128)(2,1)S(1)} async-done(((bf16[8,64,1024]{2,1,0:T(8,128)(2,1)}), bf16[8,64,1024]{2,1,0:T(8,128)(2,1)S(1)}, u32[]{:S(2)}, u32[]{:S(2)}) %all-to-all-start.5) | async-done | bytes 1048608 | tf_op jit(solution)/shard_map/all_to_all | solution.py:244
  140.1 6.7 %all-to-all-start.4 = ((bf16[16,32,256]{2,1,0:T(8,128)(2,1)}), bf16[16,32,256]{2,1,0:T(8,128)(2,1)S(1)}, u32[]{:S(2)}, u32[]{:S(2)}) async-start(bf16[16,32,256]{2,1,0:T(8,128)(2,1)} %bitcast.16), calls=%async_computation.4 | async-start | bytes 524288 | tf_op jit(solution)/shard_map/all_to_all | solution.py:237
  147.8 2.5 %copy.32 = f32[8,64,4,256]{3,0,2,1:T(8,128)} copy(f32[8,64,4,256]{3,2,1,0:T(4,128)S(1)} %reshape.85) | data formatting | bytes 4194304 | tf_op jit(solution)/shard_map/convert_element_type | solution.py:248
  150.3 2.7 %reshape.84 = f32[1,64,8192]{2,1,0:T(8,128)} reshape(f32[64,4,8,256]{3,2,1,0:T(8,128)} %bitcast.58) | data formatting | bytes 4194304 | tf_op jit(solution)/shard_map/convert_element_type | solution.py:248
  153.1 12.1 %all-to-all-done.4 = bf16[16,32,256]{2,1,0:T(8,128)(2,1)S(1)} async-done(((bf16[16,32,256]{2,1,0:T(8,128)(2,1)}), bf16[16,32,256]{2,1,0:T(8,128)(2,1)S(1)}, u32[]{:S(2)}, u32[]{:S(2)}) %all-to-all-start.4) | async-done | bytes 262176 | tf_op jit(solution)/shard_map/all_to_all | solution.py:237
  (39 shorter events, 14.3 us)
Async XLA Ops:
  2.5 10.8 %copy-start = (bf16[1,512,256]{2,1,0:T(8,128)(2,1)S(1)}, bf16[1,512,256]{2,1,0:T(8,128)(2,1)}, u32[]{:S(2)}) copy-start(bf16[1,512,256]{2,1,0:T(8,128)(2,1)} %param.9) | copy-start | bytes 786436
  2.5 11.5 %copy-start.1 = (bf16[1,512,256]{2,1,0:T(8,128)(2,1)S(1)}, bf16[1,512,256]{2,1,0:T(8,128)(2,1)}, u32[]{:S(2)}) copy-start(bf16[1,512,256]{2,1,0:T(8,128)(2,1)} %param.10) | copy-start | bytes 786436
  4.1 13.4 %copy-start.7 = (bf16[32,8192]{1,0:T(8,128)(2,1)S(1)}, bf16[32,8192]{1,0:T(8,128)(2,1)}, u32[]{:S(2)}) copy-start(bf16[32,8192]{1,0:T(8,128)(2,1)} %param.7) | copy-start | bytes 1572868
  4.1 36.6 %all-to-all-start.1 = ((bf16[8,64,1024]{2,1,0:T(8,128)(2,1)}), bf16[8,64,1024]{2,1,0:T(8,128)(2,1)S(1)}, u32[]{:S(2)}, u32[]{:S(2)}) async-start(bf16[8,64,1024]{2,1,0:T(8,128)(2,1)} %reshape.75), calls=%async_computation.1 | async-start | bytes 2097152 | tf_op jit(solution)/shard_map/all_to_all | solution.py:182
  14.8 33.2 %collective-permute-start.1 = (bf16[2,512,256]{2,1,0:T(8,128)(2,1)}, bf16[2,512,256]{2,1,0:T(8,128)(2,1)S(1)}, u32[]{:S(2)}, u32[]{:S(2)}) collective-permute-start(bf16[2,512,256]{2,1,0:T(8,128)(2,1)} %constant_dynamic-update-slice_fusion), channel_id=1, source_target_pairs={{0,2},{1,3},{2,0},{3,1},{4,6},{5,7},{6,4},{7,5},{8,10},{9,11},{10,... | collective-permute-start | bytes 1572872 | tf_op jit(solution)/shard_map/ppermute | solution.py:27
  41.8 17.2 %all-to-all-start = ((bf16[4,128,1024]{2,1,0:T(8,128)(2,1)}), bf16[4,128,1024]{2,1,0:T(8,128)(2,1)}, u32[]{:S(2)}, u32[]{:S(2)}) async-start(bf16[4,128,1024]{2,1,0:T(8,128)(2,1)} %broadcast_in_dim.3), calls=%async_computation | async-start | bytes 2097152 | tf_op jit(solution)/shard_map/all_to_all | solution.py:186
  46.1 22.6 %collective-permute-start = (bf16[2,512,256]{2,1,0:T(8,128)(2,1)}, bf16[2,512,256]{2,1,0:T(8,128)(2,1)S(1)}, u32[]{:S(2)}, u32[]{:S(2)}) collective-permute-start(bf16[2,512,256]{2,1,0:T(8,128)(2,1)} %constant_dynamic-update-slice_fusion), channel_id=1, source_target_pairs={{0,1},{1,0},{2,3},{3,2},{4,5},{5,4},{6,7},{7,6},{8,9},{9,8},{10,11... | collective-permute-start | bytes 1572872 | tf_op jit(solution)/shard_map/ppermute | solution.py:27
  48.0 20.7 %collective-permute-start.2 = (bf16[2,512,256]{2,1,0:T(8,128)(2,1)S(1)}, bf16[2,512,256]{2,1,0:T(8,128)(2,1)S(1)}, u32[]{:S(2)}, u32[]{:S(2)}) collective-permute-start(bf16[2,512,256]{2,1,0:T(8,128)(2,1)S(1)} %collective-permute-done.1.p2), channel_id=1, source_target_pairs={{0,1},{1,0},{2,3},{3,2},{4,5},{5,4},{6,7},{7,6},{8,9},{9,8},{10,11... | collective-permute-start | bytes 1572872 | tf_op jit(solution)/shard_map/ppermute | solution.py:27
  60.8 7.9 %copy-start.2 = (bf16[1,2,1024,128]{3,2,1,0:T(8,128)(2,1)S(1)}, bf16[1,2,1024,128]{3,2,1,0:T(8,128)(2,1)}, u32[]{:S(2)}) copy-start(bf16[1,2,1024,128]{3,2,1,0:T(8,128)(2,1)} %param.11) | copy-start | bytes 1572868
  60.8 7.9 %copy-start.3 = (s32[512]{0:T(512)S(1)}, s32[512]{0:T(512)}, u32[]{:S(2)}) copy-start(s32[512]{0:T(512)} %param.12) | copy-start | bytes 6148
  63.6 13.4 %all-to-all-start.2 = ((bf16[8,128,256]{2,1,0:T(8,128)(2,1)}), bf16[8,128,256]{2,1,0:T(8,128)(2,1)S(1)}, u32[]{:S(2)}, u32[]{:S(2)}) async-start(bf16[8,128,256]{2,1,0:T(8,128)(2,1)} %bitcast.63), calls=%async_computation.2 | async-start | bytes 1048576 | tf_op jit(solution)/shard_map/all_to_all | solution.py:197
  68.7 8.3 %copy-start.4 = (s32[512]{0:T(512)S(1)}, s32[512]{0:T(512)}, u32[]{:S(2)}) copy-start(s32[512]{0:T(512)} %param.13) | copy-start | bytes 6148
  83.9 15.5 %copy-start.6 = (bf16[4,64,1024]{2,1,0:T(8,128)(2,1)S(1)}, bf16[4,64,1024]{2,1,0:T(8,128)(2,1)}, u32[]{:S(2)}) copy-start(bf16[4,64,1024]{2,1,0:T(8,128)(2,1)} %get-tuple-element.7) | copy-start | bytes 1572868
  86.1 13.7 %copy-start.5 = (bf16[4,64,1024]{2,1,0:T(8,128)(2,1)S(1)}, bf16[4,64,1024]{2,1,0:T(8,128)(2,1)}, u32[]{:S(2)}) copy-start(bf16[4,64,1024]{2,1,0:T(8,128)(2,1)} %get-tuple-element.6) | copy-start | bytes 1572868
  101.3 19.4 %all-to-all-start.3 = ((bf16[4,128,1024]{2,1,0:T(8,128)(2,1)}), bf16[4,128,1024]{2,1,0:T(8,128)(2,1)S(1)}, u32[]{:S(2)}, u32[]{:S(2)}) async-start(bf16[4,128,1024]{2,1,0:T(8,128)(2,1)} %bitcast.14), calls=%async_computation.3 | async-start | bytes 2097152 | tf_op jit(solution)/shard_map/all_to_all | solution.py:234
  120.6 19.4 %all-to-all-start.5 = ((bf16[8,64,1024]{2,1,0:T(8,128)(2,1)}), bf16[8,64,1024]{2,1,0:T(8,128)(2,1)S(1)}, u32[]{:S(2)}, u32[]{:S(2)}) async-start(bf16[8,64,1024]{2,1,0:T(8,128)(2,1)} %bitcast.19), calls=%async_computation.5 | async-start | bytes 2097152 | tf_op jit(solution)/shard_map/all_to_all | solution.py:244
  140.1 25.1 %all-to-all-start.4 = ((bf16[16,32,256]{2,1,0:T(8,128)(2,1)}), bf16[16,32,256]{2,1,0:T(8,128)(2,1)S(1)}, u32[]{:S(2)}, u32[]{:S(2)}) async-start(bf16[16,32,256]{2,1,0:T(8,128)(2,1)} %bitcast.16), calls=%async_computation.4 | async-start | bytes 524288 | tf_op jit(solution)/shard_map/all_to_all | solution.py:237

commit v2 on v1

v2 whole, which is shorter than its diff:
```python
import functools

import jax
import jax.numpy as jnp
from jax import lax
from jax.experimental import pallas as pl
from jax.experimental.pallas import tpu as pltpu
from jax.sharding import Mesh, PartitionSpec as P

HEAD = 128
R = 512
POSITIONS = 1024
TOKENS = 128
SCALE = HEAD**-0.5
LOG2E = 1.4426950408889634
LOW = -1e30
PLANE = ("yh", "yl", "core")
QUAD = ("yl", "core")
NT = (((1,), (1,)), ((), ()))


def swapped(value, axes, moved):
    count = 1
    for axis in axes:
        count *= lax.axis_size(axis)
    pairs = [(source, source ^ moved) for source in range(count)]
    return lax.ppermute(value, axes, pairs)


def softmax_parts(scores, dots):
    top = jnp.max(scores, axis=0, keepdims=True)
    weights = jnp.exp2((scores - top) * (SCALE * LOG2E))
    total = jnp.sum(weights, axis=0, keepdims=True)
    accum = jnp.sum(weights * dots, axis=0, keepdims=True)
    return top, total, accum


def merged(first, second):
    top = jnp.maximum(first[0], second[0])
    fade_first = jnp.exp2((first[0] - top) * (SCALE * LOG2E))
    fade_second = jnp.exp2((second[0] - top) * (SCALE * LOG2E))
    return (
        top,
        first[1] * fade_first + second[1] * fade_second,
        first[2] * fade_first + second[2] * fade_second,
    )


def fetch(moves, sems):
    copies = [
        pltpu.make_async_copy(source, target, sems.at[index])
        for index, (source, target) in enumerate(moves)
    ]
    for copy in copies:
        copy.start()
    return copies


def fetch_pairs(sources, pairs, sems):
    moves = []
    for index, source in enumerate(sources):
        if isinstance(source, tuple):
            moves += [(part, pairs.at[index, kind]) for kind, part in enumerate(source)]
        else:
            moves += [(source.at[kind], pairs.at[index, kind]) for kind in range(2)]
    return fetch(moves, sems)


def prefix_stats(rank, lengths, sources, cache, stats, blocks, pairs, sems):
    chunk = 512
    base = pltpu.make_async_copy(cache, blocks, sems.at[4])
    base.start()
    copies = fetch_pairs(sources, pairs, sems)
    base.wait()
    for other in range(2):
        copies[2 * other].wait()
        copies[2 * other + 1].wait()
        for head in range(2):
            columns = pl.ds(head * HEAD, HEAD)
            queries = pairs[other, 0, :, columns]
            grads = pairs[other, 1, :, columns]
            parts = None
            for start in range(0, POSITIONS, chunk):
                rows = pl.ds(start, chunk)
                scores = lax.dot_general(
                    blocks[0, rows, :], queries, NT, preferred_element_type=jnp.float32
                )
                dots = lax.dot_general(
                    blocks[1, rows, :], grads, NT, preferred_element_type=jnp.float32
                )
                ids = lax.broadcasted_iota(jnp.int32, (chunk, R), 0)
                limit = lengths - (rank * POSITIONS + start)
                piece = softmax_parts(jnp.where(ids < limit, scores, LOW), dots)
                parts = piece if parts is None else merged(parts, piece)
            for kind in range(3):
                stats[kind, pl.ds(other * 2 + head, 1), :] = parts[kind]


def near_prefix_kernel(place, prefix_len, cache, q0, o0, p1, stats, *scratch):
    prefix_stats(place[0], prefix_len[...], ((q0, o0), p1), cache, stats, *scratch)


def far_prefix_kernel(place, prefix_len, cache, p2, p3, stats, *scratch):
    prefix_stats(place[0], prefix_len[...], (p2, p3), cache, stats, *scratch)


def new_scores(rank, doc_start, keys, values, queries, grads):
    scores = lax.dot_general(keys, queries, NT, preferred_element_type=jnp.float32)
    dots = lax.dot_general(values, grads, NT, preferred_element_type=jnp.float32)
    place = lax.broadcasted_iota(jnp.int32, (TOKENS, R), 0)
    token = (place // 32) * 128 + rank * 32 + place % 32
    row = lax.broadcasted_iota(jnp.int32, (TOKENS, R), 1)
    mask = (token >= doc_start) & (token <= row)
    return jnp.where(mask, scores, LOW), dots


def new_stats_kernel(
    place, doc_start, first, second, partial, q0, o0, p1, p2, p3, stats, kv, pairs, blocks, sems
):
    rank = place[0]
    base = pltpu.make_async_copy(partial, blocks, sems.at[8])
    base.start()
    copies = fetch_pairs(((q0, o0), p1, p2, p3), pairs, sems)
    base.wait()
    total_kv = blocks[0].astype(jnp.float32)
    for source in range(1, 8):
        total_kv = total_kv + blocks[source].astype(jnp.float32)
    kv[...] = total_kv.astype(jnp.bfloat16)
    starts = doc_start[...]
    for other in range(4):
        copies[2 * other].wait()
        copies[2 * other + 1].wait()
        before = first if other < 2 else second
        for head in range(2):
            columns = pl.ds(head * HEAD, HEAD)
            scores, dots = new_scores(
                rank,
                starts,
                kv[:, :HEAD],
                kv[:, HEAD:],
                pairs[other, 0, :, columns],
                pairs[other, 1, :, columns],
            )
            held = pl.ds(other % 2 * 2 + head, 1)
            parts = merged(
                softmax_parts(scores, dots), tuple(before[kind, held, :] for kind in range(3))
            )
            slot = pl.ds((rank ^ other) * 2 + head, 1)
            for kind in range(3):
                stats[kind, slot, :] = parts[kind]


def new_grads_kernel(
    place, kv, pairs, doc_start, every, out, whole, key_sum, value_sum
):
    rank = place[0]
    top = jnp.maximum(
        jnp.maximum(every[0, 0], every[1, 0]), jnp.maximum(every[2, 0], every[3, 0])
    )
    total = jnp.zeros_like(top)
    accum = jnp.zeros_like(top)
    for member in range(4):
        fade = jnp.exp2((every[member, 0] - top) * (SCALE * LOG2E))
        total = total + every[member, 1] * fade
        accum = accum + every[member, 2] * fade
    whole[0] = top
    whole[1] = 1.0 / total
    whole[2] = accum / total
    starts = doc_start[...]
    for other in range(4):
        for head in range(2):
            columns = pl.ds(head * HEAD, HEAD)
            queries = pairs[other, 0, :, columns]
            grads = pairs[other, 1, :, columns]
            scores, dots = new_scores(
                rank, starts, kv[:, :HEAD], kv[:, HEAD:], queries, grads
            )
            slot = pl.ds((rank ^ other) * 2 + head, 1)
            quotient = jnp.exp2((scores - whole[0, slot, :]) * (SCALE * LOG2E)) * whole[1, slot, :]
            probs = quotient.astype(jnp.bfloat16)
            dscores = (quotient * (dots - whole[2, slot, :])).astype(jnp.bfloat16)
            key_part = jnp.dot(dscores, queries, preferred_element_type=jnp.float32)
            value_part = jnp.dot(probs, grads, preferred_element_type=jnp.float32)
            if other == 0 and head == 0:
                key_sum[...] = key_part
                value_sum[...] = value_part
            else:
                key_sum[...] += key_part
                value_sum[...] += value_part
    out[:, :HEAD] = (key_sum[...] * SCALE).astype(jnp.bfloat16)
    out[:, HEAD:] = value_sum[...].astype(jnp.bfloat16)


def arrange_kernel(
    place, weight, hidden, queries, grads, turned, own, pair, blocks, both, arrived, left
):
    width = own.shape[1] // 4
    columns = [pl.ds(part * width, width) for part in range(4)]
    moves = [
        (weight.at[:, pl.ds((part * 8 + member) * width, width)], blocks.at[member, :, columns[part]])
        for member in range(8)
        for part in range(4)
    ]
    for part in range(4):
        start = pl.multiple_of((part * 8 + place[0]) * width, width)
        moves.append((hidden.at[:, pl.ds(start, width)], own.at[:, columns[part]]))
    moves += [(queries, both.at[0]), (grads, both.at[1])]
    copies = fetch(moves, arrived)
    sent = [
        pltpu.make_async_copy(blocks.at[member], turned.at[member], left.at[member])
        for member in range(8)
    ]
    sent += [pltpu.make_async_copy(both.at[kind], pair.at[kind], left.at[8 + kind]) for kind in range(2)]
    for member in range(8):
        for copy in copies[4 * member : 4 * member + 4]:
            copy.wait()
        sent[member].start()
    for kind in range(2):
        copies[36 + kind].wait()
        sent[8 + kind].start()
    for copy in copies[32:36] + sent:
        copy.wait()


def repeat_kernel(block, out):
    for index in range(out.shape[0]):
        out[index] = block[...]


def project_kernel(states, heads, out):
    for head in range(2):
        product = lax.dot_general(
            states[...], heads[head], NT, preferred_element_type=jnp.float32
        ).astype(jnp.bfloat16)
        for quarter in range(4):
            out[head * 4 + quarter] = product[quarter * TOKENS : (quarter + 1) * TOKENS]


def hidden_kernel(kv_grads, heads, out, parts, sems):
    copies = []
    for quarter in range(4):
        rows = pl.ds(quarter * TOKENS, TOKENS)
        parts[quarter] = (
            jnp.dot(kv_grads[0, rows, :], heads[0], preferred_element_type=jnp.float32)
            + jnp.dot(kv_grads[1, rows, :], heads[1], preferred_element_type=jnp.float32)
        ).astype(jnp.bfloat16)
        copy = pltpu.make_async_copy(parts.at[quarter], out.at[quarter], sems.at[quarter])
        copy.start()
        copies.append(copy)
    for copy in copies:
        copy.wait()


def weight_kernel(place, kv_grads, states, mine, one, three, rows):
    for head in range(2):
        rows[head * 256 : (head + 1) * 256, :] = lax.dot_general(
            kv_grads[head],
            states[...],
            (((0,), (0,)), ((), ())),
            preferred_element_type=jnp.float32,
        ).astype(jnp.bfloat16)

    def block(chip, core, start, count):
        first = ((place[0] // 2) ^ chip) * 128 + core * 64 + start
        return rows[pl.ds(pl.multiple_of(first, 32), count), :]

    for core in range(2):
        mine[core] = block(0, core, 0, 64)
        one[core, :64] = block(1, core, 0, 64)
        one[core, 64:] = block(2, core, 0, 32)
        three[core, :64] = block(3, core, 0, 64)
        three[core, 64:] = block(2, core, 32, 32)


def cores_kernel(place, mine, one, three, upper, lower, kept, passed):
    for out, core in ((kept, place[0] % 2), (passed, 1 - place[0] % 2)):
        out[0] = mine[core]
        out[1] = one[core, :64]
        out[2, :32] = upper[core]
        out[2, 32:] = lower[core]
        out[3] = three[core, :64]


def place_kernel(place, kept, taken, out):
    width = kept.shape[2] // 4
    for chip in range(4):
        for core, blocks in enumerate((kept, taken)):
            for part in range(4):
                member = place[0] ^ (chip * 2 + core)
                start = pl.multiple_of((part * 8 + member) * width, width)
                out[0, :, pl.ds(start, width)] = blocks[
                    chip, :, part * width : (part + 1) * width
                ].astype(jnp.float32)


def reduce_x_kernel(blocks, out):
    width = blocks.shape[2] // 4
    for high in range(4):
        rows = pl.ds(high * 32, 32)
        total = blocks[0, rows, :].astype(jnp.float32)
        for source in range(1, 4):
            total = total + blocks[source, rows, :].astype(jnp.float32)
        total = total.astype(jnp.bfloat16)
        for low in range(4):
            out[high * 4 + low] = total[:, low * width : (low + 1) * width]


def called(
    kernel, out_shape, operands, flops, moved, scratch=(), places=(), outs=None, limit=12, grid=()
):
    vmem = pl.BlockSpec(memory_space=pltpu.VMEM)
    return pl.pallas_call(
        kernel,
        grid=grid,
        out_shape=out_shape,
        in_specs=list(places) + [vmem] * (len(operands) - len(places)),
        out_specs=jax.tree.map(lambda leaf: vmem, out_shape) if outs is None else outs,
        scratch_shapes=list(scratch),
        compiler_params=pltpu.CompilerParams(vmem_limit_bytes=limit * 1024 * 1024),
        cost_estimate=pl.CostEstimate(
            flops=flops, bytes_accessed=moved, transcendentals=flops // 512
        ),
    )(*operands)


def shaped(dtype, *shape):
    return jax.ShapeDtypeStruct(shape, dtype)


def shards(hidden, kv_weight, queries, out_grads, cache, prefix_len, doc_start):
    plane_rank = lax.axis_index(PLANE)
    rank = lax.axis_index(QUAD)
    member = jnp.reshape(plane_rank, (1,)).astype(jnp.int32)
    place = jnp.reshape(rank, (1,)).astype(jnp.int32)
    width = hidden.shape[1] // 8
    bf16 = jnp.bfloat16
    f32 = jnp.float32
    smem = pl.BlockSpec(memory_space=pltpu.SMEM)
    vmem = pl.BlockSpec(memory_space=pltpu.VMEM)
    anywhere = pl.BlockSpec(memory_space=pl.ANY)
    hbm = pl.BlockSpec(memory_space=pltpu.HBM)
    dma = pltpu.SemaphoreType.DMA

    def far(value):
        return pltpu.with_memory_space_constraint(value, pltpu.HBM)

    q0 = queries[0]
    o0 = out_grads[0]
    turned, own, pair = called(
        arrange_kernel,
        (shaped(bf16, 8, 64, width), shaped(bf16, 32, width), shaped(bf16, 2, R, 256)),
        (member, far(kv_weight[0]), far(hidden), far(q0), far(o0)),
        0,
        4 << 20,
        (
            pltpu.VMEM((8, 64, width), bf16),
            pltpu.VMEM((2, R, 256), bf16),
            dma((38,)),
            dma((10,)),
        ),
        (smem, hbm, hbm, hbm, hbm),
        (anywhere, vmem, anywhere),
    )

    turned = lax.all_to_all(turned, PLANE, 0, 0, tiled=True)

    own = lax.all_gather(own, "zh", axis=0, tiled=True)
    own, turned, pair = lax.optimization_barrier((own, turned, pair))
    states = called(repeat_kernel, shaped(bf16, 4, 128, width), (own,), 0, 1 << 20)
    states = lax.all_to_all(states, "x", 0, 0, tiled=True)

    p2 = swapped(pair, QUAD, 2)
    p1 = swapped(pair, QUAD, 1)
    states = states.reshape(R, width)
    heads = turned.reshape(2, 256, width)
    partial = called(
        project_kernel,
        shaped(bf16, 8, TOKENS, 256),
        (states, heads),
        2 * R * 512 * width,
        3 << 20,
    )
    p2, partial = lax.optimization_barrier((p2, partial))
    p3 = swapped(p2, QUAD, 1)
    partial = lax.all_to_all(partial, PLANE, 0, 0, tiled=True)

    lengths = prefix_len.reshape(1, R)
    starts = doc_start.reshape(1, R)

    def prefix(kernel, *operands):
        return called(
            kernel,
            shaped(f32, 3, 4, R),
            (place, lengths, *(far(operand) for operand in (cache[0], *operands))),
            2 * 2 * 4 * R * POSITIONS * HEAD * 4,
            2 << 20,
            (pltpu.VMEM((2, POSITIONS, HEAD), bf16), pltpu.VMEM((2, 2, R, 256), bf16), dma((5,))),
            (smem, vmem) + (hbm,) * (1 + len(operands)),
            limit=20,
        )

    first = prefix(near_prefix_kernel, q0, o0, p1)
    second = prefix(far_prefix_kernel, p2, p3)
    stats, kv, pairs = called(
        new_stats_kernel,
        (shaped(f32, 3, 8, R), shaped(bf16, TOKENS, 256), shaped(bf16, 4, 2, R, 256)),
        (place, starts, first, second, partial, *(far(operand) for operand in (q0, o0, p1, p2, p3))),
        2 * 2 * 8 * R * TOKENS * HEAD * 4,
        3 << 20,
        (pltpu.VMEM((8, TOKENS, 256), bf16), dma((9,))),
        (smem, vmem, vmem, vmem, anywhere) + (hbm,) * 5,
    )
    every = lax.all_gather(stats, QUAD, axis=0)
    grads = called(
        new_grads_kernel,
        shaped(bf16, TOKENS, 256),
        (place, kv, pairs, starts, every),
        4 * 2 * 8 * R * TOKENS * HEAD * 4,
        3 << 20,
        (
            pltpu.VMEM((3, 8, R), f32),
            pltpu.VMEM((TOKENS, HEAD), f32),
            pltpu.VMEM((TOKENS, HEAD), f32),
        ),
        (smem,),
    )
    kv_grads = lax.all_gather(grads, PLANE, axis=0, tiled=True).reshape(2, R, 256)

    hidden_part = called(
        hidden_kernel,
        shaped(bf16, 4, TOKENS, width),
        (kv_grads, heads),
        2 * R * 512 * width,
        3 << 20,
        (pltpu.VMEM((4, TOKENS, width), bf16), dma((4,))),
        outs=anywhere,
    )
    hidden_part, kv_grads = lax.optimization_barrier((hidden_part, kv_grads))
    over_x = lax.all_to_all(hidden_part, "x", 0, 0, tiled=True)
    over_x = called(reduce_x_kernel, shaped(bf16, 16, 32, width // 4), (over_x,), 0, 1 << 20)

    mine, one, three = called(
        weight_kernel,
        (shaped(bf16, 2, 64, width),) + (shaped(bf16, 2, 96, width),) * 2,
        (member, kv_grads, states),
        2 * R * 512 * width,
        3 << 20,
        (pltpu.VMEM((512, width), bf16),),
        (smem,),
    )
    one = swapped(one, PLANE, 2)
    three = swapped(three, PLANE, 6)
    over_x, one, three = lax.optimization_barrier((over_x, one, three))
    over_z = lax.all_to_all(over_x, ("zh", "zl"), 0, 0, tiled=True)
    hidden_grads = jnp.sum(over_z.astype(f32), axis=0)

    upper = swapped(one[:, 64:], PLANE, 6)
    lower = swapped(three[:, 64:], PLANE, 2)
    kept, passed = called(
        cores_kernel,
        (shaped(bf16, 4, 64, width),) * 2,
        (member, mine, one, three, upper, lower),
        0,
        1 << 20,
        (),
        (smem,),
    )
    taken = swapped(passed, PLANE, 1)
    weight_grads = called(
        place_kernel,
        shaped(f32, 1, 64, 8 * width),
        (member, kept, taken),
        0,
        3 << 20,
        (),
        (smem,),
    )
    return hidden_grads, weight_grads


def solution(mesh):
    axes = ("zh", "x", "zl", "yh", "yl", "core")
    split = Mesh(mesh.devices.reshape(4, 4, 4, 2, 2, 2), axes)
    pipe = ("zh", "x")
    tensor = ("zl", "yh", "yl", "core")
    return jax.shard_map(
        shards,
        mesh=split,
        in_specs=(
            P(pipe, None),
            P(pipe, tensor, None),
            P(pipe, None, tensor),
            P(pipe, None, tensor),
            P(pipe, None, tensor, None),
            P(),
            P(),
        ),
        out_specs=(P(pipe, tensor), P(pipe, tensor, None)),
        check_vma=False,
    )
```

time: 168 us -> 146 us (0.87)
  waiting for transfers between devices: 47.1 us -> 26.7 us
  Pallas kernels: 9.67 us -> 24.9 us
  local copies, waits for them, and re-layouts: 14.8 us -> 0.03 us
  matrix products: 8.53 us -> 0 us
  starting transfers between devices: 41.5 us -> 48.7 us
    pallas_call x3 -> x12, Pallas kernels: 9.67 us -> 24.9 us  [called(): pl.pallas_call(kernel, grid=grid, out_shape=out_shape, in_specs=list(plac...]
    ppermute x3 -> x8, starting transfers between devices: 7.05 us -> 20 us  [swapped(): return lax.ppermute(value, axes, pairs)]
    all_to_all x2 -> x1, waiting for transfers between devices: 20.2 us -> 7.81 us  [shards(): states = lax.all_to_all(states, 'x', 0, 0, tiled=True)]
    all_to_all x1, waiting for transfers between devices: 12.1 us -> 2.35 us  [shards(): over_z = lax.all_to_all(over_x, ('zh', 'zl'), 0, 0, tiled=True)]
    dot_general x5 -> x0, matrix products: 8.53 us -> none  [the longest x2 3.72 us: shards(): lax.dot_general(states, heads[j], NT, preferred_element_type=jnp.float32)]
    ppermute x3 -> x8, waiting for transfers between devices: 0.01 us -> 8.07 us  [swapped(): return lax.ppermute(value, axes, pairs)]
    convert_element_type x3 -> x0, local copies, waits for them, and re-layouts: 6.25 us -> none  [shards(): return (hidden_grads, weight_grads.astype(jnp.float32))]
    all_to_all x2 -> x1, starting transfers between devices: 9.84 us -> 4.29 us  [shards(): states = lax.all_to_all(states, 'x', 0, 0, tiled=True)]
  transfers between devices with their start and end apart: 9 -> 13, of which waited for: 5 -> 7; matrix products, arithmetic and copies ran while one was open for 12% -> 0% of each run, Pallas kernels for 4% -> 11%
where the time goes in v2:
time: 146 us; the launch traced here: 144 us
  starting transfers between devices  48.7 us (33%)
  blocking collectives  41.9 us (29%)
  waiting for transfers between devices  26.7 us (18%)
  Pallas kernels  24.9 us (17%)
    pallas_call x12, Pallas kernels, called(): pl.pallas_call(kernel, grid=grid, out_shape=out_shape, in_specs=list(plac...  24.9 us
    all_gather x1, blocking collectives, shards(): own = lax.all_gather(own, 'zh', axis=0, tiled=True)  23 us
    ppermute x8, starting transfers between devices, swapped(): return lax.ppermute(value, axes, pairs)  20 us
    all_gather x1, blocking collectives, shards(): lax.all_gather(grads, PLANE, axis=0, tiled=True).reshape(2, R, 256)  13.1 us
    all_to_all x1, starting transfers between devices, shards(): turned = lax.all_to_all(turned, PLANE, 0, 0, tiled=True)  9.1 us
    all_to_all x1, waiting for transfers between devices, shards(): over_x = lax.all_to_all(hidden_part, 'x', 0, 0, tiled=True)  8.45 us
    ppermute x8, waiting for transfers between devices, swapped(): return lax.ppermute(value, axes, pairs)  8.07 us
    all_to_all x1, waiting for transfers between devices, shards(): states = lax.all_to_all(states, 'x', 0, 0, tiled=True)  7.81 us
  transfers between devices with their start and end apart: 13, of which 7 were waited for; matrix products, arithmetic and copies ran while one was open for 0% of the time, Pallas kernels for 11%

profile of v2, /device:TPU:24, one launch (start us, length us, event | category | flops | bytes accessed | tf_op | source)
XLA Modules:
  0.0 143.7 jit_solution(137879013878684871)
XLA Ops:
  0.6 2.3 %shard_map.86 = (bf16[8,64,1024]{2,1,0:T(8,128)(2,1)}, bf16[32,1024]{1,0:T(8,128)(2,1)S(1)}, bf16[2,512,256]{2,1,0:T(8,128)(2,1)S(1)}) custom-call(s32[1]{0:T(128)} %bitcast.6.place, bf16[64,8192]{1,0:T(8,128)(2,1)} %bitcast.23, bf16[32,8192]{1,0:T(8,128)(2,1)} %hidden.1, bf16[512,256]{1,0:T(8,128)(2,1)} %bitcast.24, bf16[512,256]{1,0:T(8,128)(2,1)} %bitcast.27), custom_call_target="tpu_custom_call" | custom-call | bytes 4194304 | tf_op jit(solution)/shard_map/pallas_call | solution.py:312
  2.9 9.1 %all-to-all-start = ((bf16[8,64,1024]{2,1,0:T(8,128)(2,1)}), bf16[8,64,1024]{2,1,0:T(8,128)(2,1)S(1)}, u32[]{:S(2)}, u32[]{:S(2)}) async-start(bf16[8,64,1024]{2,1,0:T(8,128)(2,1)} %get-tuple-element.24), calls=%async_computation | async-start | bytes 2097152 | tf_op jit(solution)/shard_map/all_to_all | solution.py:365
  12.0 23.0 %all_gather.12.block = bf16[128,1024]{1,0:T(8,128)(2,1)S(1)} all-gather(bf16[32,1024]{1,0:T(8,128)(2,1)S(1)} %get-tuple-element.23), channel_id=1, replica_groups=mesh['zh'=4,'x'=4,'zl'=4,'yh'=2,'yl'=2,'core'=2] {'zh'}, dimensions={0}, use_global_device_ids=true | all-gather | bytes 327680 | tf_op jit(solution)/shard_map/all_gather | solution.py:367
  36.1 4.3 %all-to-all-start.1 = ((bf16[4,128,1024]{2,1,0:T(8,128)(2,1)}), bf16[4,128,1024]{2,1,0:T(8,128)(2,1)S(1)}, u32[]{:S(2)}, u32[]{:S(2)}) async-start(bf16[4,128,1024]{2,1,0:T(8,128)(2,1)} %shard_map.88), calls=%async_computation.1 | async-start | bytes 2097152 | tf_op jit(solution)/shard_map/all_to_all | solution.py:370
  40.4 2.9 %collective-permute-start.1 = (bf16[2,512,256]{2,1,0:T(8,128)(2,1)S(1)}, bf16[2,512,256]{2,1,0:T(8,128)(2,1)}, u32[]{:S(2)}, u32[]{:S(2)}) collective-permute-start(bf16[2,512,256]{2,1,0:T(8,128)(2,1)S(1)} %get-tuple-element.26), channel_id=1, source_target_pairs={{0,2},{1,3},{2,0},{3,1},{4,6},{5,7},{6,4},{7,5},{8,10},{9,11},{10,... | collective-permute-start | bytes 1572872 | tf_op jit(solution)/shard_map/ppermute | solution.py:27
  43.3 1.9 %collective-permute-start = (bf16[2,512,256]{2,1,0:T(8,128)(2,1)S(1)}, bf16[2,512,256]{2,1,0:T(8,128)(2,1)}, u32[]{:S(2)}, u32[]{:S(2)}) collective-permute-start(bf16[2,512,256]{2,1,0:T(8,128)(2,1)S(1)} %get-tuple-element.26), channel_id=1, source_target_pairs={{0,1},{1,0},{2,3},{3,2},{4,5},{5,4},{6,7},{7,6},{8,9},{9,8},{10,11... | collective-permute-start | bytes 1572872 | tf_op jit(solution)/shard_map/ppermute | solution.py:27
  45.2 7.8 %all-to-all-done.1 = bf16[4,128,1024]{2,1,0:T(8,128)(2,1)S(1)} async-done(((bf16[4,128,1024]{2,1,0:T(8,128)(2,1)}), bf16[4,128,1024]{2,1,0:T(8,128)(2,1)S(1)}, u32[]{:S(2)}, u32[]{:S(2)}) %all-to-all-start.1) | async-done | bytes 1048608 | tf_op jit(solution)/shard_map/all_to_all | solution.py:370
  54.6 1.9 %collective-permute-start.2 = (bf16[2,512,256]{2,1,0:T(8,128)(2,1)}, bf16[2,512,256]{2,1,0:T(8,128)(2,1)}, u32[]{:S(2)}, u32[]{:S(2)}) collective-permute-start(bf16[2,512,256]{2,1,0:T(8,128)(2,1)} %collective-permute-done.1.p2), channel_id=1, source_target_pairs={{0,1},{1,0},{2,3},{3,2},{4,5},{5,4},{6,7},{7,6},{8,9},{9,8},{10,11... | collective-permute-start | bytes 1572872 | tf_op jit(solution)/shard_map/ppermute | solution.py:27
  56.5 4.9 %all-to-all-start.2 = ((bf16[8,128,256]{2,1,0:T(8,128)(2,1)}), bf16[8,128,256]{2,1,0:T(8,128)(2,1)S(1)}, u32[]{:S(2)}, u32[]{:S(2)}) async-start(bf16[8,128,256]{2,1,0:T(8,128)(2,1)} %shard_map.89), calls=%async_computation.2 | async-start | bytes 1048576 | tf_op jit(solution)/shard_map/all_to_all | solution.py:385
  61.4 4.9 %shard_map.87.first = f32[3,4,512]{2,1,0:T(4,128)S(1)} custom-call(s32[1]{0:T(128)} %bitcast.place, s32[1,512]{1,0:T(1,128)S(1)} %bitcast.19, bf16[2,1024,128]{2,1,0:T(8,128)(2,1)} %bitcast.30, bf16[512,256]{1,0:T(8,128)(2,1)} %bitcast.25, bf16[512,256]{1,0:T(8,128)(2,1)} %bitcast.28, bf16[2,512,256]{2,1,0:T(8,128)(2,1)} %collective-permute-done.p1), custom_call_target="tpu_custom_call" | custom-call | flops 4294967296 | bytes 2097152 | tf_op jit(solution)/shard_map/pallas_call | solution.py:312
  66.3 4.9 %shard_map.90.second = f32[3,4,512]{2,1,0:T(4,128)S(1)} custom-call(s32[1]{0:T(128)} %bitcast.place, s32[1,512]{1,0:T(1,128)S(1)} %bitcast.20, bf16[2,1024,128]{2,1,0:T(8,128)(2,1)} %bitcast.31, bf16[2,512,256]{2,1,0:T(8,128)(2,1)} %collective-permute-done.1.p2, bf16[2,512,256]{2,1,0:T(8,128)(2,1)} %collective-permute-done.2.p3), custom_call_target="tpu_custom_call" | custom-call | flops 4294967296 | bytes 2097152 | tf_op jit(solution)/shard_map/pallas_call | solution.py:312
  71.2 2.7 %shard_map.91 = (f32[3,8,512]{2,1,0:T(8,128)S(1)}, bf16[128,256]{1,0:T(8,128)(2,1)S(1)}, bf16[4,2,512,256]{3,2,1,0:T(8,128)(2,1)S(1)}) custom-call(s32[1]{0:T(128)} %bitcast.place, s32[1,512]{1,0:T(1,128)S(1)} %bitcast.21, f32[3,4,512]{2,1,0:T(4,128)S(1)} %shard_map.87.first, f32[3,4,512]{2,1,0:T(4,128)S(1)} %shard_map.90.second, ...), custom_call_target="tpu_custom_call" | custom-call | flops 1073741824 | bytes 3145728 | tf_op jit(solution)/shard_map/pallas_call | solution.py:312
  73.9 5.8 %all-gather = f32[12,8,512]{2,1,0:T(8,128)S(1)} all-gather(f32[3,8,512]{2,1,0:T(8,128)S(1)} %get-tuple-element.33), channel_id=2, replica_groups=mesh['zh'=4,'x'=4,'zl'=4,'yh'=2,'yl'=2,'core'=2] {'yl','core'}, dimensions={0}, use_global_device_ids=true | all-gather | bytes 245760 | tf_op jit(solution)/shard_map/all_gather | solution.py:413
  79.7 2.3 %shard_map.92 = bf16[128,256]{1,0:T(8,128)(2,1)S(1)} custom-call(s32[1]{0:T(128)} %bitcast.place, bf16[128,256]{1,0:T(8,128)(2,1)S(1)} %get-tuple-element.31.kv, bf16[4,2,512,256]{3,2,1,0:T(8,128)(2,1)S(1)} %get-tuple-element.32.pairs, s32[1,512]{1,0:T(1,128)S(1)} %bitcast.22, f32[4,3,8,512]{3,2,1,0:T(8,128)S(1)} %bitcast.18), custom_call_target="tpu_custom_call" | custom-call | flops 2147483648 | bytes 3145728 | tf_op jit(solution)/shard_map/pallas_call | solution.py:312
  82.0 13.1 %all_gather.15 = bf16[1024,256]{1,0:T(8,128)(2,1)S(1)} all-gather(bf16[128,256]{1,0:T(8,128)(2,1)S(1)} %shard_map.92), channel_id=1, replica_groups=mesh['zh'=4,'x'=4,'zl'=4,'yh'=2,'yl'=2,'core'=2] {'yh','yl','core'}, dimensions={0}, use_global_device_ids=true | all-gather | bytes 589824 | tf_op jit(solution)/shard_map/all_gather | solution.py:427
  96.5 3.5 %all-to-all-start.3 = ((bf16[4,128,1024]{2,1,0:T(8,128)(2,1)}), bf16[4,128,1024]{2,1,0:T(8,128)(2,1)S(1)}, u32[]{:S(2)}, u32[]{:S(2)}) async-start(bf16[4,128,1024]{2,1,0:T(8,128)(2,1)} %shard_map.93), calls=%async_computation.3 | async-start | bytes 2097152 | tf_op jit(solution)/shard_map/all_to_all | solution.py:439
  103.5 3.9 %collective-permute-start.4 = (bf16[2,96,1024]{2,1,0:T(8,128)(2,1)S(1)}, bf16[2,96,1024]{2,1,0:T(8,128)(2,1)S(1)}, u32[]{:S(2)}, u32[]{:S(2)}) collective-permute-start(bf16[2,96,1024]{2,1,0:T(8,128)(2,1)S(1)} %get-tuple-element.37), channel_id=1, source_target_pairs={{0,6},{1,7},{2,4},{3,5},{4,2},{5,3},{6,0},{7,1},{8,14},{9,15},{10,... | collective-permute-start | bytes 1179656 | tf_op jit(solution)/shard_map/ppermute | solution.py:27
  107.5 8.5 %all-to-all-done.3.blocks = bf16[4,128,1024]{2,1,0:T(8,128)(2,1)S(1)} async-done(((bf16[4,128,1024]{2,1,0:T(8,128)(2,1)}), bf16[4,128,1024]{2,1,0:T(8,128)(2,1)S(1)}, u32[]{:S(2)}, u32[]{:S(2)}) %all-to-all-start.3) | async-done | bytes 1048608 | tf_op jit(solution)/shard_map/all_to_all | solution.py:439
  118.0 6.8 %all-to-all-start.4 = ((bf16[16,32,256]{2,1,0:T(8,128)(2,1)}), bf16[16,32,256]{2,1,0:T(8,128)(2,1)S(1)}, u32[]{:S(2)}, u32[]{:S(2)}) async-start(bf16[16,32,256]{2,1,0:T(8,128)(2,1)} %shard_map.94), calls=%async_computation.4 | async-start | bytes 524288 | tf_op jit(solution)/shard_map/all_to_all | solution.py:454
  124.8 2.4 %collective-permute-start.6 = (bf16[2,32,1024]{2,1,0:T(8,128)(2,1)S(1)}, bf16[2,32,1024]{2,1,0:T(8,128)(2,1)S(1)}, u32[]{:S(2)}, u32[]{:S(2)}) collective-permute-start(bf16[2,32,1024]{2,1,0:T(8,128)(2,1)S(1)} %slice.7), channel_id=1, source_target_pairs={{0,2},{1,3},{2,0},{3,1},{4,6},{5,7},{6,4},{7,5},{8,10},{9,11},{10,... | collective-permute-start | bytes 393224 | tf_op jit(solution)/shard_map/ppermute | solution.py:27
  127.3 3.1 %collective-permute-start.5 = (bf16[2,32,1024]{2,1,0:T(8,128)(2,1)S(1)}, bf16[2,32,1024]{2,1,0:T(8,128)(2,1)S(1)}, u32[]{:S(2)}, u32[]{:S(2)}) collective-permute-start(bf16[2,32,1024]{2,1,0:T(8,128)(2,1)S(1)} %slice.6), channel_id=1, source_target_pairs={{0,6},{1,7},{2,4},{3,5},{4,2},{5,3},{6,0},{7,1},{8,14},{9,15},{10,... | collective-permute-start | bytes 393224 | tf_op jit(solution)/shard_map/ppermute | solution.py:27
  131.7 3.6 %collective-permute-done.5.upper = bf16[2,32,1024]{2,1,0:T(8,128)(2,1)S(1)} collective-permute-done((bf16[2,32,1024]{2,1,0:T(8,128)(2,1)S(1)}, bf16[2,32,1024]{2,1,0:T(8,128)(2,1)S(1)}, u32[]{:S(2)}, u32[]{:S(2)}) %collective-permute-start.5) | collective-permute-done | bytes 131104 | tf_op jit(solution)/shard_map/ppermute | solution.py:27
  135.4 1.9 %collective-permute-start.7 = (bf16[4,64,1024]{2,1,0:T(8,128)(2,1)S(1)}, bf16[4,64,1024]{2,1,0:T(8,128)(2,1)S(1)}, u32[]{:S(2)}, u32[]{:S(2)}) collective-permute-start(bf16[4,64,1024]{2,1,0:T(8,128)(2,1)S(1)} %get-tuple-element.43), channel_id=1, source_target_pairs={{0,1},{1,0},{2,3},{3,2},{4,5},{5,4},{6,7},{7,6},{8,9},{9,8},{10,11... | collective-permute-start | bytes 1572872 | tf_op jit(solution)/shard_map/ppermute | solution.py:27
  140.7 2.3 %all-to-all-done.4 = bf16[16,32,256]{2,1,0:T(8,128)(2,1)S(1)} async-done(((bf16[16,32,256]{2,1,0:T(8,128)(2,1)}), bf16[16,32,256]{2,1,0:T(8,128)(2,1)S(1)}, u32[]{:S(2)}, u32[]{:S(2)}) %all-to-all-start.4) | async-done | bytes 262176 | tf_op jit(solution)/shard_map/all_to_all | solution.py:454
  (24 shorter events, 15.0 us)
Async XLA Ops:
  2.9 32.2 %all-to-all-start = ((bf16[8,64,1024]{2,1,0:T(8,128)(2,1)}), bf16[8,64,1024]{2,1,0:T(8,128)(2,1)S(1)}, u32[]{:S(2)}, u32[]{:S(2)}) async-start(bf16[8,64,1024]{2,1,0:T(8,128)(2,1)} %get-tuple-element.24), calls=%async_computation | async-start | bytes 2097152 | tf_op jit(solution)/shard_map/all_to_all | solution.py:365
  36.1 16.9 %all-to-all-start.1 = ((bf16[4,128,1024]{2,1,0:T(8,128)(2,1)}), bf16[4,128,1024]{2,1,0:T(8,128)(2,1)S(1)}, u32[]{:S(2)}, u32[]{:S(2)}) async-start(bf16[4,128,1024]{2,1,0:T(8,128)(2,1)} %shard_map.88), calls=%async_computation.1 | async-start | bytes 2097152 | tf_op jit(solution)/shard_map/all_to_all | solution.py:370
  40.4 21.0 %copy-start = (s32[512]{0:T(512)S(1)}, s32[512]{0:T(512)}, u32[]{:S(2)}) copy-start(s32[512]{0:T(512)} %param.12) | copy-start | bytes 6148
  40.4 14.2 %collective-permute-start.1 = (bf16[2,512,256]{2,1,0:T(8,128)(2,1)S(1)}, bf16[2,512,256]{2,1,0:T(8,128)(2,1)}, u32[]{:S(2)}, u32[]{:S(2)}) collective-permute-start(bf16[2,512,256]{2,1,0:T(8,128)(2,1)S(1)} %get-tuple-element.26), channel_id=1, source_target_pairs={{0,2},{1,3},{2,0},{3,1},{4,6},{5,7},{6,4},{7,5},{8,10},{9,11},{10,... | collective-permute-start | bytes 1572872 | tf_op jit(solution)/shard_map/ppermute | solution.py:27
  43.3 18.1 %collective-permute-start = (bf16[2,512,256]{2,1,0:T(8,128)(2,1)S(1)}, bf16[2,512,256]{2,1,0:T(8,128)(2,1)}, u32[]{:S(2)}, u32[]{:S(2)}) collective-permute-start(bf16[2,512,256]{2,1,0:T(8,128)(2,1)S(1)} %get-tuple-element.26), channel_id=1, source_target_pairs={{0,1},{1,0},{2,3},{3,2},{4,5},{5,4},{6,7},{7,6},{8,9},{9,8},{10,11... | collective-permute-start | bytes 1572872 | tf_op jit(solution)/shard_map/ppermute | solution.py:27
  54.6 11.7 %collective-permute-start.2 = (bf16[2,512,256]{2,1,0:T(8,128)(2,1)}, bf16[2,512,256]{2,1,0:T(8,128)(2,1)}, u32[]{:S(2)}, u32[]{:S(2)}) collective-permute-start(bf16[2,512,256]{2,1,0:T(8,128)(2,1)} %collective-permute-done.1.p2), channel_id=1, source_target_pairs={{0,1},{1,0},{2,3},{3,2},{4,5},{5,4},{6,7},{7,6},{8,9},{9,8},{10,11... | collective-permute-start | bytes 1572872 | tf_op jit(solution)/shard_map/ppermute | solution.py:27
  56.5 14.7 %all-to-all-start.2 = ((bf16[8,128,256]{2,1,0:T(8,128)(2,1)}), bf16[8,128,256]{2,1,0:T(8,128)(2,1)S(1)}, u32[]{:S(2)}, u32[]{:S(2)}) async-start(bf16[8,128,256]{2,1,0:T(8,128)(2,1)} %shard_map.89), calls=%async_computation.2 | async-start | bytes 1048576 | tf_op jit(solution)/shard_map/all_to_all | solution.py:385
  66.3 4.9 %copy-start.1 = (s32[512]{0:T(512)S(1)}, s32[512]{0:T(512)}, u32[]{:S(2)}) copy-start(s32[512]{0:T(512)} %param.13) | copy-start | bytes 6148
  96.5 19.4 %all-to-all-start.3 = ((bf16[4,128,1024]{2,1,0:T(8,128)(2,1)}), bf16[4,128,1024]{2,1,0:T(8,128)(2,1)S(1)}, u32[]{:S(2)}, u32[]{:S(2)}) async-start(bf16[4,128,1024]{2,1,0:T(8,128)(2,1)} %shard_map.93), calls=%async_computation.3 | async-start | bytes 2097152 | tf_op jit(solution)/shard_map/all_to_all | solution.py:439
  101.6 15.1 %collective-permute-start.3 = (bf16[2,96,1024]{2,1,0:T(8,128)(2,1)}, bf16[2,96,1024]{2,1,0:T(8,128)(2,1)S(1)}, u32[]{:S(2)}, u32[]{:S(2)}) collective-permute-start(bf16[2,96,1024]{2,1,0:T(8,128)(2,1)} %get-tuple-element.36), channel_id=1, source_target_pairs={{0,2},{1,3},{2,0},{3,1},{4,6},{5,7},{6,4},{7,5},{8,10},{9,11},{10,... | collective-permute-start | bytes 1179656 | tf_op jit(solution)/shard_map/ppermute | solution.py:27
  103.5 14.5 %collective-permute-start.4 = (bf16[2,96,1024]{2,1,0:T(8,128)(2,1)S(1)}, bf16[2,96,1024]{2,1,0:T(8,128)(2,1)S(1)}, u32[]{:S(2)}, u32[]{:S(2)}) collective-permute-start(bf16[2,96,1024]{2,1,0:T(8,128)(2,1)S(1)} %get-tuple-element.37), channel_id=1, source_target_pairs={{0,6},{1,7},{2,4},{3,5},{4,2},{5,3},{6,0},{7,1},{8,14},{9,15},{10,... | collective-permute-start | bytes 1179656 | tf_op jit(solution)/shard_map/ppermute | solution.py:27
  118.0 25.0 %all-to-all-start.4 = ((bf16[16,32,256]{2,1,0:T(8,128)(2,1)}), bf16[16,32,256]{2,1,0:T(8,128)(2,1)S(1)}, u32[]{:S(2)}, u32[]{:S(2)}) async-start(bf16[16,32,256]{2,1,0:T(8,128)(2,1)} %shard_map.94), calls=%async_computation.4 | async-start | bytes 524288 | tf_op jit(solution)/shard_map/all_to_all | solution.py:454
  124.8 6.9 %collective-permute-start.6 = (bf16[2,32,1024]{2,1,0:T(8,128)(2,1)S(1)}, bf16[2,32,1024]{2,1,0:T(8,128)(2,1)S(1)}, u32[]{:S(2)}, u32[]{:S(2)}) collective-permute-start(bf16[2,32,1024]{2,1,0:T(8,128)(2,1)S(1)} %slice.7), channel_id=1, source_target_pairs={{0,2},{1,3},{2,0},{3,1},{4,6},{5,7},{6,4},{7,5},{8,10},{9,11},{10,... | collective-permute-start | bytes 393224 | tf_op jit(solution)/shard_map/ppermute | solution.py:27
  127.3 8.1 %collective-permute-start.5 = (bf16[2,32,1024]{2,1,0:T(8,128)(2,1)S(1)}, bf16[2,32,1024]{2,1,0:T(8,128)(2,1)S(1)}, u32[]{:S(2)}, u32[]{:S(2)}) collective-permute-start(bf16[2,32,1024]{2,1,0:T(8,128)(2,1)S(1)} %slice.6), channel_id=1, source_target_pairs={{0,6},{1,7},{2,4},{3,5},{4,2},{5,3},{6,0},{7,1},{8,14},{9,15},{10,... | collective-permute-start | bytes 393224 | tf_op jit(solution)/shard_map/ppermute | solution.py:27
  135.4 3.8 %collective-permute-start.7 = (bf16[4,64,1024]{2,1,0:T(8,128)(2,1)S(1)}, bf16[4,64,1024]{2,1,0:T(8,128)(2,1)S(1)}, u32[]{:S(2)}, u32[]{:S(2)}) collective-permute-start(bf16[4,64,1024]{2,1,0:T(8,128)(2,1)S(1)} %get-tuple-element.43), channel_id=1, source_target_pairs={{0,1},{1,0},{2,3},{3,2},{4,5},{5,4},{6,7},{7,6},{8,9},{9,8},{10,11... | collective-permute-start | bytes 1572872 | tf_op jit(solution)/shard_map/ppermute | solution.py:27

commit v3 on v2

--- a/solution.py
+++ b/solution.py
@@ -56,52 +56,31 @@
     return copies
 
 
-def fetch_pairs(sources, pairs, sems):
-    moves = []
-    for index, source in enumerate(sources):
-        if isinstance(source, tuple):
-            moves += [(part, pairs.at[index, kind]) for kind, part in enumerate(source)]
-        else:
-            moves += [(source.at[kind], pairs.at[index, kind]) for kind in range(2)]
-    return fetch(moves, sems)
-
-
-def prefix_stats(rank, lengths, sources, cache, stats, blocks, pairs, sems):
+def prefix_kernel(place, prefix_len, cache, beside, q0, o0, p2, stats):
+    rank = place[0]
+    lengths = prefix_len[...]
     chunk = 512
-    base = pltpu.make_async_copy(cache, blocks, sems.at[4])
-    base.start()
-    copies = fetch_pairs(sources, pairs, sems)
-    base.wait()
-    for other in range(2):
-        copies[2 * other].wait()
-        copies[2 * other + 1].wait()
+    for other, (q, o) in enumerate(((q0, o0), (p2.at[0], p2.at[1]))):
         for head in range(2):
             columns = pl.ds(head * HEAD, HEAD)
-            queries = pairs[other, 0, :, columns]
-            grads = pairs[other, 1, :, columns]
+            queries = q[:, columns]
+            grads = o[:, columns]
             parts = None
-            for start in range(0, POSITIONS, chunk):
-                rows = pl.ds(start, chunk)
-                scores = lax.dot_general(
-                    blocks[0, rows, :], queries, NT, preferred_element_type=jnp.float32
-                )
-                dots = lax.dot_general(
-                    blocks[1, rows, :], grads, NT, preferred_element_type=jnp.float32
-                )
-                ids = lax.broadcasted_iota(jnp.int32, (chunk, R), 0)
-                limit = lengths - (rank * POSITIONS + start)
-                piece = softmax_parts(jnp.where(ids < limit, scores, LOW), dots)
-                parts = piece if parts is None else merged(parts, piece)
+            for core, blocks in enumerate((cache, beside)):
+                for start in range(0, POSITIONS, chunk):
+                    rows = pl.ds(start, chunk)
+                    scores = lax.dot_general(
+                        blocks[0, rows, :], queries, NT, preferred_element_type=jnp.float32
+                    )
+                    dots = lax.dot_general(
+                        blocks[1, rows, :], grads, NT, preferred_element_type=jnp.float32
+                    )
+                    ids = lax.broadcasted_iota(jnp.int32, (chunk, R), 0)
+                    limit = lengths - ((rank ^ core) * POSITIONS + start)
+                    piece = softmax_parts(jnp.where(ids < limit, scores, LOW), dots)
+                    parts = piece if parts is None else merged(parts, piece)
             for kind in range(3):
                 stats[kind, pl.ds(other * 2 + head, 1), :] = parts[kind]
-
-
-def near_prefix_kernel(place, prefix_len, cache, q0, o0, p1, stats, *scratch):
-    prefix_stats(place[0], prefix_len[...], ((q0, o0), p1), cache, stats, *scratch)
-
-
-def far_prefix_kernel(place, prefix_len, cache, p2, p3, stats, *scratch):
-    prefix_stats(place[0], prefix_len[...], (p2, p3), cache, stats, *scratch)
 
 
 def new_scores(rank, doc_start, keys, values, queries, grads):
@@ -115,22 +94,26 @@
 
 
 def new_stats_kernel(
-    place, doc_start, first, second, partial, q0, o0, p1, p2, p3, stats, kv, pairs, blocks, sems
+    place, doc_start, before, partial, q0, o0, p1, p2, p3, stats, kv, pairs, sems
 ):
     rank = place[0]
-    base = pltpu.make_async_copy(partial, blocks, sems.at[8])
-    base.start()
-    copies = fetch_pairs(((q0, o0), p1, p2, p3), pairs, sems)
-    base.wait()
-    total_kv = blocks[0].astype(jnp.float32)
+    sources = ((q0, o0), (p1.at[0], p1.at[1]), (p2.at[0], p2.at[1]), (p3.at[0], p3.at[1]))
+    copies = fetch(
+        [
+            (part, pairs.at[other, kind])
+            for other, source in enumerate(sources)
+            for kind, part in enumerate(source)
+        ],
+        sems,
+    )
+    total_kv = partial[0].astype(jnp.float32)
     for source in range(1, 8):
-        total_kv = total_kv + blocks[source].astype(jnp.float32)
+        total_kv = total_kv + partial[source].astype(jnp.float32)
     kv[...] = total_kv.astype(jnp.bfloat16)
     starts = doc_start[...]
     for other in range(4):
         copies[2 * other].wait()
         copies[2 * other + 1].wait()
-        before = first if other < 2 else second
         for head in range(2):
             columns = pl.ds(head * HEAD, HEAD)
             scores, dots = new_scores(
@@ -141,10 +124,10 @@
                 pairs[other, 0, :, columns],
                 pairs[other, 1, :, columns],
             )
-            held = pl.ds(other % 2 * 2 + head, 1)
-            parts = merged(
-                softmax_parts(scores, dots), tuple(before[kind, held, :] for kind in range(3))
-            )
+            parts = softmax_parts(scores, dots)
+            if other % 2 == 0:
+                held = pl.ds(other + head, 1)
+                parts = merged(parts, tuple(before[kind, held, :] for kind in range(3)))
             slot = pl.ds((rank ^ other) * 2 + head, 1)
             for kind in range(3):
                 stats[kind, slot, :] = parts[kind]
@@ -306,7 +289,7 @@
 
 
 def called(
-    kernel, out_shape, operands, flops, moved, scratch=(), places=(), outs=None, limit=12, grid=()
+    kernel, out_shape, operands, flops, moved, scratch=(), places=(), outs=None, limit=16, grid=()
 ):
     vmem = pl.BlockSpec(memory_space=pltpu.VMEM)
     return pl.pallas_call(
@@ -361,16 +344,17 @@
         (smem, hbm, hbm, hbm, hbm),
         (anywhere, vmem, anywhere),
     )
-
     turned = lax.all_to_all(turned, PLANE, 0, 0, tiled=True)
 
     own = lax.all_gather(own, "zh", axis=0, tiled=True)
-    own, turned, pair = lax.optimization_barrier((own, turned, pair))
+    own, turned, pair, cached = lax.optimization_barrier((own, turned, pair, cache[0]))
     states = called(repeat_kernel, shaped(bf16, 4, 128, width), (own,), 0, 1 << 20)
     states = lax.all_to_all(states, "x", 0, 0, tiled=True)
 
     p2 = swapped(pair, QUAD, 2)
+    beside = swapped(cached, QUAD, 1)
     p1 = swapped(pair, QUAD, 1)
+
     states = states.reshape(R, width)
     heads = turned.reshape(2, 256, width)
     partial = called(
@@ -382,33 +366,28 @@
     )
     p2, partial = lax.optimization_barrier((p2, partial))
     p3 = swapped(p2, QUAD, 1)
+    sources = (q0, o0, p1, p2, p3)
+    before = called(
+        prefix_kernel,
+        shaped(f32, 3, 4, R),
+        (place, prefix_len.reshape(1, R), cache[0], beside, q0, o0, p2),
+        2 * 2 * 8 * R * POSITIONS * HEAD * 4,
+        3 << 20,
+        (),
+        (smem,),
+        limit=16,
+    )
     partial = lax.all_to_all(partial, PLANE, 0, 0, tiled=True)
 
-    lengths = prefix_len.reshape(1, R)
     starts = doc_start.reshape(1, R)
-
-    def prefix(kernel, *operands):
-        return called(
-            kernel,
-            shaped(f32, 3, 4, R),
-            (place, lengths, *(far(operand) for operand in (cache[0], *operands))),
-            2 * 2 * 4 * R * POSITIONS * HEAD * 4,
-            2 << 20,
-            (pltpu.VMEM((2, POSITIONS, HEAD), bf16), pltpu.VMEM((2, 2, R, 256), bf16), dma((5,))),
-            (smem, vmem) + (hbm,) * (1 + len(operands)),
-            limit=20,
-        )
-
-    first = prefix(near_prefix_kernel, q0, o0, p1)
-    second = prefix(far_prefix_kernel, p2, p3)
     stats, kv, pairs = called(
         new_stats_kernel,
         (shaped(f32, 3, 8, R), shaped(bf16, TOKENS, 256), shaped(bf16, 4, 2, R, 256)),
-        (place, starts, first, second, partial, *(far(operand) for operand in (q0, o0, p1, p2, p3))),
+        (place, starts, before, partial, *(far(source) for source in sources)),
         2 * 2 * 8 * R * TOKENS * HEAD * 4,
         3 << 20,
-        (pltpu.VMEM((8, TOKENS, 256), bf16), dma((9,))),
-        (smem, vmem, vmem, vmem, anywhere) + (hbm,) * 5,
+        (dma((8,)),),
+        (smem, vmem, vmem, vmem) + (hbm,) * 5,
     )
     every = lax.all_gather(stats, QUAD, axis=0)
     grads = called(
@@ -450,7 +429,7 @@
     )
     one = swapped(one, PLANE, 2)
     three = swapped(three, PLANE, 6)
-    over_x, one, three = lax.optimization_barrier((over_x, one, three))
+    over_x, one = lax.optimization_barrier((over_x, one))
     over_z = lax.all_to_all(over_x, ("zh", "zl"), 0, 0, tiled=True)
     hidden_grads = jnp.sum(over_z.astype(f32), axis=0)
 

time: 146 us -> 142 us (0.973)
  waiting for transfers between devices: 26.7 us -> 22.6 us
  starting transfers between devices: 48.7 us -> 51.5 us
  Pallas kernels: 24.9 us -> 23.4 us
    ppermute x8 -> x9, starting transfers between devices: 20 us -> 22.9 us  [swapped(): return lax.ppermute(value, axes, pairs)]
    all_to_all x1, waiting for transfers between devices: 7.81 us -> 5.38 us  [shards(): states = lax.all_to_all(states, 'x', 0, 0, tiled=True)]
    ppermute x8 -> x9, waiting for transfers between devices: 8.07 us -> 6.03 us  [swapped(): return lax.ppermute(value, axes, pairs)]
    pallas_call x12 -> x11, Pallas kernels: 24.9 us -> 23.4 us  [called(): pl.pallas_call(kernel, grid=grid, out_shape=out_shape, in_specs=list(plac...]
  transfers between devices with their start and end apart: 13 -> 14, of which waited for: 7 -> 6; matrix products, arithmetic and copies ran while one was open for 0% -> 0% of each run, Pallas kernels for 11% -> 9%
where the time goes in v3:
time: 142 us; the launch traced here: 141 us
  starting transfers between devices  51.5 us (36%)
  blocking collectives  41.9 us (30%)
  Pallas kernels  23.4 us (16%)
  waiting for transfers between devices  22.6 us (16%)
    pallas_call x11, Pallas kernels, called(): pl.pallas_call(kernel, grid=grid, out_shape=out_shape, in_specs=list(plac...  23.4 us
    all_gather x1, blocking collectives, shards(): own = lax.all_gather(own, 'zh', axis=0, tiled=True)  23 us
    ppermute x9, starting transfers between devices, swapped(): return lax.ppermute(value, axes, pairs)  22.9 us
    all_gather x1, blocking collectives, shards(): lax.all_gather(grads, PLANE, axis=0, tiled=True).reshape(2, R, 256)  13.3 us
    all_to_all x1, starting transfers between devices, shards(): turned = lax.all_to_all(turned, PLANE, 0, 0, tiled=True)  9.1 us
    all_to_all x1, waiting for transfers between devices, shards(): over_x = lax.all_to_all(hidden_part, 'x', 0, 0, tiled=True)  8.36 us
    all_to_all x1, starting transfers between devices, shards(): over_z = lax.all_to_all(over_x, ('zh', 'zl'), 0, 0, tiled=True)  6.78 us
    ppermute x9, waiting for transfers between devices, swapped(): return lax.ppermute(value, axes, pairs)  6.03 us
  transfers between devices with their start and end apart: 14, of which 6 were waited for; matrix products, arithmetic and copies ran while one was open for 0% of the time, Pallas kernels for 9%

profile of v3, /device:TPU:24, one launch (start us, length us, event | category | flops | bytes accessed | tf_op | source)
XLA Modules:
  0.0 141.0 jit_solution(7187923426391662085)
XLA Ops:
  0.6 2.6 %shard_map.86 = (bf16[8,64,1024]{2,1,0:T(8,128)(2,1)}, bf16[32,1024]{1,0:T(8,128)(2,1)S(1)}, bf16[2,512,256]{2,1,0:T(8,128)(2,1)}) custom-call(s32[1]{0:T(128)} %bitcast.4.place, bf16[64,8192]{1,0:T(8,128)(2,1)} %bitcast.28, bf16[32,8192]{1,0:T(8,128)(2,1)} %hidden.1, bf16[512,256]{1,0:T(8,128)(2,1)} %bitcast.18, bf16[512,256]{1,0:T(8,128)(2,1)} %bitcast.21), custom_call_target="tpu_custom_call" | custom-call | bytes 4194304 | tf_op jit(solution)/shard_map/pallas_call | solution.py:295
  3.3 9.1 %all-to-all-start = ((bf16[8,64,1024]{2,1,0:T(8,128)(2,1)}), bf16[8,64,1024]{2,1,0:T(8,128)(2,1)S(1)}, u32[]{:S(2)}, u32[]{:S(2)}) async-start(bf16[8,64,1024]{2,1,0:T(8,128)(2,1)} %get-tuple-element.24), calls=%async_computation | async-start | bytes 2097152 | tf_op jit(solution)/shard_map/all_to_all | solution.py:347
  12.4 23.0 %all_gather.12.block = bf16[128,1024]{1,0:T(8,128)(2,1)S(1)} all-gather(bf16[32,1024]{1,0:T(8,128)(2,1)S(1)} %get-tuple-element.23), channel_id=1, replica_groups=mesh['zh'=4,'x'=4,'zl'=4,'yh'=2,'yl'=2,'core'=2] {'zh'}, dimensions={0}, use_global_device_ids=true | all-gather | bytes 327680 | tf_op jit(solution)/shard_map/all_gather | solution.py:349
  36.5 4.3 %all-to-all-start.1 = ((bf16[4,128,1024]{2,1,0:T(8,128)(2,1)}), bf16[4,128,1024]{2,1,0:T(8,128)(2,1)S(1)}, u32[]{:S(2)}, u32[]{:S(2)}) async-start(bf16[4,128,1024]{2,1,0:T(8,128)(2,1)} %shard_map.87), calls=%async_computation.1 | async-start | bytes 2097152 | tf_op jit(solution)/shard_map/all_to_all | solution.py:352
  40.8 2.9 %collective-permute-start.1 = (bf16[2,512,256]{2,1,0:T(8,128)(2,1)}, bf16[2,512,256]{2,1,0:T(8,128)(2,1)}, u32[]{:S(2)}, u32[]{:S(2)}) collective-permute-start(bf16[2,512,256]{2,1,0:T(8,128)(2,1)} %get-tuple-element.27), channel_id=1, source_target_pairs={{0,2},{1,3},{2,0},{3,1},{4,6},{5,7},{6,4},{7,5},{8,10},{9,11},{10,... | collective-permute-start | bytes 1572872 | tf_op jit(solution)/shard_map/ppermute | solution.py:27
  43.7 1.9 %collective-permute-start = (bf16[2,1024,128]{2,1,0:T(8,128)(2,1)}, bf16[2,1024,128]{2,1,0:T(8,128)(2,1)}, u32[]{:S(2)}, u32[]{:S(2)}) collective-permute-start(bf16[2,1024,128]{2,1,0:T(8,128)(2,1)} %bitcast.3.cache), channel_id=1, source_target_pairs={{0,1},{1,0},{2,3},{3,2},{4,5},{5,4},{6,7},{7,6},{8,9},{9,8},{10,11... | collective-permute-start | bytes 1572872 | tf_op jit(solution)/shard_map/ppermute | solution.py:27
  45.6 2.4 %collective-permute-start.2 = (bf16[2,512,256]{2,1,0:T(8,128)(2,1)}, bf16[2,512,256]{2,1,0:T(8,128)(2,1)}, u32[]{:S(2)}, u32[]{:S(2)}) collective-permute-start(bf16[2,512,256]{2,1,0:T(8,128)(2,1)} %get-tuple-element.27), channel_id=1, source_target_pairs={{0,1},{1,0},{2,3},{3,2},{4,5},{5,4},{6,7},{7,6},{8,9},{9,8},{10,11... | collective-permute-start | bytes 1572872 | tf_op jit(solution)/shard_map/ppermute | solution.py:27
  48.0 5.4 %all-to-all-done.1 = bf16[4,128,1024]{2,1,0:T(8,128)(2,1)S(1)} async-done(((bf16[4,128,1024]{2,1,0:T(8,128)(2,1)}), bf16[4,128,1024]{2,1,0:T(8,128)(2,1)S(1)}, u32[]{:S(2)}, u32[]{:S(2)}) %all-to-all-start.1) | async-done | bytes 1048608 | tf_op jit(solution)/shard_map/all_to_all | solution.py:352
  55.0 4.8 %all-to-all-start.2 = ((bf16[8,128,256]{2,1,0:T(8,128)(2,1)}), bf16[8,128,256]{2,1,0:T(8,128)(2,1)S(1)}, u32[]{:S(2)}, u32[]{:S(2)}) async-start(bf16[8,128,256]{2,1,0:T(8,128)(2,1)} %shard_map.88), calls=%async_computation.2 | async-start | bytes 1048576 | tf_op jit(solution)/shard_map/all_to_all | solution.py:380
  59.8 2.0 %collective-permute-start.3 = (bf16[2,512,256]{2,1,0:T(8,128)(2,1)}, bf16[2,512,256]{2,1,0:T(8,128)(2,1)}, u32[]{:S(2)}, u32[]{:S(2)}) collective-permute-start(bf16[2,512,256]{2,1,0:T(8,128)(2,1)} %collective-permute-done.1.p2), channel_id=1, source_target_pairs={{0,1},{1,0},{2,3},{3,2},{4,5},{5,4},{6,7},{7,6},{8,9},{9,8},{10,11... | collective-permute-start | bytes 1572872 | tf_op jit(solution)/shard_map/ppermute | solution.py:27
  61.9 7.9 %shard_map.89.before = f32[3,4,512]{2,1,0:T(4,128)S(1)} custom-call(s32[1]{0:T(128)} %bitcast.place, s32[1,512]{1,0:T(1,128)S(1)} %bitcast.25, bf16[2,1024,128]{2,1,0:T(8,128)(2,1)} %bitcast.3.cache, bf16[2,1024,128]{2,1,0:T(8,128)(2,1)} %collective-permute-done.beside, bf16[512,256]{1,0:T(8,128)(2,1)S(1)} %bitcast.20, bf16[512,256]{1,0:T(8,128)(2,1)S(1)} %bitcast.23, ...), custom_call_target="tpu_custom_call" | custom-call | flops 8589934592 | bytes 3145728 | tf_op jit(solution)/shard_map/pallas_call | solution.py:295
  69.8 2.6 %shard_map.90 = (f32[3,8,512]{2,1,0:T(8,128)S(1)}, bf16[128,256]{1,0:T(8,128)(2,1)S(1)}, bf16[4,2,512,256]{3,2,1,0:T(8,128)(2,1)S(1)}) custom-call(s32[1]{0:T(128)} %bitcast.place, s32[1,512]{1,0:T(1,128)S(1)} %bitcast.26, f32[3,4,512]{2,1,0:T(4,128)S(1)} %shard_map.89.before, bf16[8,128,256]{2,1,0:T(8,128)(2,1)S(1)} %all-to-all-done.2.partial, ...), custom_call_target="tpu_custom_call" | custom-call | flops 1073741824 | bytes 3145728 | tf_op jit(solution)/shard_map/pallas_call | solution.py:295
  72.4 5.6 %all-gather = f32[12,8,512]{2,1,0:T(8,128)S(1)} all-gather(f32[3,8,512]{2,1,0:T(8,128)S(1)} %get-tuple-element.34), channel_id=2, replica_groups=mesh['zh'=4,'x'=4,'zl'=4,'yh'=2,'yl'=2,'core'=2] {'yl','core'}, dimensions={0}, use_global_device_ids=true | all-gather | bytes 245760 | tf_op jit(solution)/shard_map/all_gather | solution.py:392
  78.1 2.3 %shard_map.91 = bf16[128,256]{1,0:T(8,128)(2,1)S(1)} custom-call(s32[1]{0:T(128)} %bitcast.place, bf16[128,256]{1,0:T(8,128)(2,1)S(1)} %get-tuple-element.32.kv, bf16[4,2,512,256]{3,2,1,0:T(8,128)(2,1)S(1)} %get-tuple-element.33.pairs, s32[1,512]{1,0:T(1,128)S(1)} %bitcast.27, f32[4,3,8,512]{3,2,1,0:T(8,128)S(1)} %bitcast.24), custom_call_target="tpu_custom_call" | custom-call | flops 2147483648 | bytes 3145728 | tf_op jit(solution)/shard_map/pallas_call | solution.py:295
  80.3 13.3 %all_gather.15 = bf16[1024,256]{1,0:T(8,128)(2,1)S(1)} all-gather(bf16[128,256]{1,0:T(8,128)(2,1)S(1)} %shard_map.91), channel_id=1, replica_groups=mesh['zh'=4,'x'=4,'zl'=4,'yh'=2,'yl'=2,'core'=2] {'yh','yl','core'}, dimensions={0}, use_global_device_ids=true | all-gather | bytes 589824 | tf_op jit(solution)/shard_map/all_gather | solution.py:406
  95.1 3.6 %all-to-all-start.3 = ((bf16[4,128,1024]{2,1,0:T(8,128)(2,1)}), bf16[4,128,1024]{2,1,0:T(8,128)(2,1)S(1)}, u32[]{:S(2)}, u32[]{:S(2)}) async-start(bf16[4,128,1024]{2,1,0:T(8,128)(2,1)} %shard_map.92), calls=%async_computation.3 | async-start | bytes 2097152 | tf_op jit(solution)/shard_map/all_to_all | solution.py:418
  102.2 3.9 %collective-permute-start.5 = (bf16[2,96,1024]{2,1,0:T(8,128)(2,1)S(1)}, bf16[2,96,1024]{2,1,0:T(8,128)(2,1)S(1)}, u32[]{:S(2)}, u32[]{:S(2)}) collective-permute-start(bf16[2,96,1024]{2,1,0:T(8,128)(2,1)S(1)} %get-tuple-element.41), channel_id=1, source_target_pairs={{0,6},{1,7},{2,4},{3,5},{4,2},{5,3},{6,0},{7,1},{8,14},{9,15},{10,... | collective-permute-start | bytes 1179656 | tf_op jit(solution)/shard_map/ppermute | solution.py:27
  106.1 8.4 %all-to-all-done.3.blocks = bf16[4,128,1024]{2,1,0:T(8,128)(2,1)S(1)} async-done(((bf16[4,128,1024]{2,1,0:T(8,128)(2,1)}), bf16[4,128,1024]{2,1,0:T(8,128)(2,1)S(1)}, u32[]{:S(2)}, u32[]{:S(2)}) %all-to-all-start.3) | async-done | bytes 1048608 | tf_op jit(solution)/shard_map/all_to_all | solution.py:418
  115.3 6.8 %all-to-all-start.4 = ((bf16[16,32,256]{2,1,0:T(8,128)(2,1)}), bf16[16,32,256]{2,1,0:T(8,128)(2,1)S(1)}, u32[]{:S(2)}, u32[]{:S(2)}) async-start(bf16[16,32,256]{2,1,0:T(8,128)(2,1)} %shard_map.93), calls=%async_computation.4 | async-start | bytes 524288 | tf_op jit(solution)/shard_map/all_to_all | solution.py:433
  122.1 1.9 %collective-permute-start.7 = (bf16[2,32,1024]{2,1,0:T(8,128)(2,1)S(1)}, bf16[2,32,1024]{2,1,0:T(8,128)(2,1)S(1)}, u32[]{:S(2)}, u32[]{:S(2)}) collective-permute-start(bf16[2,32,1024]{2,1,0:T(8,128)(2,1)S(1)} %slice.8), channel_id=1, source_target_pairs={{0,2},{1,3},{2,0},{3,1},{4,6},{5,7},{6,4},{7,5},{8,10},{9,11},{10,... | collective-permute-start | bytes 393224 | tf_op jit(solution)/shard_map/ppermute | solution.py:27
  124.1 3.9 %collective-permute-start.6 = (bf16[2,32,1024]{2,1,0:T(8,128)(2,1)S(1)}, bf16[2,32,1024]{2,1,0:T(8,128)(2,1)S(1)}, u32[]{:S(2)}, u32[]{:S(2)}) collective-permute-start(bf16[2,32,1024]{2,1,0:T(8,128)(2,1)S(1)} %slice.6), channel_id=1, source_target_pairs={{0,6},{1,7},{2,4},{3,5},{4,2},{5,3},{6,0},{7,1},{8,14},{9,15},{10,... | collective-permute-start | bytes 393224 | tf_op jit(solution)/shard_map/ppermute | solution.py:27
  129.0 3.2 %collective-permute-done.6.upper = bf16[2,32,1024]{2,1,0:T(8,128)(2,1)S(1)} collective-permute-done((bf16[2,32,1024]{2,1,0:T(8,128)(2,1)S(1)}, bf16[2,32,1024]{2,1,0:T(8,128)(2,1)S(1)}, u32[]{:S(2)}, u32[]{:S(2)}) %collective-permute-start.6) | collective-permute-done | bytes 131104 | tf_op jit(solution)/shard_map/ppermute | solution.py:27
  132.2 1.9 %collective-permute-start.8 = (bf16[4,64,1024]{2,1,0:T(8,128)(2,1)S(1)}, bf16[4,64,1024]{2,1,0:T(8,128)(2,1)S(1)}, u32[]{:S(2)}, u32[]{:S(2)}) collective-permute-start(bf16[4,64,1024]{2,1,0:T(8,128)(2,1)S(1)} %get-tuple-element.43), channel_id=1, source_target_pairs={{0,1},{1,0},{2,3},{3,2},{4,5},{5,4},{6,7},{7,6},{8,9},{9,8},{10,11... | collective-permute-start | bytes 1572872 | tf_op jit(solution)/shard_map/ppermute | solution.py:27
  137.5 2.8 %all-to-all-done.4 = bf16[16,32,256]{2,1,0:T(8,128)(2,1)S(1)} async-done(((bf16[16,32,256]{2,1,0:T(8,128)(2,1)}), bf16[16,32,256]{2,1,0:T(8,128)(2,1)S(1)}, u32[]{:S(2)}, u32[]{:S(2)}) %all-to-all-start.4) | async-done | bytes 262176 | tf_op jit(solution)/shard_map/all_to_all | solution.py:433
  (29 shorter events, 13.4 us)
Async XLA Ops:
  3.3 32.2 %all-to-all-start = ((bf16[8,64,1024]{2,1,0:T(8,128)(2,1)}), bf16[8,64,1024]{2,1,0:T(8,128)(2,1)S(1)}, u32[]{:S(2)}, u32[]{:S(2)}) async-start(bf16[8,64,1024]{2,1,0:T(8,128)(2,1)} %get-tuple-element.24), calls=%async_computation | async-start | bytes 2097152 | tf_op jit(solution)/shard_map/all_to_all | solution.py:347
  36.5 16.9 %all-to-all-start.1 = ((bf16[4,128,1024]{2,1,0:T(8,128)(2,1)}), bf16[4,128,1024]{2,1,0:T(8,128)(2,1)S(1)}, u32[]{:S(2)}, u32[]{:S(2)}) async-start(bf16[4,128,1024]{2,1,0:T(8,128)(2,1)} %shard_map.87), calls=%async_computation.1 | async-start | bytes 2097152 | tf_op jit(solution)/shard_map/all_to_all | solution.py:352
  40.8 21.0 %copy-start = (bf16[1,512,256]{2,1,0:T(8,128)(2,1)S(1)}, bf16[1,512,256]{2,1,0:T(8,128)(2,1)}, u32[]{:S(2)}) copy-start(bf16[1,512,256]{2,1,0:T(8,128)(2,1)} %param.9) | copy-start | bytes 786436
  40.8 21.1 %copy-start.1 = (bf16[1,512,256]{2,1,0:T(8,128)(2,1)S(1)}, bf16[1,512,256]{2,1,0:T(8,128)(2,1)}, u32[]{:S(2)}) copy-start(bf16[1,512,256]{2,1,0:T(8,128)(2,1)} %param.10) | copy-start | bytes 786436
  40.8 21.1 %copy-start.2 = (s32[512]{0:T(512)S(1)}, s32[512]{0:T(512)}, u32[]{:S(2)}) copy-start(s32[512]{0:T(512)} %param.12) | copy-start | bytes 6148
  40.8 14.2 %collective-permute-start.1 = (bf16[2,512,256]{2,1,0:T(8,128)(2,1)}, bf16[2,512,256]{2,1,0:T(8,128)(2,1)}, u32[]{:S(2)}, u32[]{:S(2)}) collective-permute-start(bf16[2,512,256]{2,1,0:T(8,128)(2,1)} %get-tuple-element.27), channel_id=1, source_target_pairs={{0,2},{1,3},{2,0},{3,1},{4,6},{5,7},{6,4},{7,5},{8,10},{9,11},{10,... | collective-permute-start | bytes 1572872 | tf_op jit(solution)/shard_map/ppermute | solution.py:27
  43.7 18.1 %collective-permute-start = (bf16[2,1024,128]{2,1,0:T(8,128)(2,1)}, bf16[2,1024,128]{2,1,0:T(8,128)(2,1)}, u32[]{:S(2)}, u32[]{:S(2)}) collective-permute-start(bf16[2,1024,128]{2,1,0:T(8,128)(2,1)} %bitcast.3.cache), channel_id=1, source_target_pairs={{0,1},{1,0},{2,3},{3,2},{4,5},{5,4},{6,7},{7,6},{8,9},{9,8},{10,11... | collective-permute-start | bytes 1572872 | tf_op jit(solution)/shard_map/ppermute | solution.py:27
  45.6 24.1 %collective-permute-start.2 = (bf16[2,512,256]{2,1,0:T(8,128)(2,1)}, bf16[2,512,256]{2,1,0:T(8,128)(2,1)}, u32[]{:S(2)}, u32[]{:S(2)}) collective-permute-start(bf16[2,512,256]{2,1,0:T(8,128)(2,1)} %get-tuple-element.27), channel_id=1, source_target_pairs={{0,1},{1,0},{2,3},{3,2},{4,5},{5,4},{6,7},{7,6},{8,9},{9,8},{10,11... | collective-permute-start | bytes 1572872 | tf_op jit(solution)/shard_map/ppermute | solution.py:27
  55.0 14.8 %all-to-all-start.2 = ((bf16[8,128,256]{2,1,0:T(8,128)(2,1)}), bf16[8,128,256]{2,1,0:T(8,128)(2,1)S(1)}, u32[]{:S(2)}, u32[]{:S(2)}) async-start(bf16[8,128,256]{2,1,0:T(8,128)(2,1)} %shard_map.88), calls=%async_computation.2 | async-start | bytes 1048576 | tf_op jit(solution)/shard_map/all_to_all | solution.py:380
  59.8 10.0 %collective-permute-start.3 = (bf16[2,512,256]{2,1,0:T(8,128)(2,1)}, bf16[2,512,256]{2,1,0:T(8,128)(2,1)}, u32[]{:S(2)}, u32[]{:S(2)}) collective-permute-start(bf16[2,512,256]{2,1,0:T(8,128)(2,1)} %collective-permute-done.1.p2), channel_id=1, source_target_pairs={{0,1},{1,0},{2,3},{3,2},{4,5},{5,4},{6,7},{7,6},{8,9},{9,8},{10,11... | collective-permute-start | bytes 1572872 | tf_op jit(solution)/shard_map/ppermute | solution.py:27
  61.9 7.9 %copy-start.3 = (s32[512]{0:T(512)S(1)}, s32[512]{0:T(512)}, u32[]{:S(2)}) copy-start(s32[512]{0:T(512)} %param.13) | copy-start | bytes 6148
  95.1 19.4 %all-to-all-start.3 = ((bf16[4,128,1024]{2,1,0:T(8,128)(2,1)}), bf16[4,128,1024]{2,1,0:T(8,128)(2,1)S(1)}, u32[]{:S(2)}, u32[]{:S(2)}) async-start(bf16[4,128,1024]{2,1,0:T(8,128)(2,1)} %shard_map.92), calls=%async_computation.3 | async-start | bytes 2097152 | tf_op jit(solution)/shard_map/all_to_all | solution.py:418
  100.3 15.1 %collective-permute-start.4 = (bf16[2,96,1024]{2,1,0:T(8,128)(2,1)}, bf16[2,96,1024]{2,1,0:T(8,128)(2,1)S(1)}, u32[]{:S(2)}, u32[]{:S(2)}) collective-permute-start(bf16[2,96,1024]{2,1,0:T(8,128)(2,1)} %get-tuple-element.37), channel_id=1, source_target_pairs={{0,2},{1,3},{2,0},{3,1},{4,6},{5,7},{6,4},{7,5},{8,10},{9,11},{10,... | collective-permute-start | bytes 1179656 | tf_op jit(solution)/shard_map/ppermute | solution.py:27
  102.2 19.9 %collective-permute-start.5 = (bf16[2,96,1024]{2,1,0:T(8,128)(2,1)S(1)}, bf16[2,96,1024]{2,1,0:T(8,128)(2,1)S(1)}, u32[]{:S(2)}, u32[]{:S(2)}) collective-permute-start(bf16[2,96,1024]{2,1,0:T(8,128)(2,1)S(1)} %get-tuple-element.41), channel_id=1, source_target_pairs={{0,6},{1,7},{2,4},{3,5},{4,2},{5,3},{6,0},{7,1},{8,14},{9,15},{10,... | collective-permute-start | bytes 1179656 | tf_op jit(solution)/shard_map/ppermute | solution.py:27
  115.3 25.0 %all-to-all-start.4 = ((bf16[16,32,256]{2,1,0:T(8,128)(2,1)}), bf16[16,32,256]{2,1,0:T(8,128)(2,1)S(1)}, u32[]{:S(2)}, u32[]{:S(2)}) async-start(bf16[16,32,256]{2,1,0:T(8,128)(2,1)} %shard_map.93), calls=%async_computation.4 | async-start | bytes 524288 | tf_op jit(solution)/shard_map/all_to_all | solution.py:433
  122.1 6.9 %collective-permute-start.7 = (bf16[2,32,1024]{2,1,0:T(8,128)(2,1)S(1)}, bf16[2,32,1024]{2,1,0:T(8,128)(2,1)S(1)}, u32[]{:S(2)}, u32[]{:S(2)}) collective-permute-start(bf16[2,32,1024]{2,1,0:T(8,128)(2,1)S(1)} %slice.8), channel_id=1, source_target_pairs={{0,2},{1,3},{2,0},{3,1},{4,6},{5,7},{6,4},{7,5},{8,10},{9,11},{10,... | collective-permute-start | bytes 393224 | tf_op jit(solution)/shard_map/ppermute | solution.py:27
  124.1 8.1 %collective-permute-start.6 = (bf16[2,32,1024]{2,1,0:T(8,128)(2,1)S(1)}, bf16[2,32,1024]{2,1,0:T(8,128)(2,1)S(1)}, u32[]{:S(2)}, u32[]{:S(2)}) collective-permute-start(bf16[2,32,1024]{2,1,0:T(8,128)(2,1)S(1)} %slice.6), channel_id=1, source_target_pairs={{0,6},{1,7},{2,4},{3,5},{4,2},{5,3},{6,0},{7,1},{8,14},{9,15},{10,... | collective-permute-start | bytes 393224 | tf_op jit(solution)/shard_map/ppermute | solution.py:27
  132.2 3.8 %collective-permute-start.8 = (bf16[4,64,1024]{2,1,0:T(8,128)(2,1)S(1)}, bf16[4,64,1024]{2,1,0:T(8,128)(2,1)S(1)}, u32[]{:S(2)}, u32[]{:S(2)}) collective-permute-start(bf16[4,64,1024]{2,1,0:T(8,128)(2,1)S(1)} %get-tuple-element.43), channel_id=1, source_target_pairs={{0,1},{1,0},{2,3},{3,2},{4,5},{5,4},{6,7},{7,6},{8,9},{9,8},{10,11... | collective-permute-start | bytes 1572872 | tf_op jit(solution)/shard_map/ppermute | solution.py:27

commit v4 on v3

--- a/solution.py
+++ b/solution.py
@@ -56,31 +56,47 @@
     return copies
 
 
-def prefix_kernel(place, prefix_len, cache, beside, q0, o0, p2, stats):
-    rank = place[0]
-    lengths = prefix_len[...]
+def prefix_stats(rank, lengths, blocks_of, queries, grads):
     chunk = 512
-    for other, (q, o) in enumerate(((q0, o0), (p2.at[0], p2.at[1]))):
-        for head in range(2):
-            columns = pl.ds(head * HEAD, HEAD)
-            queries = q[:, columns]
-            grads = o[:, columns]
-            parts = None
-            for core, blocks in enumerate((cache, beside)):
-                for start in range(0, POSITIONS, chunk):
-                    rows = pl.ds(start, chunk)
-                    scores = lax.dot_general(
-                        blocks[0, rows, :], queries, NT, preferred_element_type=jnp.float32
-                    )
-                    dots = lax.dot_general(
-                        blocks[1, rows, :], grads, NT, preferred_element_type=jnp.float32
-                    )
-                    ids = lax.broadcasted_iota(jnp.int32, (chunk, R), 0)
-                    limit = lengths - ((rank ^ core) * POSITIONS + start)
-                    piece = softmax_parts(jnp.where(ids < limit, scores, LOW), dots)
-                    parts = piece if parts is None else merged(parts, piece)
-            for kind in range(3):
-                stats[kind, pl.ds(other * 2 + head, 1), :] = parts[kind]
+    parts = None
+    for core, blocks in blocks_of:
+        for start in range(0, POSITIONS, chunk):
+            rows = pl.ds(start, chunk)
+            scores = lax.dot_general(
+                blocks[0, rows, :], queries, NT, preferred_element_type=jnp.float32
+            )
+            dots = lax.dot_general(
+                blocks[1, rows, :], grads, NT, preferred_element_type=jnp.float32
+            )
+            ids = lax.broadcasted_iota(jnp.int32, (chunk, R), 0)
+            limit = lengths - ((rank ^ core) * POSITIONS + start)
+            piece = softmax_parts(jnp.where(ids < limit, scores, LOW), dots)
+            parts = piece if parts is None else merged(parts, piece)
+    return parts
+
+
+def first_prefix_kernel(place, prefix_len, cache, q0, o0, stats):
+    for head in range(2):
+        columns = pl.ds(head * HEAD, HEAD)
+        parts = prefix_stats(
+            place[0], prefix_len[...], ((0, cache),), q0[:, columns], o0[:, columns]
+        )
+        for kind in range(3):
+            stats[kind, pl.ds(head, 1), :] = parts[kind]
+
+
+def prefix_kernel(place, prefix_len, first, cache, beside, q0, o0, p2, stats):
+    for slot in range(4):
+        q, o = (q0, o0) if slot < 2 else (p2.at[0], p2.at[1])
+        blocks_of = ((1, beside),) if slot < 2 else ((0, cache), (1, beside))
+        columns = pl.ds(slot % 2 * HEAD, HEAD)
+        parts = prefix_stats(
+            place[0], prefix_len[...], blocks_of, q[:, columns], o[:, columns]
+        )
+        if slot < 2:
+            parts = merged(parts, tuple(first[kind, pl.ds(slot, 1), :] for kind in range(3)))
+        for kind in range(3):
+            stats[kind, pl.ds(slot, 1), :] = parts[kind]
 
 
 def new_scores(rank, doc_start, keys, values, queries, grads):
@@ -174,9 +190,7 @@
     out[:, HEAD:] = value_sum[...].astype(jnp.bfloat16)
 
 
-def arrange_kernel(
-    place, weight, hidden, queries, grads, turned, own, pair, blocks, both, arrived, left
-):
+def arrange_kernel(place, weight, hidden, turned, own, blocks, arrived, left):
     width = own.shape[1] // 4
     columns = [pl.ds(part * width, width) for part in range(4)]
     moves = [
@@ -187,22 +201,22 @@
     for part in range(4):
         start = pl.multiple_of((part * 8 + place[0]) * width, width)
         moves.append((hidden.at[:, pl.ds(start, width)], own.at[:, columns[part]]))
-    moves += [(queries, both.at[0]), (grads, both.at[1])]
     copies = fetch(moves, arrived)
     sent = [
         pltpu.make_async_copy(blocks.at[member], turned.at[member], left.at[member])
         for member in range(8)
     ]
-    sent += [pltpu.make_async_copy(both.at[kind], pair.at[kind], left.at[8 + kind]) for kind in range(2)]
     for member in range(8):
         for copy in copies[4 * member : 4 * member + 4]:
             copy.wait()
         sent[member].start()
-    for kind in range(2):
-        copies[36 + kind].wait()
-        sent[8 + kind].start()
-    for copy in copies[32:36] + sent:
+    for copy in copies[32:] + sent:
         copy.wait()
+
+
+def pair_kernel(queries, grads, pair):
+    pair[0] = queries[...]
+    pair[1] = grads[...]
 
 
 def repeat_kernel(block, out):
@@ -276,8 +290,9 @@
                 ].astype(jnp.float32)
 
 
-def reduce_x_kernel(blocks, out):
+def reduce_x_kernel(blocks, out, sums, sems):
     width = blocks.shape[2] // 4
+    copies = []
     for high in range(4):
         rows = pl.ds(high * 32, 32)
         total = blocks[0, rows, :].astype(jnp.float32)
@@ -285,7 +300,13 @@
             total = total + blocks[source, rows, :].astype(jnp.float32)
         total = total.astype(jnp.bfloat16)
         for low in range(4):
-            out[high * 4 + low] = total[:, low * width : (low + 1) * width]
+            sums[high * 4 + low] = total[:, low * width : (low + 1) * width]
+        quarter = pl.ds(high * 4, 4)
+        copy = pltpu.make_async_copy(sums.at[quarter], out.at[quarter], sems.at[high])
+        copy.start()
+        copies.append(copy)
+    for copy in copies:
+        copy.wait()
 
 
 def called(
@@ -329,31 +350,41 @@
 
     q0 = queries[0]
     o0 = out_grads[0]
-    turned, own, pair = called(
+    turned, own = called(
         arrange_kernel,
-        (shaped(bf16, 8, 64, width), shaped(bf16, 32, width), shaped(bf16, 2, R, 256)),
-        (member, far(kv_weight[0]), far(hidden), far(q0), far(o0)),
+        (shaped(bf16, 8, 64, width), shaped(bf16, 32, width)),
+        (member, far(kv_weight[0]), far(hidden)),
         0,
         4 << 20,
-        (
-            pltpu.VMEM((8, 64, width), bf16),
-            pltpu.VMEM((2, R, 256), bf16),
-            dma((38,)),
-            dma((10,)),
-        ),
-        (smem, hbm, hbm, hbm, hbm),
-        (anywhere, vmem, anywhere),
-    )
+        (pltpu.VMEM((8, 64, width), bf16), dma((36,)), dma((8,))),
+        (smem, hbm, hbm),
+        (anywhere, vmem),
+    )
+
     turned = lax.all_to_all(turned, PLANE, 0, 0, tiled=True)
 
     own = lax.all_gather(own, "zh", axis=0, tiled=True)
-    own, turned, pair, cached = lax.optimization_barrier((own, turned, pair, cache[0]))
+    own, turned, cached = lax.optimization_barrier((own, turned, cache[0]))
     states = called(repeat_kernel, shaped(bf16, 4, 128, width), (own,), 0, 1 << 20)
+    states, sent_q, sent_o = lax.optimization_barrier((states, q0, o0))
+    pair = called(pair_kernel, shaped(bf16, 2, R, 256), (sent_q, sent_o), 0, 1 << 16)
     states = lax.all_to_all(states, "x", 0, 0, tiled=True)
 
     p2 = swapped(pair, QUAD, 2)
     beside = swapped(cached, QUAD, 1)
     p1 = swapped(pair, QUAD, 1)
+    lengths = prefix_len.reshape(1, R)
+    first = called(
+        first_prefix_kernel,
+        shaped(f32, 3, 2, R),
+        (place, lengths, far(cache[0]), far(q0), far(o0)),
+        2 * 2 * 2 * R * POSITIONS * HEAD,
+        1 << 20,
+        (),
+        (smem,),
+        limit=16,
+    )
+    states, first = lax.optimization_barrier((states, first))
 
     states = states.reshape(R, width)
     heads = turned.reshape(2, 256, width)
@@ -370,7 +401,7 @@
     before = called(
         prefix_kernel,
         shaped(f32, 3, 4, R),
-        (place, prefix_len.reshape(1, R), cache[0], beside, q0, o0, p2),
+        (place, lengths, first, far(cache[0]), beside, far(q0), far(o0), p2),
         2 * 2 * 8 * R * POSITIONS * HEAD * 4,
         3 << 20,
         (),
@@ -416,7 +447,15 @@
     )
     hidden_part, kv_grads = lax.optimization_barrier((hidden_part, kv_grads))
     over_x = lax.all_to_all(hidden_part, "x", 0, 0, tiled=True)
-    over_x = called(reduce_x_kernel, shaped(bf16, 16, 32, width // 4), (over_x,), 0, 1 << 20)
+    over_x = called(
+        reduce_x_kernel,
+        shaped(bf16, 16, 32, width // 4),
+        (over_x,),
+        0,
+        1 << 20,
+        (pltpu.VMEM((16, 32, width // 4), bf16), dma((4,))),
+        outs=anywhere,
+    )
 
     mine, one, three = called(
         weight_kernel,

time: 142 us -> 141 us (level)
  waiting for transfers between devices: 22.6 us -> 19.8 us
    all_to_all x1, waiting for transfers between devices: 5.38 us -> 2.51 us  [shards(): states = lax.all_to_all(states, 'x', 0, 0, tiled=True)]
    pallas_call x11 -> x13, Pallas kernels: 23.4 us -> 24.5 us  [called(): pl.pallas_call(kernel, grid=grid, out_shape=out_shape, in_specs=list(plac...]
  transfers between devices with their start and end apart: 14 -> 14, of which waited for: 6 -> 6; matrix products, arithmetic and copies ran while one was open for 0% -> 0% of each run, Pallas kernels for 9% -> 11%
where the time goes in v4:
time: 141 us; the launch traced here: 139 us
  starting transfers between devices  51.4 us (36%)
  blocking collectives  42.1 us (30%)
  Pallas kernels  24.5 us (17%)
  waiting for transfers between devices  19.8 us (14%)
    pallas_call x13, Pallas kernels, called(): pl.pallas_call(kernel, grid=grid, out_shape=out_shape, in_specs=list(plac...  24.5 us
    all_gather x1, blocking collectives, shards(): own = lax.all_gather(own, 'zh', axis=0, tiled=True)  23.2 us
    ppermute x9, starting transfers between devices, swapped(): return lax.ppermute(value, axes, pairs)  22.9 us
    all_gather x1, blocking collectives, shards(): lax.all_gather(grads, PLANE, axis=0, tiled=True).reshape(2, R, 256)  13.1 us
    all_to_all x1, starting transfers between devices, shards(): turned = lax.all_to_all(turned, PLANE, 0, 0, tiled=True)  9.1 us
    all_to_all x1, waiting for transfers between devices, shards(): over_x = lax.all_to_all(hidden_part, 'x', 0, 0, tiled=True)  8.45 us
    all_to_all x1, starting transfers between devices, shards(): over_z = lax.all_to_all(over_x, ('zh', 'zl'), 0, 0, tiled=True)  6.79 us
    ppermute x9, waiting for transfers between devices, swapped(): return lax.ppermute(value, axes, pairs)  6.44 us
  transfers between devices with their start and end apart: 14, of which 6 were waited for; matrix products, arithmetic and copies ran while one was open for 0% of the time, Pallas kernels for 11%

profile of v4, /device:TPU:24, one launch (start us, length us, event | category | flops | bytes accessed | tf_op | source)
XLA Modules:
  0.0 139.4 jit_solution(942624879890242497)
XLA Ops:
  0.6 2.2 %shard_map.86 = (bf16[8,64,1024]{2,1,0:T(8,128)(2,1)}, bf16[32,1024]{1,0:T(8,128)(2,1)S(1)}) custom-call(s32[1]{0:T(128)} %bitcast.3.place, bf16[64,8192]{1,0:T(8,128)(2,1)} %bitcast.31, bf16[32,8192]{1,0:T(8,128)(2,1)} %hidden.1), custom_call_target="tpu_custom_call" | custom-call | bytes 4194304 | tf_op jit(solution)/shard_map/pallas_call | solution.py:316
  2.9 9.1 %all-to-all-start = ((bf16[8,64,1024]{2,1,0:T(8,128)(2,1)}), bf16[8,64,1024]{2,1,0:T(8,128)(2,1)S(1)}, u32[]{:S(2)}, u32[]{:S(2)}) async-start(bf16[8,64,1024]{2,1,0:T(8,128)(2,1)} %get-tuple-element.27), calls=%async_computation | async-start | bytes 2097152 | tf_op jit(solution)/shard_map/all_to_all | solution.py:364
  12.0 23.2 %all_gather.12.block = bf16[128,1024]{1,0:T(8,128)(2,1)S(1)} all-gather(bf16[32,1024]{1,0:T(8,128)(2,1)S(1)} %get-tuple-element.26), channel_id=1, replica_groups=mesh['zh'=4,'x'=4,'zl'=4,'yh'=2,'yl'=2,'core'=2] {'zh'}, dimensions={0}, use_global_device_ids=true | all-gather | bytes 327680 | tf_op jit(solution)/shard_map/all_gather | solution.py:366
  36.2 4.3 %all-to-all-start.1 = ((bf16[4,128,1024]{2,1,0:T(8,128)(2,1)}), bf16[4,128,1024]{2,1,0:T(8,128)(2,1)S(1)}, u32[]{:S(2)}, u32[]{:S(2)}) async-start(bf16[4,128,1024]{2,1,0:T(8,128)(2,1)} %shard_map.87), calls=%async_computation.1 | async-start | bytes 2097152 | tf_op jit(solution)/shard_map/all_to_all | solution.py:371
  40.5 2.8 %collective-permute-start.1 = (bf16[2,512,256]{2,1,0:T(8,128)(2,1)S(1)}, bf16[2,512,256]{2,1,0:T(8,128)(2,1)}, u32[]{:S(2)}, u32[]{:S(2)}) collective-permute-start(bf16[2,512,256]{2,1,0:T(8,128)(2,1)S(1)} %shard_map.89), channel_id=1, source_target_pairs={{0,2},{1,3},{2,0},{3,1},{4,6},{5,7},{6,4},{7,5},{8,10},{9,11},{10,... | collective-permute-start | bytes 1572872 | tf_op jit(solution)/shard_map/ppermute | solution.py:27
  45.3 2.9 %shard_map.88.first = f32[3,2,512]{2,1,0:T(2,128)S(1)} custom-call(s32[1]{0:T(128)} %bitcast.place, s32[1,512]{1,0:T(1,128)S(1)} %bitcast.27, bf16[2,1024,128]{2,1,0:T(8,128)(2,1)} %bitcast.33, bf16[512,256]{1,0:T(8,128)(2,1)} %bitcast.18, bf16[512,256]{1,0:T(8,128)(2,1)} %bitcast.22), custom_call_target="tpu_custom_call" | custom-call | flops 536870912 | bytes 1048576 | tf_op jit(solution)/shard_map/pallas_call | solution.py:316
  48.2 2.4 %collective-permute-start.2 = (bf16[2,512,256]{2,1,0:T(8,128)(2,1)S(1)}, bf16[2,512,256]{2,1,0:T(8,128)(2,1)}, u32[]{:S(2)}, u32[]{:S(2)}) collective-permute-start(bf16[2,512,256]{2,1,0:T(8,128)(2,1)S(1)} %shard_map.89), channel_id=1, source_target_pairs={{0,1},{1,0},{2,3},{3,2},{4,5},{5,4},{6,7},{7,6},{8,9},{9,8},{10,11... | collective-permute-start | bytes 1572872 | tf_op jit(solution)/shard_map/ppermute | solution.py:27
  50.6 2.5 %all-to-all-done.1 = bf16[4,128,1024]{2,1,0:T(8,128)(2,1)S(1)} async-done(((bf16[4,128,1024]{2,1,0:T(8,128)(2,1)}), bf16[4,128,1024]{2,1,0:T(8,128)(2,1)S(1)}, u32[]{:S(2)}, u32[]{:S(2)}) %all-to-all-start.1) | async-done | bytes 1048608 | tf_op jit(solution)/shard_map/all_to_all | solution.py:371
  54.7 4.8 %all-to-all-start.2 = ((bf16[8,128,256]{2,1,0:T(8,128)(2,1)}), bf16[8,128,256]{2,1,0:T(8,128)(2,1)S(1)}, u32[]{:S(2)}, u32[]{:S(2)}) async-start(bf16[8,128,256]{2,1,0:T(8,128)(2,1)} %shard_map.90), calls=%async_computation.2 | async-start | bytes 1048576 | tf_op jit(solution)/shard_map/all_to_all | solution.py:411
  59.5 2.2 %collective-permute-start.3 = (bf16[2,512,256]{2,1,0:T(8,128)(2,1)}, bf16[2,512,256]{2,1,0:T(8,128)(2,1)}, u32[]{:S(2)}, u32[]{:S(2)}) collective-permute-start(bf16[2,512,256]{2,1,0:T(8,128)(2,1)} %collective-permute-done.1.p2), channel_id=1, source_target_pairs={{0,1},{1,0},{2,3},{3,2},{4,5},{5,4},{6,7},{7,6},{8,9},{9,8},{10,11... | collective-permute-start | bytes 1572872 | tf_op jit(solution)/shard_map/ppermute | solution.py:27
  61.7 6.5 %shard_map.91.before = f32[3,4,512]{2,1,0:T(4,128)S(1)} custom-call(s32[1]{0:T(128)} %bitcast.place, s32[1,512]{1,0:T(1,128)S(1)} %bitcast.28, f32[3,2,512]{2,1,0:T(2,128)S(1)} %shard_map.88.first, bf16[2,1024,128]{2,1,0:T(8,128)(2,1)} %bitcast.34, bf16[2,1024,128]{2,1,0:T(8,128)(2,1)} %collective-permute-done.beside, bf16[512,256]{1,0:T(8,128)(2,1)} %bitcast.19, ...), custom_call_target="tpu_custom_call" | custom-call | flops 8589934592 | bytes 3145728 | tf_op jit(solution)/shard_map/pallas_call | solution.py:316
  68.2 2.6 %shard_map.92 = (f32[3,8,512]{2,1,0:T(8,128)S(1)}, bf16[128,256]{1,0:T(8,128)(2,1)S(1)}, bf16[4,2,512,256]{3,2,1,0:T(8,128)(2,1)S(1)}) custom-call(s32[1]{0:T(128)} %bitcast.place, s32[1,512]{1,0:T(1,128)S(1)} %bitcast.29, f32[3,4,512]{2,1,0:T(4,128)S(1)} %shard_map.91.before, bf16[8,128,256]{2,1,0:T(8,128)(2,1)S(1)} %all-to-all-done.2.partial, ...), custom_call_target="tpu_custom_call" | custom-call | flops 1073741824 | bytes 3145728 | tf_op jit(solution)/shard_map/pallas_call | solution.py:316
  70.8 5.8 %all-gather = f32[12,8,512]{2,1,0:T(8,128)S(1)} all-gather(f32[3,8,512]{2,1,0:T(8,128)S(1)} %get-tuple-element.40), channel_id=2, replica_groups=mesh['zh'=4,'x'=4,'zl'=4,'yh'=2,'yl'=2,'core'=2] {'yl','core'}, dimensions={0}, use_global_device_ids=true | all-gather | bytes 245760 | tf_op jit(solution)/shard_map/all_gather | solution.py:423
  76.6 2.3 %shard_map.93 = bf16[128,256]{1,0:T(8,128)(2,1)S(1)} custom-call(s32[1]{0:T(128)} %bitcast.place, bf16[128,256]{1,0:T(8,128)(2,1)S(1)} %get-tuple-element.38.kv, bf16[4,2,512,256]{3,2,1,0:T(8,128)(2,1)S(1)} %get-tuple-element.39.pairs, s32[1,512]{1,0:T(1,128)S(1)} %bitcast.30, f32[4,3,8,512]{3,2,1,0:T(8,128)S(1)} %bitcast.26), custom_call_target="tpu_custom_call" | custom-call | flops 2147483648 | bytes 3145728 | tf_op jit(solution)/shard_map/pallas_call | solution.py:316
  78.9 13.1 %all_gather.15 = bf16[1024,256]{1,0:T(8,128)(2,1)S(1)} all-gather(bf16[128,256]{1,0:T(8,128)(2,1)S(1)} %shard_map.93), channel_id=1, replica_groups=mesh['zh'=4,'x'=4,'zl'=4,'yh'=2,'yl'=2,'core'=2] {'yh','yl','core'}, dimensions={0}, use_global_device_ids=true | all-gather | bytes 589824 | tf_op jit(solution)/shard_map/all_gather | solution.py:437
  93.5 3.5 %all-to-all-start.3 = ((bf16[4,128,1024]{2,1,0:T(8,128)(2,1)}), bf16[4,128,1024]{2,1,0:T(8,128)(2,1)S(1)}, u32[]{:S(2)}, u32[]{:S(2)}) async-start(bf16[4,128,1024]{2,1,0:T(8,128)(2,1)} %shard_map.94), calls=%async_computation.3 | async-start | bytes 2097152 | tf_op jit(solution)/shard_map/all_to_all | solution.py:449
  98.6 2.3 %collective-permute-start.4 = (bf16[2,96,1024]{2,1,0:T(8,128)(2,1)}, bf16[2,96,1024]{2,1,0:T(8,128)(2,1)S(1)}, u32[]{:S(2)}, u32[]{:S(2)}) collective-permute-start(bf16[2,96,1024]{2,1,0:T(8,128)(2,1)} %get-tuple-element.43), channel_id=1, source_target_pairs={{0,2},{1,3},{2,0},{3,1},{4,6},{5,7},{6,4},{7,5},{8,10},{9,11},{10,... | collective-permute-start | bytes 1179656 | tf_op jit(solution)/shard_map/ppermute | solution.py:27
  100.9 3.5 %collective-permute-start.5 = (bf16[2,96,1024]{2,1,0:T(8,128)(2,1)S(1)}, bf16[2,96,1024]{2,1,0:T(8,128)(2,1)S(1)}, u32[]{:S(2)}, u32[]{:S(2)}) collective-permute-start(bf16[2,96,1024]{2,1,0:T(8,128)(2,1)S(1)} %get-tuple-element.47), channel_id=1, source_target_pairs={{0,6},{1,7},{2,4},{3,5},{4,2},{5,3},{6,0},{7,1},{8,14},{9,15},{10,... | collective-permute-start | bytes 1179656 | tf_op jit(solution)/shard_map/ppermute | solution.py:27
  104.4 8.4 %all-to-all-done.3.blocks = bf16[4,128,1024]{2,1,0:T(8,128)(2,1)S(1)} async-done(((bf16[4,128,1024]{2,1,0:T(8,128)(2,1)}), bf16[4,128,1024]{2,1,0:T(8,128)(2,1)S(1)}, u32[]{:S(2)}, u32[]{:S(2)}) %all-to-all-start.3) | async-done | bytes 1048608 | tf_op jit(solution)/shard_map/all_to_all | solution.py:449
  113.7 6.8 %all-to-all-start.4 = ((bf16[16,32,256]{2,1,0:T(8,128)(2,1)}), bf16[16,32,256]{2,1,0:T(8,128)(2,1)S(1)}, u32[]{:S(2)}, u32[]{:S(2)}) async-start(bf16[16,32,256]{2,1,0:T(8,128)(2,1)} %shard_map.95), calls=%async_computation.4 | async-start | bytes 524288 | tf_op jit(solution)/shard_map/all_to_all | solution.py:472
  120.5 2.3 %collective-permute-start.7 = (bf16[2,32,1024]{2,1,0:T(8,128)(2,1)S(1)}, bf16[2,32,1024]{2,1,0:T(8,128)(2,1)S(1)}, u32[]{:S(2)}, u32[]{:S(2)}) collective-permute-start(bf16[2,32,1024]{2,1,0:T(8,128)(2,1)S(1)} %slice.8), channel_id=1, source_target_pairs={{0,2},{1,3},{2,0},{3,1},{4,6},{5,7},{6,4},{7,5},{8,10},{9,11},{10,... | collective-permute-start | bytes 393224 | tf_op jit(solution)/shard_map/ppermute | solution.py:27
  122.9 3.5 %collective-permute-start.6 = (bf16[2,32,1024]{2,1,0:T(8,128)(2,1)S(1)}, bf16[2,32,1024]{2,1,0:T(8,128)(2,1)S(1)}, u32[]{:S(2)}, u32[]{:S(2)}) collective-permute-start(bf16[2,32,1024]{2,1,0:T(8,128)(2,1)S(1)} %slice.6), channel_id=1, source_target_pairs={{0,6},{1,7},{2,4},{3,5},{4,2},{5,3},{6,0},{7,1},{8,14},{9,15},{10,... | collective-permute-start | bytes 393224 | tf_op jit(solution)/shard_map/ppermute | solution.py:27
  127.4 3.6 %collective-permute-done.6.upper = bf16[2,32,1024]{2,1,0:T(8,128)(2,1)S(1)} collective-permute-done((bf16[2,32,1024]{2,1,0:T(8,128)(2,1)S(1)}, bf16[2,32,1024]{2,1,0:T(8,128)(2,1)S(1)}, u32[]{:S(2)}, u32[]{:S(2)}) %collective-permute-start.6) | collective-permute-done | bytes 131104 | tf_op jit(solution)/shard_map/ppermute | solution.py:27
  136.3 2.4 %all-to-all-done.4 = bf16[16,32,256]{2,1,0:T(8,128)(2,1)S(1)} async-done(((bf16[16,32,256]{2,1,0:T(8,128)(2,1)}), bf16[16,32,256]{2,1,0:T(8,128)(2,1)S(1)}, u32[]{:S(2)}, u32[]{:S(2)}) %all-to-all-start.4) | async-done | bytes 262176 | tf_op jit(solution)/shard_map/all_to_all | solution.py:472
  (31 shorter events, 15.4 us)
Async XLA Ops:
  2.9 32.3 %all-to-all-start = ((bf16[8,64,1024]{2,1,0:T(8,128)(2,1)}), bf16[8,64,1024]{2,1,0:T(8,128)(2,1)S(1)}, u32[]{:S(2)}, u32[]{:S(2)}) async-start(bf16[8,64,1024]{2,1,0:T(8,128)(2,1)} %get-tuple-element.27), calls=%async_computation | async-start | bytes 2097152 | tf_op jit(solution)/shard_map/all_to_all | solution.py:364
  12.0 28.5 %copy-start = (bf16[1,512,256]{2,1,0:T(8,128)(2,1)S(1)}, bf16[1,512,256]{2,1,0:T(8,128)(2,1)}, u32[]{:S(2)}) copy-start(bf16[1,512,256]{2,1,0:T(8,128)(2,1)} %param.9) | copy-start | bytes 786436
  12.0 28.5 %copy-start.1 = (bf16[1,512,256]{2,1,0:T(8,128)(2,1)S(1)}, bf16[1,512,256]{2,1,0:T(8,128)(2,1)}, u32[]{:S(2)}) copy-start(bf16[1,512,256]{2,1,0:T(8,128)(2,1)} %param.10) | copy-start | bytes 786436
  35.2 10.1 %copy-start.2 = (s32[512]{0:T(512)S(1)}, s32[512]{0:T(512)}, u32[]{:S(2)}) copy-start(s32[512]{0:T(512)} %param.12) | copy-start | bytes 6148
  36.2 16.9 %all-to-all-start.1 = ((bf16[4,128,1024]{2,1,0:T(8,128)(2,1)}), bf16[4,128,1024]{2,1,0:T(8,128)(2,1)S(1)}, u32[]{:S(2)}, u32[]{:S(2)}) async-start(bf16[4,128,1024]{2,1,0:T(8,128)(2,1)} %shard_map.87), calls=%async_computation.1 | async-start | bytes 2097152 | tf_op jit(solution)/shard_map/all_to_all | solution.py:371
  40.5 14.1 %collective-permute-start.1 = (bf16[2,512,256]{2,1,0:T(8,128)(2,1)S(1)}, bf16[2,512,256]{2,1,0:T(8,128)(2,1)}, u32[]{:S(2)}, u32[]{:S(2)}) collective-permute-start(bf16[2,512,256]{2,1,0:T(8,128)(2,1)S(1)} %shard_map.89), channel_id=1, source_target_pairs={{0,2},{1,3},{2,0},{3,1},{4,6},{5,7},{6,4},{7,5},{8,10},{9,11},{10,... | collective-permute-start | bytes 1572872 | tf_op jit(solution)/shard_map/ppermute | solution.py:27
  43.3 18.4 %collective-permute-start = (bf16[2,1024,128]{2,1,0:T(8,128)(2,1)}, bf16[2,1024,128]{2,1,0:T(8,128)(2,1)}, u32[]{:S(2)}, u32[]{:S(2)}) collective-permute-start(bf16[2,1024,128]{2,1,0:T(8,128)(2,1)} %bitcast.32), channel_id=1, source_target_pairs={{0,1},{1,0},{2,3},{3,2},{4,5},{5,4},{6,7},{7,6},{8,9},{9,8},{10,11... | collective-permute-start | bytes 1572872 | tf_op jit(solution)/shard_map/ppermute | solution.py:27
  48.2 20.0 %collective-permute-start.2 = (bf16[2,512,256]{2,1,0:T(8,128)(2,1)S(1)}, bf16[2,512,256]{2,1,0:T(8,128)(2,1)}, u32[]{:S(2)}, u32[]{:S(2)}) collective-permute-start(bf16[2,512,256]{2,1,0:T(8,128)(2,1)S(1)} %shard_map.89), channel_id=1, source_target_pairs={{0,1},{1,0},{2,3},{3,2},{4,5},{5,4},{6,7},{7,6},{8,9},{9,8},{10,11... | collective-permute-start | bytes 1572872 | tf_op jit(solution)/shard_map/ppermute | solution.py:27
  54.7 13.5 %all-to-all-start.2 = ((bf16[8,128,256]{2,1,0:T(8,128)(2,1)}), bf16[8,128,256]{2,1,0:T(8,128)(2,1)S(1)}, u32[]{:S(2)}, u32[]{:S(2)}) async-start(bf16[8,128,256]{2,1,0:T(8,128)(2,1)} %shard_map.90), calls=%async_computation.2 | async-start | bytes 1048576 | tf_op jit(solution)/shard_map/all_to_all | solution.py:411
  59.5 8.7 %copy-start.3 = (s32[512]{0:T(512)S(1)}, s32[512]{0:T(512)}, u32[]{:S(2)}) copy-start(s32[512]{0:T(512)} %param.13) | copy-start | bytes 6148
  59.5 8.7 %collective-permute-start.3 = (bf16[2,512,256]{2,1,0:T(8,128)(2,1)}, bf16[2,512,256]{2,1,0:T(8,128)(2,1)}, u32[]{:S(2)}, u32[]{:S(2)}) collective-permute-start(bf16[2,512,256]{2,1,0:T(8,128)(2,1)} %collective-permute-done.1.p2), channel_id=1, source_target_pairs={{0,1},{1,0},{2,3},{3,2},{4,5},{5,4},{6,7},{7,6},{8,9},{9,8},{10,11... | collective-permute-start | bytes 1572872 | tf_op jit(solution)/shard_map/ppermute | solution.py:27
  93.5 19.4 %all-to-all-start.3 = ((bf16[4,128,1024]{2,1,0:T(8,128)(2,1)}), bf16[4,128,1024]{2,1,0:T(8,128)(2,1)S(1)}, u32[]{:S(2)}, u32[]{:S(2)}) async-start(bf16[4,128,1024]{2,1,0:T(8,128)(2,1)} %shard_map.94), calls=%async_computation.3 | async-start | bytes 2097152 | tf_op jit(solution)/shard_map/all_to_all | solution.py:449
  98.6 15.1 %collective-permute-start.4 = (bf16[2,96,1024]{2,1,0:T(8,128)(2,1)}, bf16[2,96,1024]{2,1,0:T(8,128)(2,1)S(1)}, u32[]{:S(2)}, u32[]{:S(2)}) collective-permute-start(bf16[2,96,1024]{2,1,0:T(8,128)(2,1)} %get-tuple-element.43), channel_id=1, source_target_pairs={{0,2},{1,3},{2,0},{3,1},{4,6},{5,7},{6,4},{7,5},{8,10},{9,11},{10,... | collective-permute-start | bytes 1179656 | tf_op jit(solution)/shard_map/ppermute | solution.py:27
  100.9 19.6 %collective-permute-start.5 = (bf16[2,96,1024]{2,1,0:T(8,128)(2,1)S(1)}, bf16[2,96,1024]{2,1,0:T(8,128)(2,1)S(1)}, u32[]{:S(2)}, u32[]{:S(2)}) collective-permute-start(bf16[2,96,1024]{2,1,0:T(8,128)(2,1)S(1)} %get-tuple-element.47), channel_id=1, source_target_pairs={{0,6},{1,7},{2,4},{3,5},{4,2},{5,3},{6,0},{7,1},{8,14},{9,15},{10,... | collective-permute-start | bytes 1179656 | tf_op jit(solution)/shard_map/ppermute | solution.py:27
  113.7 25.0 %all-to-all-start.4 = ((bf16[16,32,256]{2,1,0:T(8,128)(2,1)}), bf16[16,32,256]{2,1,0:T(8,128)(2,1)S(1)}, u32[]{:S(2)}, u32[]{:S(2)}) async-start(bf16[16,32,256]{2,1,0:T(8,128)(2,1)} %shard_map.95), calls=%async_computation.4 | async-start | bytes 524288 | tf_op jit(solution)/shard_map/all_to_all | solution.py:472
  120.5 6.9 %collective-permute-start.7 = (bf16[2,32,1024]{2,1,0:T(8,128)(2,1)S(1)}, bf16[2,32,1024]{2,1,0:T(8,128)(2,1)S(1)}, u32[]{:S(2)}, u32[]{:S(2)}) collective-permute-start(bf16[2,32,1024]{2,1,0:T(8,128)(2,1)S(1)} %slice.8), channel_id=1, source_target_pairs={{0,2},{1,3},{2,0},{3,1},{4,6},{5,7},{6,4},{7,5},{8,10},{9,11},{10,... | collective-permute-start | bytes 393224 | tf_op jit(solution)/shard_map/ppermute | solution.py:27
  122.9 8.1 %collective-permute-start.6 = (bf16[2,32,1024]{2,1,0:T(8,128)(2,1)S(1)}, bf16[2,32,1024]{2,1,0:T(8,128)(2,1)S(1)}, u32[]{:S(2)}, u32[]{:S(2)}) collective-permute-start(bf16[2,32,1024]{2,1,0:T(8,128)(2,1)S(1)} %slice.6), channel_id=1, source_target_pairs={{0,6},{1,7},{2,4},{3,5},{4,2},{5,3},{6,0},{7,1},{8,14},{9,15},{10,... | collective-permute-start | bytes 393224 | tf_op jit(solution)/shard_map/ppermute | solution.py:27
  131.0 3.8 %collective-permute-start.8 = (bf16[4,64,1024]{2,1,0:T(8,128)(2,1)S(1)}, bf16[4,64,1024]{2,1,0:T(8,128)(2,1)S(1)}, u32[]{:S(2)}, u32[]{:S(2)}) collective-permute-start(bf16[4,64,1024]{2,1,0:T(8,128)(2,1)S(1)} %get-tuple-element.49), channel_id=1, source_target_pairs={{0,1},{1,0},{2,3},{3,2},{4,5},{5,4},{6,7},{7,6},{8,9},{9,8},{10,11... | collective-permute-start | bytes 1572872 | tf_op jit(solution)/shard_map/ppermute | solution.py:27

commit v5 on v4

--- a/solution.py
+++ b/solution.py
@@ -14,6 +14,7 @@
 SCALE = HEAD**-0.5
 LOG2E = 1.4426950408889634
 LOW = -1e30
+SPREAD = 128.0
 PLANE = ("yh", "yl", "core")
 QUAD = ("yl", "core")
 NT = (((1,), (1,)), ((), ()))
@@ -110,7 +111,7 @@
 
 
 def new_stats_kernel(
-    place, doc_start, before, partial, q0, o0, p1, p2, p3, stats, kv, pairs, sems
+    place, doc_start, before, kv, q0, o0, p1, p2, p3, stats, pairs, sems
 ):
     rank = place[0]
     sources = ((q0, o0), (p1.at[0], p1.at[1]), (p2.at[0], p2.at[1]), (p3.at[0], p3.at[1]))
@@ -122,10 +123,6 @@
         ],
         sems,
     )
-    total_kv = partial[0].astype(jnp.float32)
-    for source in range(1, 8):
-        total_kv = total_kv + partial[source].astype(jnp.float32)
-    kv[...] = total_kv.astype(jnp.bfloat16)
     starts = doc_start[...]
     for other in range(4):
         copies[2 * other].wait()
@@ -228,7 +225,8 @@
     for head in range(2):
         product = lax.dot_general(
             states[...], heads[head], NT, preferred_element_type=jnp.float32
-        ).astype(jnp.bfloat16)
+        )
+        product = product * SPREAD
         for quarter in range(4):
             out[head * 4 + quarter] = product[quarter * TOKENS : (quarter + 1) * TOKENS]
 
@@ -390,7 +388,7 @@
     heads = turned.reshape(2, 256, width)
     partial = called(
         project_kernel,
-        shaped(bf16, 8, TOKENS, 256),
+        shaped(f32, 8, TOKENS, 256),
         (states, heads),
         2 * R * 512 * width,
         3 << 20,
@@ -408,13 +406,14 @@
         (smem,),
         limit=16,
     )
-    partial = lax.all_to_all(partial, PLANE, 0, 0, tiled=True)
+    partial = lax.all_to_all(partial.astype(jnp.float16), PLANE, 0, 0, tiled=True)
+    kv = (jnp.sum(partial.astype(f32), axis=0) * (1 / SPREAD)).astype(bf16)
 
     starts = doc_start.reshape(1, R)
-    stats, kv, pairs = called(
+    stats, pairs = called(
         new_stats_kernel,
-        (shaped(f32, 3, 8, R), shaped(bf16, TOKENS, 256), shaped(bf16, 4, 2, R, 256)),
-        (place, starts, before, partial, *(far(source) for source in sources)),
+        (shaped(f32, 3, 8, R), shaped(bf16, 4, 2, R, 256)),
+        (place, starts, before, kv, *(far(source) for source in sources)),
         2 * 2 * 8 * R * TOKENS * HEAD * 4,
         3 << 20,
         (dma((8,)),),

time: 141 us -> 143 us (1.014)
  other arithmetic: 0.66 us -> 2.75 us
  transfers between devices with their start and end apart: 14 -> 14, of which waited for: 6 -> 6; matrix products, arithmetic and copies ran while one was open for 0% -> 2% of each run, Pallas kernels for 11% -> 10%
where the time goes in v5:
time: 143 us; the launch traced here: 141 us
  starting transfers between devices  51.8 us (36%)
  blocking collectives  42.1 us (29%)
  Pallas kernels  23.5 us (16%)
  waiting for transfers between devices  19.5 us (14%)
  other arithmetic  2.75 us (2%)
    pallas_call x13, Pallas kernels, called(): pl.pallas_call(kernel, grid=grid, out_shape=out_shape, in_specs=list(plac...  23.5 us
    all_gather x1, blocking collectives, shards(): own = lax.all_gather(own, 'zh', axis=0, tiled=True)  23.2 us
    ppermute x9, starting transfers between devices, swapped(): return lax.ppermute(value, axes, pairs)  22.9 us
    all_gather x1, blocking collectives, shards(): lax.all_gather(grads, PLANE, axis=0, tiled=True).reshape(2, R, 256)  13.1 us
    all_to_all x1, starting transfers between devices, shards(): turned = lax.all_to_all(turned, PLANE, 0, 0, tiled=True)  9.1 us
    all_to_all x1, waiting for transfers between devices, shards(): over_x = lax.all_to_all(hidden_part, 'x', 0, 0, tiled=True)  8.21 us
    all_to_all x1, starting transfers between devices, shards(): over_z = lax.all_to_all(over_x, ('zh', 'zl'), 0, 0, tiled=True)  6.79 us
    ppermute x9, waiting for transfers between devices, swapped(): return lax.ppermute(value, axes, pairs)  6.71 us
  transfers between devices with their start and end apart: 14, of which 6 were waited for; matrix products, arithmetic and copies ran while one was open for 2% of the time, Pallas kernels for 10%

profile of v5, /device:TPU:24, one launch (start us, length us, event | category | flops | bytes accessed | tf_op | source)
XLA Modules:
  0.0 140.7 jit_solution(2237667283481908086)
XLA Ops:
  0.6 2.2 %shard_map.86 = (bf16[8,64,1024]{2,1,0:T(8,128)(2,1)}, bf16[32,1024]{1,0:T(8,128)(2,1)S(1)}) custom-call(s32[1]{0:T(128)} %bitcast.1.place, bf16[64,8192]{1,0:T(8,128)(2,1)} %bitcast.31, bf16[32,8192]{1,0:T(8,128)(2,1)} %hidden.1), custom_call_target="tpu_custom_call" | custom-call | bytes 4194304 | tf_op jit(solution)/shard_map/pallas_call | solution.py:314
  2.9 9.1 %all-to-all-start = ((bf16[8,64,1024]{2,1,0:T(8,128)(2,1)}), bf16[8,64,1024]{2,1,0:T(8,128)(2,1)S(1)}, u32[]{:S(2)}, u32[]{:S(2)}) async-start(bf16[8,64,1024]{2,1,0:T(8,128)(2,1)} %get-tuple-element.26), calls=%async_computation | async-start | bytes 2097152 | tf_op jit(solution)/shard_map/all_to_all | solution.py:362
  12.0 23.2 %all_gather.12.block = bf16[128,1024]{1,0:T(8,128)(2,1)S(1)} all-gather(bf16[32,1024]{1,0:T(8,128)(2,1)S(1)} %get-tuple-element.25), channel_id=1, replica_groups=mesh['zh'=4,'x'=4,'zl'=4,'yh'=2,'yl'=2,'core'=2] {'zh'}, dimensions={0}, use_global_device_ids=true | all-gather | bytes 327680 | tf_op jit(solution)/shard_map/all_gather | solution.py:364
  36.2 4.3 %all-to-all-start.1 = ((bf16[4,128,1024]{2,1,0:T(8,128)(2,1)}), bf16[4,128,1024]{2,1,0:T(8,128)(2,1)S(1)}, u32[]{:S(2)}, u32[]{:S(2)}) async-start(bf16[4,128,1024]{2,1,0:T(8,128)(2,1)} %shard_map.87), calls=%async_computation.1 | async-start | bytes 2097152 | tf_op jit(solution)/shard_map/all_to_all | solution.py:369
  40.5 2.8 %collective-permute-start = (bf16[2,512,256]{2,1,0:T(8,128)(2,1)S(1)}, bf16[2,512,256]{2,1,0:T(8,128)(2,1)S(1)}, u32[]{:S(2)}, u32[]{:S(2)}) collective-permute-start(bf16[2,512,256]{2,1,0:T(8,128)(2,1)S(1)} %shard_map.88), channel_id=1, source_target_pairs={{0,2},{1,3},{2,0},{3,1},{4,6},{5,7},{6,4},{7,5},{8,10},{9,11},{10,... | collective-permute-start | bytes 1572872 | tf_op jit(solution)/shard_map/ppermute | solution.py:28
  45.3 2.9 %shard_map.89.first = f32[3,2,512]{2,1,0:T(2,128)S(1)} custom-call(s32[1]{0:T(128)} %bitcast.place, s32[1,512]{1,0:T(1,128)S(1)} %bitcast.27, bf16[2,1024,128]{2,1,0:T(8,128)(2,1)} %bitcast.33, bf16[512,256]{1,0:T(8,128)(2,1)} %bitcast.18, bf16[512,256]{1,0:T(8,128)(2,1)} %bitcast.22), custom_call_target="tpu_custom_call" | custom-call | flops 536870912 | bytes 1048576 | tf_op jit(solution)/shard_map/pallas_call | solution.py:314
  48.2 2.4 %collective-permute-start.2 = (bf16[2,512,256]{2,1,0:T(8,128)(2,1)S(1)}, bf16[2,512,256]{2,1,0:T(8,128)(2,1)}, u32[]{:S(2)}, u32[]{:S(2)}) collective-permute-start(bf16[2,512,256]{2,1,0:T(8,128)(2,1)S(1)} %shard_map.88), channel_id=1, source_target_pairs={{0,1},{1,0},{2,3},{3,2},{4,5},{5,4},{6,7},{7,6},{8,9},{9,8},{10,11... | collective-permute-start | bytes 1572872 | tf_op jit(solution)/shard_map/ppermute | solution.py:28
  50.6 2.5 %all-to-all-done.1 = bf16[4,128,1024]{2,1,0:T(8,128)(2,1)S(1)} async-done(((bf16[4,128,1024]{2,1,0:T(8,128)(2,1)}), bf16[4,128,1024]{2,1,0:T(8,128)(2,1)S(1)}, u32[]{:S(2)}, u32[]{:S(2)}) %all-to-all-start.1) | async-done | bytes 1048608 | tf_op jit(solution)/shard_map/all_to_all | solution.py:369
  54.9 4.8 %all-to-all-start.2 = ((f16[8,128,256]{2,1,0:T(8,128)(2,1)}), f16[8,128,256]{2,1,0:T(8,128)(2,1)}, u32[]{:S(2)}, u32[]{:S(2)}) async-start(f16[8,128,256]{2,1,0:T(8,128)(2,1)} %convert_element_type.12), calls=%async_computation.2 | async-start | bytes 1048576 | tf_op jit(solution)/shard_map/all_to_all | solution.py:409
  59.7 2.2 %collective-permute-start.3 = (bf16[2,512,256]{2,1,0:T(8,128)(2,1)S(1)}, bf16[2,512,256]{2,1,0:T(8,128)(2,1)}, u32[]{:S(2)}, u32[]{:S(2)}) collective-permute-start(bf16[2,512,256]{2,1,0:T(8,128)(2,1)S(1)} %collective-permute-done.p2), channel_id=1, source_target_pairs={{0,1},{1,0},{2,3},{3,2},{4,5},{5,4},{6,7},{7,6},{8,9},{9,8},{10,11... | collective-permute-start | bytes 1572872 | tf_op jit(solution)/shard_map/ppermute | solution.py:28
  61.9 6.3 %shard_map.91.before = f32[3,4,512]{2,1,0:T(4,128)S(1)} custom-call(s32[1]{0:T(128)} %bitcast.place, s32[1,512]{1,0:T(1,128)S(1)} %bitcast.28, f32[3,2,512]{2,1,0:T(2,128)S(1)} %shard_map.89.first, bf16[2,1024,128]{2,1,0:T(8,128)(2,1)} %bitcast.34, bf16[2,1024,128]{2,1,0:T(8,128)(2,1)} %collective-permute-done.1.beside, bf16[512,256]{1,0:T(8,128)(2,1)} %bitcast.19, ...), custom_call_target="tpu_custom_call" | custom-call | flops 8589934592 | bytes 3145728 | tf_op jit(solution)/shard_map/pallas_call | solution.py:314
  69.4 2.6 %shard_map.92 = (f32[3,8,512]{2,1,0:T(8,128)S(1)}, bf16[4,2,512,256]{3,2,1,0:T(8,128)(2,1)S(1)}) custom-call(s32[1]{0:T(128)} %bitcast.place, s32[1,512]{1,0:T(1,128)S(1)} %bitcast.29, f32[3,4,512]{2,1,0:T(4,128)S(1)} %shard_map.91.before, bf16[128,256]{1,0:T(8,128)(2,1)S(1)} %multiply_convert_fusion.kv, bf16[512,256]{1,0:T(8,128)(2,1)} %bitcast.20, ...), custom_call_target="tpu_custom_call" | custom-call | flops 1073741824 | bytes 3145728 | tf_op jit(solution)/shard_map/pallas_call | solution.py:314
  72.0 5.8 %all-gather = f32[12,8,512]{2,1,0:T(8,128)S(1)} all-gather(f32[3,8,512]{2,1,0:T(8,128)S(1)} %get-tuple-element.38), channel_id=2, replica_groups=mesh['zh'=4,'x'=4,'zl'=4,'yh'=2,'yl'=2,'core'=2] {'yl','core'}, dimensions={0}, use_global_device_ids=true | all-gather | bytes 245760 | tf_op jit(solution)/shard_map/all_gather | solution.py:422
  77.8 2.3 %shard_map.93 = bf16[128,256]{1,0:T(8,128)(2,1)S(1)} custom-call(s32[1]{0:T(128)} %bitcast.place, bf16[128,256]{1,0:T(8,128)(2,1)S(1)} %multiply_convert_fusion.kv, bf16[4,2,512,256]{3,2,1,0:T(8,128)(2,1)S(1)} %get-tuple-element.37.pairs, s32[1,512]{1,0:T(1,128)S(1)} %bitcast.30, f32[4,3,8,512]{3,2,1,0:T(8,128)S(1)} %bitcast.26), custom_call_target="tpu_custom_call" | custom-call | flops 2147483648 | bytes 3145728 | tf_op jit(solution)/shard_map/pallas_call | solution.py:314
  80.1 13.1 %all_gather.15 = bf16[1024,256]{1,0:T(8,128)(2,1)S(1)} all-gather(bf16[128,256]{1,0:T(8,128)(2,1)S(1)} %shard_map.93), channel_id=1, replica_groups=mesh['zh'=4,'x'=4,'zl'=4,'yh'=2,'yl'=2,'core'=2] {'yh','yl','core'}, dimensions={0}, use_global_device_ids=true | all-gather | bytes 589824 | tf_op jit(solution)/shard_map/all_gather | solution.py:436
  94.7 4.0 %all-to-all-start.3 = ((bf16[4,128,1024]{2,1,0:T(8,128)(2,1)}), bf16[4,128,1024]{2,1,0:T(8,128)(2,1)S(1)}, u32[]{:S(2)}, u32[]{:S(2)}) async-start(bf16[4,128,1024]{2,1,0:T(8,128)(2,1)} %shard_map.94), calls=%async_computation.3 | async-start | bytes 2097152 | tf_op jit(solution)/shard_map/all_to_all | solution.py:448
  100.2 2.6 %collective-permute-start.4 = (bf16[2,96,1024]{2,1,0:T(8,128)(2,1)}, bf16[2,96,1024]{2,1,0:T(8,128)(2,1)S(1)}, u32[]{:S(2)}, u32[]{:S(2)}) collective-permute-start(bf16[2,96,1024]{2,1,0:T(8,128)(2,1)} %get-tuple-element.41), channel_id=1, source_target_pairs={{0,2},{1,3},{2,0},{3,1},{4,6},{5,7},{6,4},{7,5},{8,10},{9,11},{10,... | collective-permute-start | bytes 1179656 | tf_op jit(solution)/shard_map/ppermute | solution.py:28
  102.8 3.2 %collective-permute-start.5 = (bf16[2,96,1024]{2,1,0:T(8,128)(2,1)S(1)}, bf16[2,96,1024]{2,1,0:T(8,128)(2,1)S(1)}, u32[]{:S(2)}, u32[]{:S(2)}) collective-permute-start(bf16[2,96,1024]{2,1,0:T(8,128)(2,1)S(1)} %get-tuple-element.45), channel_id=1, source_target_pairs={{0,6},{1,7},{2,4},{3,5},{4,2},{5,3},{6,0},{7,1},{8,14},{9,15},{10,... | collective-permute-start | bytes 1179656 | tf_op jit(solution)/shard_map/ppermute | solution.py:28
  106.1 8.2 %all-to-all-done.3.blocks = bf16[4,128,1024]{2,1,0:T(8,128)(2,1)S(1)} async-done(((bf16[4,128,1024]{2,1,0:T(8,128)(2,1)}), bf16[4,128,1024]{2,1,0:T(8,128)(2,1)S(1)}, u32[]{:S(2)}, u32[]{:S(2)}) %all-to-all-start.3) | async-done | bytes 1048608 | tf_op jit(solution)/shard_map/all_to_all | solution.py:448
  115.1 6.8 %all-to-all-start.4 = ((bf16[16,32,256]{2,1,0:T(8,128)(2,1)}), bf16[16,32,256]{2,1,0:T(8,128)(2,1)S(1)}, u32[]{:S(2)}, u32[]{:S(2)}) async-start(bf16[16,32,256]{2,1,0:T(8,128)(2,1)} %shard_map.95), calls=%async_computation.4 | async-start | bytes 524288 | tf_op jit(solution)/shard_map/all_to_all | solution.py:471
  121.9 2.6 %collective-permute-start.7 = (bf16[2,32,1024]{2,1,0:T(8,128)(2,1)S(1)}, bf16[2,32,1024]{2,1,0:T(8,128)(2,1)S(1)}, u32[]{:S(2)}, u32[]{:S(2)}) collective-permute-start(bf16[2,32,1024]{2,1,0:T(8,128)(2,1)S(1)} %slice.8), channel_id=1, source_target_pairs={{0,2},{1,3},{2,0},{3,1},{4,6},{5,7},{6,4},{7,5},{8,10},{9,11},{10,... | collective-permute-start | bytes 393224 | tf_op jit(solution)/shard_map/ppermute | solution.py:28
  124.5 3.2 %collective-permute-start.6 = (bf16[2,32,1024]{2,1,0:T(8,128)(2,1)S(1)}, bf16[2,32,1024]{2,1,0:T(8,128)(2,1)S(1)}, u32[]{:S(2)}, u32[]{:S(2)}) collective-permute-start(bf16[2,32,1024]{2,1,0:T(8,128)(2,1)S(1)} %slice.6), channel_id=1, source_target_pairs={{0,6},{1,7},{2,4},{3,5},{4,2},{5,3},{6,0},{7,1},{8,14},{9,15},{10,... | collective-permute-start | bytes 393224 | tf_op jit(solution)/shard_map/ppermute | solution.py:28
  128.8 3.8 %collective-permute-done.6.upper = bf16[2,32,1024]{2,1,0:T(8,128)(2,1)S(1)} collective-permute-done((bf16[2,32,1024]{2,1,0:T(8,128)(2,1)S(1)}, bf16[2,32,1024]{2,1,0:T(8,128)(2,1)S(1)}, u32[]{:S(2)}, u32[]{:S(2)}) %collective-permute-start.6) | collective-permute-done | bytes 131104 | tf_op jit(solution)/shard_map/ppermute | solution.py:28
  137.9 2.1 %all-to-all-done.4 = bf16[16,32,256]{2,1,0:T(8,128)(2,1)S(1)} async-done(((bf16[16,32,256]{2,1,0:T(8,128)(2,1)}), bf16[16,32,256]{2,1,0:T(8,128)(2,1)S(1)}, u32[]{:S(2)}, u32[]{:S(2)}) %all-to-all-start.4) | async-done | bytes 262176 | tf_op jit(solution)/shard_map/all_to_all | solution.py:471
  (36 shorter events, 16.7 us)
Async XLA Ops:
  2.9 32.3 %all-to-all-start = ((bf16[8,64,1024]{2,1,0:T(8,128)(2,1)}), bf16[8,64,1024]{2,1,0:T(8,128)(2,1)S(1)}, u32[]{:S(2)}, u32[]{:S(2)}) async-start(bf16[8,64,1024]{2,1,0:T(8,128)(2,1)} %get-tuple-element.26), calls=%async_computation | async-start | bytes 2097152 | tf_op jit(solution)/shard_map/all_to_all | solution.py:362
  12.0 28.5 %copy-start = (bf16[1,512,256]{2,1,0:T(8,128)(2,1)S(1)}, bf16[1,512,256]{2,1,0:T(8,128)(2,1)}, u32[]{:S(2)}) copy-start(bf16[1,512,256]{2,1,0:T(8,128)(2,1)} %param.9) | copy-start | bytes 786436
  12.0 28.5 %copy-start.1 = (bf16[1,512,256]{2,1,0:T(8,128)(2,1)S(1)}, bf16[1,512,256]{2,1,0:T(8,128)(2,1)}, u32[]{:S(2)}) copy-start(bf16[1,512,256]{2,1,0:T(8,128)(2,1)} %param.10) | copy-start | bytes 786436
  35.2 10.1 %copy-start.3 = (s32[512]{0:T(512)S(1)}, s32[512]{0:T(512)}, u32[]{:S(2)}) copy-start(s32[512]{0:T(512)} %param.12) | copy-start | bytes 6148
  36.2 16.9 %all-to-all-start.1 = ((bf16[4,128,1024]{2,1,0:T(8,128)(2,1)}), bf16[4,128,1024]{2,1,0:T(8,128)(2,1)S(1)}, u32[]{:S(2)}, u32[]{:S(2)}) async-start(bf16[4,128,1024]{2,1,0:T(8,128)(2,1)} %shard_map.87), calls=%async_computation.1 | async-start | bytes 2097152 | tf_op jit(solution)/shard_map/all_to_all | solution.py:369
  40.5 13.3 %collective-permute-start = (bf16[2,512,256]{2,1,0:T(8,128)(2,1)S(1)}, bf16[2,512,256]{2,1,0:T(8,128)(2,1)S(1)}, u32[]{:S(2)}, u32[]{:S(2)}) collective-permute-start(bf16[2,512,256]{2,1,0:T(8,128)(2,1)S(1)} %shard_map.88), channel_id=1, source_target_pairs={{0,2},{1,3},{2,0},{3,1},{4,6},{5,7},{6,4},{7,5},{8,10},{9,11},{10,... | collective-permute-start | bytes 1572872 | tf_op jit(solution)/shard_map/ppermute | solution.py:28
  43.3 18.5 %collective-permute-start.1 = (bf16[2,1024,128]{2,1,0:T(8,128)(2,1)}, bf16[2,1024,128]{2,1,0:T(8,128)(2,1)}, u32[]{:S(2)}, u32[]{:S(2)}) collective-permute-start(bf16[2,1024,128]{2,1,0:T(8,128)(2,1)} %bitcast.32), channel_id=1, source_target_pairs={{0,1},{1,0},{2,3},{3,2},{4,5},{5,4},{6,7},{7,6},{8,9},{9,8},{10,11... | collective-permute-start | bytes 1572872 | tf_op jit(solution)/shard_map/ppermute | solution.py:28
  48.2 21.2 %collective-permute-start.2 = (bf16[2,512,256]{2,1,0:T(8,128)(2,1)S(1)}, bf16[2,512,256]{2,1,0:T(8,128)(2,1)}, u32[]{:S(2)}, u32[]{:S(2)}) collective-permute-start(bf16[2,512,256]{2,1,0:T(8,128)(2,1)S(1)} %shard_map.88), channel_id=1, source_target_pairs={{0,1},{1,0},{2,3},{3,2},{4,5},{5,4},{6,7},{7,6},{8,9},{9,8},{10,11... | collective-permute-start | bytes 1572872 | tf_op jit(solution)/shard_map/ppermute | solution.py:28
  53.9 14.3 %copy-start.2 = (bf16[2,512,256]{2,1,0:T(8,128)(2,1)}, bf16[2,512,256]{2,1,0:T(8,128)(2,1)S(1)}, u32[]{:S(2)}) copy-start(bf16[2,512,256]{2,1,0:T(8,128)(2,1)S(1)} %collective-permute-done.p2) | copy-start | bytes 1572868
  54.9 13.3 %all-to-all-start.2 = ((f16[8,128,256]{2,1,0:T(8,128)(2,1)}), f16[8,128,256]{2,1,0:T(8,128)(2,1)}, u32[]{:S(2)}, u32[]{:S(2)}) async-start(f16[8,128,256]{2,1,0:T(8,128)(2,1)} %convert_element_type.12), calls=%async_computation.2 | async-start | bytes 1048576 | tf_op jit(solution)/shard_map/all_to_all | solution.py:409
  59.7 9.7 %copy-start.4 = (s32[512]{0:T(512)S(1)}, s32[512]{0:T(512)}, u32[]{:S(2)}) copy-start(s32[512]{0:T(512)} %param.13) | copy-start | bytes 6148
  59.7 9.7 %collective-permute-start.3 = (bf16[2,512,256]{2,1,0:T(8,128)(2,1)S(1)}, bf16[2,512,256]{2,1,0:T(8,128)(2,1)}, u32[]{:S(2)}, u32[]{:S(2)}) collective-permute-start(bf16[2,512,256]{2,1,0:T(8,128)(2,1)S(1)} %collective-permute-done.p2), channel_id=1, source_target_pairs={{0,1},{1,0},{2,3},{3,2},{4,5},{5,4},{6,7},{7,6},{8,9},{9,8},{10,11... | collective-permute-start | bytes 1572872 | tf_op jit(solution)/shard_map/ppermute | solution.py:28
  94.7 19.6 %all-to-all-start.3 = ((bf16[4,128,1024]{2,1,0:T(8,128)(2,1)}), bf16[4,128,1024]{2,1,0:T(8,128)(2,1)S(1)}, u32[]{:S(2)}, u32[]{:S(2)}) async-start(bf16[4,128,1024]{2,1,0:T(8,128)(2,1)} %shard_map.94), calls=%async_computation.3 | async-start | bytes 2097152 | tf_op jit(solution)/shard_map/all_to_all | solution.py:448
  100.2 14.9 %collective-permute-start.4 = (bf16[2,96,1024]{2,1,0:T(8,128)(2,1)}, bf16[2,96,1024]{2,1,0:T(8,128)(2,1)S(1)}, u32[]{:S(2)}, u32[]{:S(2)}) collective-permute-start(bf16[2,96,1024]{2,1,0:T(8,128)(2,1)} %get-tuple-element.41), channel_id=1, source_target_pairs={{0,2},{1,3},{2,0},{3,1},{4,6},{5,7},{6,4},{7,5},{8,10},{9,11},{10,... | collective-permute-start | bytes 1179656 | tf_op jit(solution)/shard_map/ppermute | solution.py:28
  102.8 19.1 %collective-permute-start.5 = (bf16[2,96,1024]{2,1,0:T(8,128)(2,1)S(1)}, bf16[2,96,1024]{2,1,0:T(8,128)(2,1)S(1)}, u32[]{:S(2)}, u32[]{:S(2)}) collective-permute-start(bf16[2,96,1024]{2,1,0:T(8,128)(2,1)S(1)} %get-tuple-element.45), channel_id=1, source_target_pairs={{0,6},{1,7},{2,4},{3,5},{4,2},{5,3},{6,0},{7,1},{8,14},{9,15},{10,... | collective-permute-start | bytes 1179656 | tf_op jit(solution)/shard_map/ppermute | solution.py:28
  115.1 24.9 %all-to-all-start.4 = ((bf16[16,32,256]{2,1,0:T(8,128)(2,1)}), bf16[16,32,256]{2,1,0:T(8,128)(2,1)S(1)}, u32[]{:S(2)}, u32[]{:S(2)}) async-start(bf16[16,32,256]{2,1,0:T(8,128)(2,1)} %shard_map.95), calls=%async_computation.4 | async-start | bytes 524288 | tf_op jit(solution)/shard_map/all_to_all | solution.py:471
  121.9 6.9 %collective-permute-start.7 = (bf16[2,32,1024]{2,1,0:T(8,128)(2,1)S(1)}, bf16[2,32,1024]{2,1,0:T(8,128)(2,1)S(1)}, u32[]{:S(2)}, u32[]{:S(2)}) collective-permute-start(bf16[2,32,1024]{2,1,0:T(8,128)(2,1)S(1)} %slice.8), channel_id=1, source_target_pairs={{0,2},{1,3},{2,0},{3,1},{4,6},{5,7},{6,4},{7,5},{8,10},{9,11},{10,... | collective-permute-start | bytes 393224 | tf_op jit(solution)/shard_map/ppermute | solution.py:28
  124.5 8.1 %collective-permute-start.6 = (bf16[2,32,1024]{2,1,0:T(8,128)(2,1)S(1)}, bf16[2,32,1024]{2,1,0:T(8,128)(2,1)S(1)}, u32[]{:S(2)}, u32[]{:S(2)}) collective-permute-start(bf16[2,32,1024]{2,1,0:T(8,128)(2,1)S(1)} %slice.6), channel_id=1, source_target_pairs={{0,6},{1,7},{2,4},{3,5},{4,2},{5,3},{6,0},{7,1},{8,14},{9,15},{10,... | collective-permute-start | bytes 393224 | tf_op jit(solution)/shard_map/ppermute | solution.py:28
  132.7 3.8 %collective-permute-start.8 = (bf16[4,64,1024]{2,1,0:T(8,128)(2,1)S(1)}, bf16[4,64,1024]{2,1,0:T(8,128)(2,1)S(1)}, u32[]{:S(2)}, u32[]{:S(2)}) collective-permute-start(bf16[4,64,1024]{2,1,0:T(8,128)(2,1)S(1)} %get-tuple-element.47), channel_id=1, source_target_pairs={{0,1},{1,0},{2,3},{3,2},{4,5},{5,4},{6,7},{7,6},{8,9},{9,8},{10,11... | collective-permute-start | bytes 1572872 | tf_op jit(solution)/shard_map/ppermute | solution.py:28

commit v6 on v5

--- a/solution.py
+++ b/solution.py
@@ -162,27 +162,38 @@
     whole[0] = top
     whole[1] = 1.0 / total
     whole[2] = accum / total
+    key_sum[...] = jnp.zeros_like(key_sum)
+    value_sum[...] = jnp.zeros_like(value_sum)
     starts = doc_start[...]
     for other in range(4):
         for head in range(2):
             columns = pl.ds(head * HEAD, HEAD)
             queries = pairs[other, 0, :, columns]
             grads = pairs[other, 1, :, columns]
-            scores, dots = new_scores(
-                rank, starts, kv[:, :HEAD], kv[:, HEAD:], queries, grads
-            )
             slot = pl.ds((rank ^ other) * 2 + head, 1)
-            quotient = jnp.exp2((scores - whole[0, slot, :]) * (SCALE * LOG2E)) * whole[1, slot, :]
-            probs = quotient.astype(jnp.bfloat16)
-            dscores = (quotient * (dots - whole[2, slot, :])).astype(jnp.bfloat16)
-            key_part = jnp.dot(dscores, queries, preferred_element_type=jnp.float32)
-            value_part = jnp.dot(probs, grads, preferred_element_type=jnp.float32)
-            if other == 0 and head == 0:
-                key_sum[...] = key_part
-                value_sum[...] = value_part
-            else:
-                key_sum[...] += key_part
-                value_sum[...] += value_part
+            stats_of = [whole[kind, slot, :] for kind in range(3)]
+            for block in range(4):
+                rows = slice(block * 128, block * 128 + 128)
+                count = 32 * (block + 1)
+                query = queries[rows]
+                grad = grads[rows]
+                scores = lax.dot_general(
+                    kv[:count, :HEAD], query, NT, preferred_element_type=jnp.float32
+                )
+                dots = lax.dot_general(
+                    kv[:count, HEAD:], grad, NT, preferred_element_type=jnp.float32
+                )
+                place_of = lax.broadcasted_iota(jnp.int32, (count, 128), 0)
+                token = (place_of // 32) * 128 + rank * 32 + place_of % 32
+                row = lax.broadcasted_iota(jnp.int32, (count, 128), 1) + block * 128
+                mask = (token >= starts[:, rows]) & (token <= row)
+                scores = jnp.where(mask, scores, LOW)
+                top_of, inverse, mean = (value[:, rows] for value in stats_of)
+                quotient = jnp.exp2((scores - top_of) * (SCALE * LOG2E)) * inverse
+                probs = quotient.astype(jnp.bfloat16)
+                dscores = (quotient * (dots - mean)).astype(jnp.bfloat16)
+                key_sum[:count] += jnp.dot(dscores, query, preferred_element_type=jnp.float32)
+                value_sum[:count] += jnp.dot(probs, grad, preferred_element_type=jnp.float32)
     out[:, :HEAD] = (key_sum[...] * SCALE).astype(jnp.bfloat16)
     out[:, HEAD:] = value_sum[...].astype(jnp.bfloat16)
 

time: 143 us -> 146 us (1.021)
  Pallas kernels: 23.5 us -> 26.9 us
    pallas_call x13, Pallas kernels: 23.5 us -> 26.9 us  [called(): pl.pallas_call(kernel, grid=grid, out_shape=out_shape, in_specs=list(plac...]
  transfers between devices with their start and end apart: 14 -> 14, of which waited for: 6 -> 6; matrix products, arithmetic and copies ran while one was open for 2% -> 1% of each run, Pallas kernels for 10% -> 10%
where the time goes in v6:
time: 146 us; the launch traced here: 144 us
  starting transfers between devices  51.8 us (35%)
  blocking collectives  42.1 us (29%)
  Pallas kernels  26.9 us (18%)
  waiting for transfers between devices  19.5 us (13%)
  other arithmetic  2.75 us (2%)
    pallas_call x13, Pallas kernels, called(): pl.pallas_call(kernel, grid=grid, out_shape=out_shape, in_specs=list(plac...  26.9 us
    all_gather x1, blocking collectives, shards(): own = lax.all_gather(own, 'zh', axis=0, tiled=True)  23.2 us
    ppermute x9, starting transfers between devices, swapped(): return lax.ppermute(value, axes, pairs)  22.9 us
    all_gather x1, blocking collectives, shards(): lax.all_gather(grads, PLANE, axis=0, tiled=True).reshape(2, R, 256)  13.1 us
    all_to_all x1, starting transfers between devices, shards(): turned = lax.all_to_all(turned, PLANE, 0, 0, tiled=True)  9.1 us
    all_to_all x1, waiting for transfers between devices, shards(): over_x = lax.all_to_all(hidden_part, 'x', 0, 0, tiled=True)  8.2 us
    all_to_all x1, starting transfers between devices, shards(): over_z = lax.all_to_all(over_x, ('zh', 'zl'), 0, 0, tiled=True)  6.79 us
    ppermute x9, waiting for transfers between devices, swapped(): return lax.ppermute(value, axes, pairs)  6.72 us
  transfers between devices with their start and end apart: 14, of which 6 were waited for; matrix products, arithmetic and copies ran while one was open for 1% of the time, Pallas kernels for 10%

profile of v6, /device:TPU:24, one launch (start us, length us, event | category | flops | bytes accessed | tf_op | source)
XLA Modules:
  0.0 144.0 jit_solution(16309537665856454656)
XLA Ops:
  0.6 2.2 %shard_map.86 = (bf16[8,64,1024]{2,1,0:T(8,128)(2,1)}, bf16[32,1024]{1,0:T(8,128)(2,1)S(1)}) custom-call(s32[1]{0:T(128)} %bitcast.1.place, bf16[64,8192]{1,0:T(8,128)(2,1)} %bitcast.31, bf16[32,8192]{1,0:T(8,128)(2,1)} %hidden.1), custom_call_target="tpu_custom_call" | custom-call | bytes 4194304 | tf_op jit(solution)/shard_map/pallas_call | solution.py:325
  2.9 9.1 %all-to-all-start = ((bf16[8,64,1024]{2,1,0:T(8,128)(2,1)}), bf16[8,64,1024]{2,1,0:T(8,128)(2,1)S(1)}, u32[]{:S(2)}, u32[]{:S(2)}) async-start(bf16[8,64,1024]{2,1,0:T(8,128)(2,1)} %get-tuple-element.26), calls=%async_computation | async-start | bytes 2097152 | tf_op jit(solution)/shard_map/all_to_all | solution.py:373
  12.0 23.2 %all_gather.12.block = bf16[128,1024]{1,0:T(8,128)(2,1)S(1)} all-gather(bf16[32,1024]{1,0:T(8,128)(2,1)S(1)} %get-tuple-element.25), channel_id=1, replica_groups=mesh['zh'=4,'x'=4,'zl'=4,'yh'=2,'yl'=2,'core'=2] {'zh'}, dimensions={0}, use_global_device_ids=true | all-gather | bytes 327680 | tf_op jit(solution)/shard_map/all_gather | solution.py:375
  36.2 4.3 %all-to-all-start.1 = ((bf16[4,128,1024]{2,1,0:T(8,128)(2,1)}), bf16[4,128,1024]{2,1,0:T(8,128)(2,1)S(1)}, u32[]{:S(2)}, u32[]{:S(2)}) async-start(bf16[4,128,1024]{2,1,0:T(8,128)(2,1)} %shard_map.87), calls=%async_computation.1 | async-start | bytes 2097152 | tf_op jit(solution)/shard_map/all_to_all | solution.py:380
  40.5 2.8 %collective-permute-start = (bf16[2,512,256]{2,1,0:T(8,128)(2,1)S(1)}, bf16[2,512,256]{2,1,0:T(8,128)(2,1)S(1)}, u32[]{:S(2)}, u32[]{:S(2)}) collective-permute-start(bf16[2,512,256]{2,1,0:T(8,128)(2,1)S(1)} %shard_map.88), channel_id=1, source_target_pairs={{0,2},{1,3},{2,0},{3,1},{4,6},{5,7},{6,4},{7,5},{8,10},{9,11},{10,... | collective-permute-start | bytes 1572872 | tf_op jit(solution)/shard_map/ppermute | solution.py:28
  45.3 2.9 %shard_map.89.first = f32[3,2,512]{2,1,0:T(2,128)S(1)} custom-call(s32[1]{0:T(128)} %bitcast.place, s32[1,512]{1,0:T(1,128)S(1)} %bitcast.27, bf16[2,1024,128]{2,1,0:T(8,128)(2,1)} %bitcast.33, bf16[512,256]{1,0:T(8,128)(2,1)} %bitcast.18, bf16[512,256]{1,0:T(8,128)(2,1)} %bitcast.22), custom_call_target="tpu_custom_call" | custom-call | flops 536870912 | bytes 1048576 | tf_op jit(solution)/shard_map/pallas_call | solution.py:325
  48.2 2.4 %collective-permute-start.2 = (bf16[2,512,256]{2,1,0:T(8,128)(2,1)S(1)}, bf16[2,512,256]{2,1,0:T(8,128)(2,1)}, u32[]{:S(2)}, u32[]{:S(2)}) collective-permute-start(bf16[2,512,256]{2,1,0:T(8,128)(2,1)S(1)} %shard_map.88), channel_id=1, source_target_pairs={{0,1},{1,0},{2,3},{3,2},{4,5},{5,4},{6,7},{7,6},{8,9},{9,8},{10,11... | collective-permute-start | bytes 1572872 | tf_op jit(solution)/shard_map/ppermute | solution.py:28
  50.6 2.5 %all-to-all-done.1 = bf16[4,128,1024]{2,1,0:T(8,128)(2,1)S(1)} async-done(((bf16[4,128,1024]{2,1,0:T(8,128)(2,1)}), bf16[4,128,1024]{2,1,0:T(8,128)(2,1)S(1)}, u32[]{:S(2)}, u32[]{:S(2)}) %all-to-all-start.1) | async-done | bytes 1048608 | tf_op jit(solution)/shard_map/all_to_all | solution.py:380
  54.9 4.8 %all-to-all-start.2 = ((f16[8,128,256]{2,1,0:T(8,128)(2,1)}), f16[8,128,256]{2,1,0:T(8,128)(2,1)}, u32[]{:S(2)}, u32[]{:S(2)}) async-start(f16[8,128,256]{2,1,0:T(8,128)(2,1)} %convert_element_type.12), calls=%async_computation.2 | async-start | bytes 1048576 | tf_op jit(solution)/shard_map/all_to_all | solution.py:420
  59.7 2.2 %collective-permute-start.3 = (bf16[2,512,256]{2,1,0:T(8,128)(2,1)S(1)}, bf16[2,512,256]{2,1,0:T(8,128)(2,1)}, u32[]{:S(2)}, u32[]{:S(2)}) collective-permute-start(bf16[2,512,256]{2,1,0:T(8,128)(2,1)S(1)} %collective-permute-done.p2), channel_id=1, source_target_pairs={{0,1},{1,0},{2,3},{3,2},{4,5},{5,4},{6,7},{7,6},{8,9},{9,8},{10,11... | collective-permute-start | bytes 1572872 | tf_op jit(solution)/shard_map/ppermute | solution.py:28
  61.9 6.3 %shard_map.91.before = f32[3,4,512]{2,1,0:T(4,128)S(1)} custom-call(s32[1]{0:T(128)} %bitcast.place, s32[1,512]{1,0:T(1,128)S(1)} %bitcast.28, f32[3,2,512]{2,1,0:T(2,128)S(1)} %shard_map.89.first, bf16[2,1024,128]{2,1,0:T(8,128)(2,1)} %bitcast.34, bf16[2,1024,128]{2,1,0:T(8,128)(2,1)} %collective-permute-done.1.beside, bf16[512,256]{1,0:T(8,128)(2,1)} %bitcast.19, ...), custom_call_target="tpu_custom_call" | custom-call | flops 8589934592 | bytes 3145728 | tf_op jit(solution)/shard_map/pallas_call | solution.py:325
  69.4 2.6 %shard_map.92 = (f32[3,8,512]{2,1,0:T(8,128)S(1)}, bf16[4,2,512,256]{3,2,1,0:T(8,128)(2,1)S(1)}) custom-call(s32[1]{0:T(128)} %bitcast.place, s32[1,512]{1,0:T(1,128)S(1)} %bitcast.29, f32[3,4,512]{2,1,0:T(4,128)S(1)} %shard_map.91.before, bf16[128,256]{1,0:T(8,128)(2,1)S(1)} %multiply_convert_fusion.kv, bf16[512,256]{1,0:T(8,128)(2,1)} %bitcast.20, ...), custom_call_target="tpu_custom_call" | custom-call | flops 1073741824 | bytes 3145728 | tf_op jit(solution)/shard_map/pallas_call | solution.py:325
  72.0 5.8 %all-gather = f32[12,8,512]{2,1,0:T(8,128)S(1)} all-gather(f32[3,8,512]{2,1,0:T(8,128)S(1)} %get-tuple-element.38), channel_id=2, replica_groups=mesh['zh'=4,'x'=4,'zl'=4,'yh'=2,'yl'=2,'core'=2] {'yl','core'}, dimensions={0}, use_global_device_ids=true | all-gather | bytes 245760 | tf_op jit(solution)/shard_map/all_gather | solution.py:433
  77.8 5.6 %shard_map.93 = bf16[128,256]{1,0:T(8,128)(2,1)S(1)} custom-call(s32[1]{0:T(128)} %bitcast.place, bf16[128,256]{1,0:T(8,128)(2,1)S(1)} %multiply_convert_fusion.kv, bf16[4,2,512,256]{3,2,1,0:T(8,128)(2,1)S(1)} %get-tuple-element.37.pairs, s32[1,512]{1,0:T(1,128)S(1)} %bitcast.30, f32[4,3,8,512]{3,2,1,0:T(8,128)S(1)} %bitcast.26), custom_call_target="tpu_custom_call" | custom-call | flops 2147483648 | bytes 3145728 | tf_op jit(solution)/shard_map/pallas_call | solution.py:325
  83.4 13.1 %all_gather.15 = bf16[1024,256]{1,0:T(8,128)(2,1)S(1)} all-gather(bf16[128,256]{1,0:T(8,128)(2,1)S(1)} %shard_map.93), channel_id=1, replica_groups=mesh['zh'=4,'x'=4,'zl'=4,'yh'=2,'yl'=2,'core'=2] {'yh','yl','core'}, dimensions={0}, use_global_device_ids=true | all-gather | bytes 589824 | tf_op jit(solution)/shard_map/all_gather | solution.py:447
  98.0 4.0 %all-to-all-start.3 = ((bf16[4,128,1024]{2,1,0:T(8,128)(2,1)}), bf16[4,128,1024]{2,1,0:T(8,128)(2,1)S(1)}, u32[]{:S(2)}, u32[]{:S(2)}) async-start(bf16[4,128,1024]{2,1,0:T(8,128)(2,1)} %shard_map.94), calls=%async_computation.3 | async-start | bytes 2097152 | tf_op jit(solution)/shard_map/all_to_all | solution.py:459
  103.6 2.6 %collective-permute-start.4 = (bf16[2,96,1024]{2,1,0:T(8,128)(2,1)}, bf16[2,96,1024]{2,1,0:T(8,128)(2,1)S(1)}, u32[]{:S(2)}, u32[]{:S(2)}) collective-permute-start(bf16[2,96,1024]{2,1,0:T(8,128)(2,1)} %get-tuple-element.41), channel_id=1, source_target_pairs={{0,2},{1,3},{2,0},{3,1},{4,6},{5,7},{6,4},{7,5},{8,10},{9,11},{10,... | collective-permute-start | bytes 1179656 | tf_op jit(solution)/shard_map/ppermute | solution.py:28
  106.2 3.2 %collective-permute-start.5 = (bf16[2,96,1024]{2,1,0:T(8,128)(2,1)S(1)}, bf16[2,96,1024]{2,1,0:T(8,128)(2,1)S(1)}, u32[]{:S(2)}, u32[]{:S(2)}) collective-permute-start(bf16[2,96,1024]{2,1,0:T(8,128)(2,1)S(1)} %get-tuple-element.45), channel_id=1, source_target_pairs={{0,6},{1,7},{2,4},{3,5},{4,2},{5,3},{6,0},{7,1},{8,14},{9,15},{10,... | collective-permute-start | bytes 1179656 | tf_op jit(solution)/shard_map/ppermute | solution.py:28
  109.4 8.2 %all-to-all-done.3.blocks = bf16[4,128,1024]{2,1,0:T(8,128)(2,1)S(1)} async-done(((bf16[4,128,1024]{2,1,0:T(8,128)(2,1)}), bf16[4,128,1024]{2,1,0:T(8,128)(2,1)S(1)}, u32[]{:S(2)}, u32[]{:S(2)}) %all-to-all-start.3) | async-done | bytes 1048608 | tf_op jit(solution)/shard_map/all_to_all | solution.py:459
  118.4 6.8 %all-to-all-start.4 = ((bf16[16,32,256]{2,1,0:T(8,128)(2,1)}), bf16[16,32,256]{2,1,0:T(8,128)(2,1)S(1)}, u32[]{:S(2)}, u32[]{:S(2)}) async-start(bf16[16,32,256]{2,1,0:T(8,128)(2,1)} %shard_map.95), calls=%async_computation.4 | async-start | bytes 524288 | tf_op jit(solution)/shard_map/all_to_all | solution.py:482
  125.3 2.6 %collective-permute-start.7 = (bf16[2,32,1024]{2,1,0:T(8,128)(2,1)S(1)}, bf16[2,32,1024]{2,1,0:T(8,128)(2,1)S(1)}, u32[]{:S(2)}, u32[]{:S(2)}) collective-permute-start(bf16[2,32,1024]{2,1,0:T(8,128)(2,1)S(1)} %slice.8), channel_id=1, source_target_pairs={{0,2},{1,3},{2,0},{3,1},{4,6},{5,7},{6,4},{7,5},{8,10},{9,11},{10,... | collective-permute-start | bytes 393224 | tf_op jit(solution)/shard_map/ppermute | solution.py:28
  127.9 3.2 %collective-permute-start.6 = (bf16[2,32,1024]{2,1,0:T(8,128)(2,1)S(1)}, bf16[2,32,1024]{2,1,0:T(8,128)(2,1)S(1)}, u32[]{:S(2)}, u32[]{:S(2)}) collective-permute-start(bf16[2,32,1024]{2,1,0:T(8,128)(2,1)S(1)} %slice.6), channel_id=1, source_target_pairs={{0,6},{1,7},{2,4},{3,5},{4,2},{5,3},{6,0},{7,1},{8,14},{9,15},{10,... | collective-permute-start | bytes 393224 | tf_op jit(solution)/shard_map/ppermute | solution.py:28
  132.1 3.8 %collective-permute-done.6.upper = bf16[2,32,1024]{2,1,0:T(8,128)(2,1)S(1)} collective-permute-done((bf16[2,32,1024]{2,1,0:T(8,128)(2,1)S(1)}, bf16[2,32,1024]{2,1,0:T(8,128)(2,1)S(1)}, u32[]{:S(2)}, u32[]{:S(2)}) %collective-permute-start.6) | collective-permute-done | bytes 131104 | tf_op jit(solution)/shard_map/ppermute | solution.py:28
  141.3 2.0 %all-to-all-done.4 = bf16[16,32,256]{2,1,0:T(8,128)(2,1)S(1)} async-done(((bf16[16,32,256]{2,1,0:T(8,128)(2,1)}), bf16[16,32,256]{2,1,0:T(8,128)(2,1)S(1)}, u32[]{:S(2)}, u32[]{:S(2)}) %all-to-all-start.4) | async-done | bytes 262176 | tf_op jit(solution)/shard_map/all_to_all | solution.py:482
  (36 shorter events, 16.7 us)
Async XLA Ops:
  2.9 32.3 %all-to-all-start = ((bf16[8,64,1024]{2,1,0:T(8,128)(2,1)}), bf16[8,64,1024]{2,1,0:T(8,128)(2,1)S(1)}, u32[]{:S(2)}, u32[]{:S(2)}) async-start(bf16[8,64,1024]{2,1,0:T(8,128)(2,1)} %get-tuple-element.26), calls=%async_computation | async-start | bytes 2097152 | tf_op jit(solution)/shard_map/all_to_all | solution.py:373
  12.0 28.5 %copy-start = (bf16[1,512,256]{2,1,0:T(8,128)(2,1)S(1)}, bf16[1,512,256]{2,1,0:T(8,128)(2,1)}, u32[]{:S(2)}) copy-start(bf16[1,512,256]{2,1,0:T(8,128)(2,1)} %param.9) | copy-start | bytes 786436
  12.0 28.5 %copy-start.1 = (bf16[1,512,256]{2,1,0:T(8,128)(2,1)S(1)}, bf16[1,512,256]{2,1,0:T(8,128)(2,1)}, u32[]{:S(2)}) copy-start(bf16[1,512,256]{2,1,0:T(8,128)(2,1)} %param.10) | copy-start | bytes 786436
  35.2 10.1 %copy-start.3 = (s32[512]{0:T(512)S(1)}, s32[512]{0:T(512)}, u32[]{:S(2)}) copy-start(s32[512]{0:T(512)} %param.12) | copy-start | bytes 6148
  36.2 16.9 %all-to-all-start.1 = ((bf16[4,128,1024]{2,1,0:T(8,128)(2,1)}), bf16[4,128,1024]{2,1,0:T(8,128)(2,1)S(1)}, u32[]{:S(2)}, u32[]{:S(2)}) async-start(bf16[4,128,1024]{2,1,0:T(8,128)(2,1)} %shard_map.87), calls=%async_computation.1 | async-start | bytes 2097152 | tf_op jit(solution)/shard_map/all_to_all | solution.py:380
  40.5 13.3 %collective-permute-start = (bf16[2,512,256]{2,1,0:T(8,128)(2,1)S(1)}, bf16[2,512,256]{2,1,0:T(8,128)(2,1)S(1)}, u32[]{:S(2)}, u32[]{:S(2)}) collective-permute-start(bf16[2,512,256]{2,1,0:T(8,128)(2,1)S(1)} %shard_map.88), channel_id=1, source_target_pairs={{0,2},{1,3},{2,0},{3,1},{4,6},{5,7},{6,4},{7,5},{8,10},{9,11},{10,... | collective-permute-start | bytes 1572872 | tf_op jit(solution)/shard_map/ppermute | solution.py:28
  43.3 18.5 %collective-permute-start.1 = (bf16[2,1024,128]{2,1,0:T(8,128)(2,1)}, bf16[2,1024,128]{2,1,0:T(8,128)(2,1)}, u32[]{:S(2)}, u32[]{:S(2)}) collective-permute-start(bf16[2,1024,128]{2,1,0:T(8,128)(2,1)} %bitcast.32), channel_id=1, source_target_pairs={{0,1},{1,0},{2,3},{3,2},{4,5},{5,4},{6,7},{7,6},{8,9},{9,8},{10,11... | collective-permute-start | bytes 1572872 | tf_op jit(solution)/shard_map/ppermute | solution.py:28
  48.2 21.2 %collective-permute-start.2 = (bf16[2,512,256]{2,1,0:T(8,128)(2,1)S(1)}, bf16[2,512,256]{2,1,0:T(8,128)(2,1)}, u32[]{:S(2)}, u32[]{:S(2)}) collective-permute-start(bf16[2,512,256]{2,1,0:T(8,128)(2,1)S(1)} %shard_map.88), channel_id=1, source_target_pairs={{0,1},{1,0},{2,3},{3,2},{4,5},{5,4},{6,7},{7,6},{8,9},{9,8},{10,11... | collective-permute-start | bytes 1572872 | tf_op jit(solution)/shard_map/ppermute | solution.py:28
  53.9 14.3 %copy-start.2 = (bf16[2,512,256]{2,1,0:T(8,128)(2,1)}, bf16[2,512,256]{2,1,0:T(8,128)(2,1)S(1)}, u32[]{:S(2)}) copy-start(bf16[2,512,256]{2,1,0:T(8,128)(2,1)S(1)} %collective-permute-done.p2) | copy-start | bytes 1572868
  54.9 13.3 %all-to-all-start.2 = ((f16[8,128,256]{2,1,0:T(8,128)(2,1)}), f16[8,128,256]{2,1,0:T(8,128)(2,1)}, u32[]{:S(2)}, u32[]{:S(2)}) async-start(f16[8,128,256]{2,1,0:T(8,128)(2,1)} %convert_element_type.12), calls=%async_computation.2 | async-start | bytes 1048576 | tf_op jit(solution)/shard_map/all_to_all | solution.py:420
  59.7 9.7 %copy-start.4 = (s32[512]{0:T(512)S(1)}, s32[512]{0:T(512)}, u32[]{:S(2)}) copy-start(s32[512]{0:T(512)} %param.13) | copy-start | bytes 6148
  59.7 9.7 %collective-permute-start.3 = (bf16[2,512,256]{2,1,0:T(8,128)(2,1)S(1)}, bf16[2,512,256]{2,1,0:T(8,128)(2,1)}, u32[]{:S(2)}, u32[]{:S(2)}) collective-permute-start(bf16[2,512,256]{2,1,0:T(8,128)(2,1)S(1)} %collective-permute-done.p2), channel_id=1, source_target_pairs={{0,1},{1,0},{2,3},{3,2},{4,5},{5,4},{6,7},{7,6},{8,9},{9,8},{10,11... | collective-permute-start | bytes 1572872 | tf_op jit(solution)/shard_map/ppermute | solution.py:28
  98.0 19.6 %all-to-all-start.3 = ((bf16[4,128,1024]{2,1,0:T(8,128)(2,1)}), bf16[4,128,1024]{2,1,0:T(8,128)(2,1)S(1)}, u32[]{:S(2)}, u32[]{:S(2)}) async-start(bf16[4,128,1024]{2,1,0:T(8,128)(2,1)} %shard_map.94), calls=%async_computation.3 | async-start | bytes 2097152 | tf_op jit(solution)/shard_map/all_to_all | solution.py:459
  103.6 14.9 %collective-permute-start.4 = (bf16[2,96,1024]{2,1,0:T(8,128)(2,1)}, bf16[2,96,1024]{2,1,0:T(8,128)(2,1)S(1)}, u32[]{:S(2)}, u32[]{:S(2)}) collective-permute-start(bf16[2,96,1024]{2,1,0:T(8,128)(2,1)} %get-tuple-element.41), channel_id=1, source_target_pairs={{0,2},{1,3},{2,0},{3,1},{4,6},{5,7},{6,4},{7,5},{8,10},{9,11},{10,... | collective-permute-start | bytes 1179656 | tf_op jit(solution)/shard_map/ppermute | solution.py:28
  106.2 19.1 %collective-permute-start.5 = (bf16[2,96,1024]{2,1,0:T(8,128)(2,1)S(1)}, bf16[2,96,1024]{2,1,0:T(8,128)(2,1)S(1)}, u32[]{:S(2)}, u32[]{:S(2)}) collective-permute-start(bf16[2,96,1024]{2,1,0:T(8,128)(2,1)S(1)} %get-tuple-element.45), channel_id=1, source_target_pairs={{0,6},{1,7},{2,4},{3,5},{4,2},{5,3},{6,0},{7,1},{8,14},{9,15},{10,... | collective-permute-start | bytes 1179656 | tf_op jit(solution)/shard_map/ppermute | solution.py:28
  118.4 24.9 %all-to-all-start.4 = ((bf16[16,32,256]{2,1,0:T(8,128)(2,1)}), bf16[16,32,256]{2,1,0:T(8,128)(2,1)S(1)}, u32[]{:S(2)}, u32[]{:S(2)}) async-start(bf16[16,32,256]{2,1,0:T(8,128)(2,1)} %shard_map.95), calls=%async_computation.4 | async-start | bytes 524288 | tf_op jit(solution)/shard_map/all_to_all | solution.py:482
  125.3 6.9 %collective-permute-start.7 = (bf16[2,32,1024]{2,1,0:T(8,128)(2,1)S(1)}, bf16[2,32,1024]{2,1,0:T(8,128)(2,1)S(1)}, u32[]{:S(2)}, u32[]{:S(2)}) collective-permute-start(bf16[2,32,1024]{2,1,0:T(8,128)(2,1)S(1)} %slice.8), channel_id=1, source_target_pairs={{0,2},{1,3},{2,0},{3,1},{4,6},{5,7},{6,4},{7,5},{8,10},{9,11},{10,... | collective-permute-start | bytes 393224 | tf_op jit(solution)/shard_map/ppermute | solution.py:28
  127.9 8.1 %collective-permute-start.6 = (bf16[2,32,1024]{2,1,0:T(8,128)(2,1)S(1)}, bf16[2,32,1024]{2,1,0:T(8,128)(2,1)S(1)}, u32[]{:S(2)}, u32[]{:S(2)}) collective-permute-start(bf16[2,32,1024]{2,1,0:T(8,128)(2,1)S(1)} %slice.6), channel_id=1, source_target_pairs={{0,6},{1,7},{2,4},{3,5},{4,2},{5,3},{6,0},{7,1},{8,14},{9,15},{10,... | collective-permute-start | bytes 393224 | tf_op jit(solution)/shard_map/ppermute | solution.py:28
  136.0 3.8 %collective-permute-start.8 = (bf16[4,64,1024]{2,1,0:T(8,128)(2,1)S(1)}, bf16[4,64,1024]{2,1,0:T(8,128)(2,1)S(1)}, u32[]{:S(2)}, u32[]{:S(2)}) collective-permute-start(bf16[4,64,1024]{2,1,0:T(8,128)(2,1)S(1)} %get-tuple-element.47), channel_id=1, source_target_pairs={{0,1},{1,0},{2,3},{3,2},{4,5},{5,4},{6,7},{7,6},{8,9},{9,8},{10,11... | collective-permute-start | bytes 1572872 | tf_op jit(solution)/shard_map/ppermute | solution.py:28
